TPU v7x, 256 devices: a whole 4x4x8 slice. The times are simulated.
256 devices in a mesh: grid: 64 (over z, y_hi, x), head: 4 (over y_lo, core).
Axes of the slice: x: 4, y: 4 (y_hi: 2, y_lo: 2; y = y_hi * 2 + y_lo), z: 8, core: 2. Of those that a mesh axis runs over, the one named last changes fastest.
Arguments:
- hidden_in: bfloat16 [64, 32, 16, 1024], P('grid', 'head'), may hold values from -16 to 16
- queries: bfloat16 [64, 32, 16, 1024], P('grid', None, None, 'head'), may hold values from -8 to 8
- keys: bfloat16 [64, 32, 16, 1024], P('grid', None, None, 'head'), may hold values from -8 to 8
- values: bfloat16 [64, 32, 16, 1024], P('grid', None, None, 'head'), may hold values from -6 to 6
- w_qkv: bfloat16 [1024, 3, 1024], P(None, None, 'head'), may hold values from -0.1875 to 0.1875
- w_out: bfloat16 [1024, 1024], P('head'), may hold values from -0.1875 to 0.1875
- out_grad: bfloat16 [64, 32, 16, 1024], P('grid', 'head'), may hold values from -16 to 16
Outputs:
- grad_hidden: bfloat16 [64, 32, 16, 1024], P('grid', 'head')
- grad_wqkv: float32 [1024, 3, 1024], P('grid', None, 'head')
- grad_wout: float32 [1024, 1024], P('head', 'grid')
All inputs are finite; a program needn't handle non-finite values.
Results may differ from a plain program's by a relative error of at most 0.027.
Values may be sent and summed in bfloat16 or wider, within the bound.
No kernel may reach another device: no remote copies, remote signals or barrier semaphores. Data moves between devices by JAX's collectives and lax.ppermute only.
A program may use at most 128 MiB of HBM per device.

v0:
```python
import jax
import jax.numpy as jnp
from jax import lax
from jax.sharding import PartitionSpec as P

D = 1024
HD = 64
WIN = 7
TILE_COLS = 8


neighbour_steps = [(-1, -1), (-1, 0), (-1, 1), (0, -1), (0, 1), (1, -1), (1, 0), (1, 1)]


def passed_along(value, axis, steps):
    count = lax.axis_size(axis)
    initial, last = (max(0, -steps), min(count, count - steps))
    return lax.ppermute(value, axis, [(source, source + steps) for source in range(initial, last)])


def side_span(side, length, depth):
    if side < 0:
        return (0, depth)
    if side > 0:
        return (length - depth, length)
    return (0, length)


def pad_span(side, length, depth):
    if side < 0:
        return (0, depth)
    if side > 0:
        return (depth + length, 2 * depth + length)
    return (depth, depth + length)


def neighbour_pass(query, padded, grad_attn, near_mask, scale):
    scores = (
        jnp.einsum("the,khe->htk", query, padded[0], preferred_element_type=jnp.float32) * scale
    )
    scores = jnp.where(near_mask[None], scores, -jnp.inf)
    top = jnp.max(scores, axis=2, keepdims=True)
    expo = jnp.exp(scores - top)
    probs = expo / jnp.sum(expo, axis=2, keepdims=True)
    probs16 = probs.astype(jnp.bfloat16)
    attn = jnp.einsum("htk,khe->the", probs16, padded[1], preferred_element_type=jnp.float32)
    attn = attn.astype(jnp.bfloat16)
    delta = jnp.einsum("the,the->ht", grad_attn, attn, preferred_element_type=jnp.float32)
    dprob = jnp.einsum("the,khe->htk", grad_attn, padded[1], preferred_element_type=jnp.float32)
    dscore = (probs * (dprob - delta[:, :, None])).astype(jnp.bfloat16)
    grad_q = jnp.einsum("htk,khe->the", dscore, padded[0], preferred_element_type=jnp.float32)
    grad_k = jnp.einsum("htk,the->khe", dscore, query, preferred_element_type=jnp.float32) * scale
    grad_v = jnp.einsum("htk,the->khe", probs16, grad_attn, preferred_element_type=jnp.float32)
    return (attn, (grad_q * scale).astype(jnp.bfloat16), jnp.stack([grad_k, grad_v]))


def per_device(hidden_in, queries, keys, values, w_qkv, w_out, out_grad):
    depth = WIN // 2
    scale = HD ** (-0.5)
    tile_index = lax.axis_index("grid")
    tile_row = tile_index // TILE_COLS
    tile_col = tile_index % TILE_COLS
    tile_rows_all = lax.axis_size("grid") // TILE_COLS
    query = queries[0]
    height, width, features = query.shape
    heads_here = features // HD
    pair = jnp.stack([keys[0], values[0]])

    def col_valid(step_c):
        return (tile_col + step_c >= 0) & (tile_col + step_c < TILE_COLS)

    padded = jnp.zeros((2, height + 2 * depth, width + 2 * depth, features), jnp.bfloat16)
    padded = padded.at[:, depth : depth + height, depth : depth + width].set(pair)
    for step_r, step_c in neighbour_steps:
        take_r = side_span(-step_r, height, depth)
        take_c = side_span(-step_c, width, depth)
        piece = pair[:, take_r[0] : take_r[1], take_c[0] : take_c[1]]
        got = passed_along(piece, "grid", -(step_r * TILE_COLS + step_c))
        got = jnp.where(col_valid(step_c), got, jnp.zeros_like(got))
        put_r = pad_span(step_r, height, depth)
        put_c = pad_span(step_c, width, depth)
        padded = padded.at[:, put_r[0] : put_r[1], put_c[0] : put_c[1]].set(got)
    pad_h = height + 2 * depth
    pad_w = width + 2 * depth
    key_row = jnp.arange(pad_h)
    key_col = jnp.arange(pad_w)
    row_global = tile_row * height + key_row - depth
    col_global = tile_col * width + key_col - depth
    row_inside = (row_global >= 0) & (row_global < tile_rows_all * height)
    col_inside = (col_global >= 0) & (col_global < TILE_COLS * width)
    row_near = (
        jnp.abs(key_row[None, :] - depth - jnp.arange(height)[:, None]) <= depth
    ) & row_inside[None, :]
    col_near = (
        jnp.abs(key_col[None, :] - depth - jnp.arange(width)[:, None]) <= depth
    ) & col_inside[None, :]
    near_mask = (row_near[:, None, :, None] & col_near[None, :, None, :]).reshape(
        height * width, pad_h * pad_w
    )
    grad_rows = lax.all_gather(out_grad, "head", axis=1, tiled=True)[0]
    grad_attn = lax.dot_general(
        grad_rows, w_out, (((2,), (1,)), ((), ())), preferred_element_type=jnp.float32
    ).astype(jnp.bfloat16)
    tokens = height * width
    attn, grad_q, grad_pad = neighbour_pass(
        query.reshape(tokens, heads_here, HD),
        padded.reshape(2, pad_h * pad_w, heads_here, HD),
        grad_attn.reshape(tokens, heads_here, HD),
        near_mask,
        scale,
    )
    grad_pad = grad_pad.reshape(2, pad_h, pad_w, features)
    inner = grad_pad[:, depth : depth + height, depth : depth + width]
    for step_r, step_c in neighbour_steps:
        take_r = pad_span(step_r, height, depth)
        take_c = pad_span(step_c, width, depth)
        piece = grad_pad[:, take_r[0] : take_r[1], take_c[0] : take_c[1]]
        got = passed_along(piece.astype(jnp.bfloat16), "grid", step_r * TILE_COLS + step_c).astype(
            piece.dtype
        )
        got = jnp.where(col_valid(-step_c), got, jnp.zeros_like(got))
        put_r = side_span(-step_r, height, depth)
        put_c = side_span(-step_c, width, depth)
        inner = inner.at[:, put_r[0] : put_r[1], put_c[0] : put_c[1]].add(got)
    grad_kv = inner.astype(jnp.bfloat16)
    grad_qkv = jnp.stack([grad_q.reshape(height, width, features), grad_kv[0], grad_kv[1]], axis=2)
    flat_grad = grad_qkv.reshape(tokens, 3 * features)
    whole_rows = lax.all_gather(hidden_in, "head", axis=1, tiled=True)[0].reshape(tokens, D)
    term = lax.dot_general(
        whole_rows, flat_grad, (((0,), (0,)), ((), ())), preferred_element_type=jnp.float32
    )
    grad_wqkv = lax.psum_scatter(
        term.reshape(lax.axis_size("grid") * (D // lax.axis_size("grid")), 3, features),
        "grid",
        scatter_dimension=0,
        tiled=True,
    )
    wout_term = lax.dot_general(
        attn.reshape(tokens, features),
        grad_rows.reshape(tokens, D),
        (((0,), (0,)), ((), ())),
        preferred_element_type=jnp.float32,
    )
    grad_wout = lax.psum_scatter(wout_term, "grid", scatter_dimension=1, tiled=True)
    piece = grad_qkv
    summed = lax.psum_scatter(
        lax.dot_general(
            piece, w_qkv, (((2, 3), (1, 2)), ((), ())), preferred_element_type=jnp.float32
        ).astype(jnp.bfloat16),
        "head",
        scatter_dimension=0,
        tiled=True,
    )
    grad_hidden = summed[None]
    return (grad_hidden, grad_wqkv, grad_wout)


def solution(mesh):
    return jax.shard_map(
        per_device,
        mesh=mesh,
        in_specs=(
            P("grid", "head", None, None),
            P("grid", None, None, "head"),
            P("grid", None, None, "head"),
            P("grid", None, None, "head"),
            P(None, None, "head"),
            P("head", None),
            P("grid", "head", None, None),
        ),
        out_specs=(P("grid", "head", None, None), P("grid", None, "head"), P("head", "grid")),
        check_vma=False,
    )
```

profile of v0, /device:TPU:8, one launch (start us, length us, event | category | flops | bytes accessed | tf_op | source)
XLA Modules:
  0.0 922.3 jit_solution(1864205978441818386)
XLA Ops:
  12.5 8.2 collective-permute-start.2
  20.7 5.2 collective-permute-start
  38.0 5.7 and.167
  45.0 4.5 collective-permute-start.1
  50.9 4.7 collective-permute-start.3
  70.0 6.5 fusion.28
  76.4 5.8 fusion.5
  85.0 4.2 convolution_bitcast_fusion
  90.8 4.1 multiply_convert_fusion
  118.4 8.5 collective-permute-start.15
  126.9 15.1 %collective-permute-start.13 = (bf16[2,3,3,256]{3,2,1,0:T(4,128)(2,1)S(1)}, bf16[2,3,3,256]{3,2,1,0:T(4,128)(2,1)}, u32[]{:S(2)}, u32[]{:S(2)}) collective-permute-start(bf16[2,3,3,256]{3,2,1,0:T(4,128)(2,1)S(1)} %get-tuple-element.212), channel_id=1, source_target_pairs={{0,28},{4,32},{8,36},{12,40},{16,44},{20,48},{24,52},{28,56},{32,6... | collective-permute-start | bytes 27656 | tf_op jit(solution)/shard_map/ppermute | solution.py:18
  146.1 4.0 collective-permute-start.14
  152.0 2.8 fusion.30
  159.1 8.4 collective-permute-done.9
  173.9 3.6 collective-permute-done.11
  178.7 3.4 scatter-add.31
  183.2 4.0 scatter-add.34
  187.2 2.7 add_select_fusion
  190.0 2.8 scatter-add.35
  200.9 3.9 fusion.29
  204.8 3.5 copy.54
  208.4 315.6 %reduce-scatter.8.cloned.1.call-done = f32[256,16]{0,1:T(8,128)} async-done(((f32[256,1024]{0,1:T(8,128)}), f32[256,16]{0,1:T(8,128)}) %reduce-scatter.8.cloned.1.call-update) | async-done | bytes 16400 | tf_op jit(solution)/shard_map/reduce_scatter | solution.py:144
  524.0 20.1 %reduce-scatter.4.cloned.1.call-done = bf16[8,16,1024]{2,1,0:T(8,128)(2,1)} async-done(((bf16[32,16,1024]{2,1,0:T(8,128)(2,1)}), bf16[8,16,1024]{2,1,0:T(8,128)(2,1)}) %reduce-scatter.4.cloned.1.call-update) | async-done | bytes 262160 | tf_op jit(solution)/shard_map/reduce_scatter | solution.py:146
  544.2 371.6 %reduce-scatter.6.cloned.1.call-done = f32[16,3,256]{2,0,1:T(8,128)} async-done(((f32[1024,3,256]{2,0,1:T(8,128)}), f32[16,3,256]{2,0,1:T(8,128)}) %reduce-scatter.6.cloned.1.call-update) | async-done | bytes 49168 | tf_op jit(solution)/shard_map/reduce_scatter | solution.py:132
  (142 shorter events, 88.6 us)
Async XLA Ops:
  7.2 190.7 %copy-start = (bf16[1024,3,256]{2,0,1:T(8,128)(2,1)S(1)}, bf16[1024,3,256]{2,0,1:T(8,128)(2,1)}, u32[]{:S(2)}) copy-start(bf16[1024,3,256]{2,0,1:T(8,128)(2,1)} %param.45) | copy-start | bytes 4718596
  7.2 29.2 %copy-start.9 = (bf16[1,32,16,256]{3,2,1,0:T(8,128)(2,1)S(1)}, bf16[1,32,16,256]{3,2,1,0:T(8,128)(2,1)}, u32[]{:S(2)}) copy-start(bf16[1,32,16,256]{3,2,1,0:T(8,128)(2,1)} %param.42) | copy-start | bytes 786436
  7.2 75.1 %all-gather.3.cloned.1.call-start = ((), (), s32[]{:S(2)}) async-start(), calls=%async_computation.3 | async-start | bytes 1310720 | tf_op jit(solution)/shard_map/all_gather | solution.py:100
  7.9 193.0 %all-gather.5.cloned.1.call-start = ((), (), s32[]{:S(2)}) async-start(), calls=%async_computation.5 | async-start | bytes 1310720 | tf_op jit(solution)/shard_map/all_gather | solution.py:128
  9.9 41.0 %collective-permute-start.7 = (bf16[2,3,3,256]{3,2,1,0:T(4,128)(2,1)S(1)}, bf16[2,3,3,256]{3,2,1,0:T(4,128)(2,1)S(1)}, u32[]{:S(2)}, u32[]{:S(2)}) collective-permute-start(bf16[2,3,3,256]{3,2,1,0:T(4,128)(2,1)S(1)} %get-tuple-element.223), channel_id=1, source_target_pairs={{36,0},{40,4},{44,8},{48,12},{52,16},{56,20},{60,24},{64,28},{68,3... | collective-permute-start | bytes 27656 | tf_op jit(solution)/shard_map/ppermute | solution.py:18
  11.2 33.8 %collective-permute-start.5 = (bf16[2,3,3,256]{3,2,1,0:T(4,128)(2,1)S(1)}, bf16[2,3,3,256]{3,2,1,0:T(4,128)(2,1)S(1)}, u32[]{:S(2)}, u32[]{:S(2)}) collective-permute-start(bf16[2,3,3,256]{3,2,1,0:T(4,128)(2,1)S(1)} %get-tuple-element.224), channel_id=1, source_target_pairs={{28,0},{32,4},{36,8},{40,12},{44,16},{48,20},{52,24},{56,28},{60,3... | collective-permute-start | bytes 27656 | tf_op jit(solution)/shard_map/ppermute | solution.py:18
  12.5 46.9 %collective-permute-start.2 = (bf16[2,3,3,256]{3,2,1,0:T(4,128)(2,1)S(1)}, bf16[2,3,3,256]{3,2,1,0:T(4,128)(2,1)S(1)}, u32[]{:S(2)}, u32[]{:S(2)}) collective-permute-start(bf16[2,3,3,256]{3,2,1,0:T(4,128)(2,1)S(1)} %get-tuple-element.225), channel_id=1, source_target_pairs={{0,28},{4,32},{8,36},{12,40},{16,44},{20,48},{24,52},{28,56},{32,6... | collective-permute-start | bytes 27656 | tf_op jit(solution)/shard_map/ppermute | solution.py:18
  20.7 28.9 %collective-permute-start = (bf16[2,3,3,256]{3,2,1,0:T(4,128)(2,1)S(1)}, bf16[2,3,3,256]{3,2,1,0:T(4,128)(2,1)S(1)}, u32[]{:S(2)}, u32[]{:S(2)}) collective-permute-start(bf16[2,3,3,256]{3,2,1,0:T(4,128)(2,1)S(1)} %get-tuple-element.226), channel_id=1, source_target_pairs={{0,36},{4,40},{8,44},{12,48},{16,52},{20,56},{24,60},{28,64},{32,6... | collective-permute-start | bytes 27656 | tf_op jit(solution)/shard_map/ppermute | solution.py:18
  26.0 29.9 %collective-permute-start.6 = (bf16[2,3,16,256]{3,2,1,0:T(8,128)(2,1)S(1)}, bf16[2,3,16,256]{3,2,1,0:T(8,128)(2,1)S(1)}, u32[]{:S(2)}, u32[]{:S(2)}) collective-permute-start(bf16[2,3,16,256]{3,2,1,0:T(8,128)(2,1)S(1)} %get-tuple-element.227), channel_id=1, source_target_pairs={{32,0},{36,4},{40,8},{44,12},{48,16},{52,20},{56,24},{60,28},{64,3... | collective-permute-start | bytes 147464 | tf_op jit(solution)/shard_map/ppermute | solution.py:18
  27.3 496.7 %reduce-scatter.8.cloned.1.call-start = ((), (), s32[]{:S(2)}) async-start(), calls=%async_computation.7 | async-start | bytes 1064960 | tf_op jit(solution)/shard_map/reduce_scatter | solution.py:144
  45.0 10.9 %collective-permute-start.1 = (bf16[2,3,16,256]{3,2,1,0:T(8,128)(2,1)S(1)}, bf16[2,3,16,256]{3,2,1,0:T(8,128)(2,1)S(1)}, u32[]{:S(2)}, u32[]{:S(2)}) collective-permute-start(bf16[2,3,16,256]{3,2,1,0:T(8,128)(2,1)S(1)} %get-tuple-element.228), channel_id=1, source_target_pairs={{0,32},{4,36},{8,40},{12,44},{16,48},{20,52},{24,56},{28,60},{32,6... | collective-permute-start | bytes 147464 | tf_op jit(solution)/shard_map/ppermute | solution.py:18
  49.6 14.6 %collective-permute-start.4 = (bf16[2,32,3,256]{3,2,1,0:T(4,128)(2,1)S(1)}, bf16[2,32,3,256]{3,2,1,0:T(4,128)(2,1)S(1)}, u32[]{:S(2)}, u32[]{:S(2)}) collective-permute-start(bf16[2,32,3,256]{3,2,1,0:T(4,128)(2,1)S(1)} %get-tuple-element.229), channel_id=1, source_target_pairs={{4,0},{8,4},{12,8},{16,12},{20,16},{24,20},{28,24},{32,28},{36,32}... | collective-permute-start | bytes 294920 | tf_op jit(solution)/shard_map/ppermute | solution.py:18
  50.9 11.7 %collective-permute-start.3 = (bf16[2,32,3,256]{3,2,1,0:T(4,128)(2,1)S(1)}, bf16[2,32,3,256]{3,2,1,0:T(4,128)(2,1)S(1)}, u32[]{:S(2)}, u32[]{:S(2)}) collective-permute-start(bf16[2,32,3,256]{3,2,1,0:T(4,128)(2,1)S(1)} %get-tuple-element.230), channel_id=1, source_target_pairs={{0,4},{4,8},{8,12},{12,16},{16,20},{20,24},{24,28},{28,32},{32,36}... | collective-permute-start | bytes 294920 | tf_op jit(solution)/shard_map/ppermute | solution.py:18
  118.4 75.9 %collective-permute-start.15 = (bf16[2,3,3,256]{3,2,1,0:T(4,128)(2,1)S(1)}, bf16[2,3,3,256]{3,2,1,0:T(4,128)(2,1)}, u32[]{:S(2)}, u32[]{:S(2)}) collective-permute-start(bf16[2,3,3,256]{3,2,1,0:T(4,128)(2,1)S(1)} %get-tuple-element.211), channel_id=1, source_target_pairs={{0,36},{4,40},{8,44},{12,48},{16,52},{20,56},{24,60},{28,64},{32,6... | collective-permute-start | bytes 27656 | tf_op jit(solution)/shard_map/ppermute | solution.py:18
  126.9 60.4 %collective-permute-start.13 = (bf16[2,3,3,256]{3,2,1,0:T(4,128)(2,1)S(1)}, bf16[2,3,3,256]{3,2,1,0:T(4,128)(2,1)}, u32[]{:S(2)}, u32[]{:S(2)}) collective-permute-start(bf16[2,3,3,256]{3,2,1,0:T(4,128)(2,1)S(1)} %get-tuple-element.212), channel_id=1, source_target_pairs={{0,28},{4,32},{8,36},{12,40},{16,44},{20,48},{24,52},{28,56},{32,6... | collective-permute-start | bytes 27656 | tf_op jit(solution)/shard_map/ppermute | solution.py:18
  142.0 28.4 %collective-permute-start.10 = (bf16[2,3,3,256]{3,2,1,0:T(4,128)(2,1)S(1)}, bf16[2,3,3,256]{3,2,1,0:T(4,128)(2,1)}, u32[]{:S(2)}, u32[]{:S(2)}) collective-permute-start(bf16[2,3,3,256]{3,2,1,0:T(4,128)(2,1)S(1)} %get-tuple-element.213), channel_id=1, source_target_pairs={{28,0},{32,4},{36,8},{40,12},{44,16},{48,20},{52,24},{56,28},{60,3... | collective-permute-start | bytes 27656 | tf_op jit(solution)/shard_map/ppermute | solution.py:18
  143.3 11.7 %collective-permute-start.8 = (bf16[2,3,3,256]{3,2,1,0:T(4,128)(2,1)S(1)}, bf16[2,3,3,256]{3,2,1,0:T(4,128)(2,1)S(1)}, u32[]{:S(2)}, u32[]{:S(2)}) collective-permute-start(bf16[2,3,3,256]{3,2,1,0:T(4,128)(2,1)S(1)} %get-tuple-element.214), channel_id=1, source_target_pairs={{36,0},{40,4},{44,8},{48,12},{52,16},{56,20},{60,24},{64,28},{68,3... | collective-permute-start | bytes 27656 | tf_op jit(solution)/shard_map/ppermute | solution.py:18
  146.1 46.6 %collective-permute-start.14 = (bf16[2,3,16,256]{3,2,1,0:T(8,128)(2,1)S(1)}, bf16[2,3,16,256]{3,2,1,0:T(8,128)(2,1)}, u32[]{:S(2)}, u32[]{:S(2)}) collective-permute-start(bf16[2,3,16,256]{3,2,1,0:T(8,128)(2,1)S(1)} %get-tuple-element.215), channel_id=1, source_target_pairs={{0,32},{4,36},{8,40},{12,44},{16,48},{20,52},{24,56},{28,60},{32,6... | collective-permute-start | bytes 147464 | tf_op jit(solution)/shard_map/ppermute | solution.py:18
  154.9 389.3 %reduce-scatter.4.cloned.1.call-start = ((), (), s32[]{:S(2)}) async-start(), calls=%async_computation.4 | async-start | bytes 1310720 | tf_op jit(solution)/shard_map/reduce_scatter | solution.py:146
  155.5 12.0 %collective-permute-start.9 = (bf16[2,3,16,256]{3,2,1,0:T(8,128)(2,1)}, bf16[2,3,16,256]{3,2,1,0:T(8,128)(2,1)}, u32[]{:S(2)}, u32[]{:S(2)}) collective-permute-start(bf16[2,3,16,256]{3,2,1,0:T(8,128)(2,1)} %get-tuple-element.216), channel_id=1, source_target_pairs={{32,0},{36,4},{40,8},{44,12},{48,16},{52,20},{56,24},{60,28},{64,3... | collective-permute-start | bytes 147464 | tf_op jit(solution)/shard_map/ppermute | solution.py:18
  157.5 40.3 %copy-start.8 = (bf16[32,16,1,256]{3,1,0,2:T(8,128)(2,1)S(1)}, bf16[32,16,1,256]{3,1,0,2:T(8,128)(2,1)}, u32[]{:S(2)}) copy-start(bf16[32,16,1,256]{3,1,0,2:T(8,128)(2,1)} %stack_reshape.3) | copy-start | bytes 786436
  167.5 14.6 %collective-permute-start.12 = (bf16[2,32,3,256]{3,2,1,0:T(4,128)(2,1)}, bf16[2,32,3,256]{3,2,1,0:T(4,128)(2,1)S(1)}, u32[]{:S(2)}, u32[]{:S(2)}) collective-permute-start(bf16[2,32,3,256]{3,2,1,0:T(4,128)(2,1)} %get-tuple-element.217), channel_id=1, source_target_pairs={{0,4},{4,8},{8,12},{12,16},{16,20},{20,24},{24,28},{28,32},{32,36}... | collective-permute-start | bytes 294920 | tf_op jit(solution)/shard_map/ppermute | solution.py:18
  170.4 7.1 collective-permute-start.11
  200.0 715.8 %reduce-scatter.6.cloned.1.call-start = ((), (), s32[]{:S(2)}) async-start(), calls=%async_computation.6 | async-start | bytes 3194880 | tf_op jit(solution)/shard_map/reduce_scatter | solution.py:132
  (9 other events, 38.2 us)
Sparse Core Ops, SparseCore 0:
  9.8 25.5 all-gather.2
  37.3 24.2 all-gather.4
  155.0 368.9 reduce-scatter.7
  527.2 16.9 reduce-scatter.3
  547.1 368.6 reduce-scatter.5
where the time goes:
time: 924 us; the launch traced here: 922 us
  waiting for transfers between devices  720 us (78%)
  local copies, waits for them, and re-layouts  65.6 us (7%)
  starting transfers between devices  62 us (7%)
  matrix products  30.4 us (3%)
  other arithmetic  29.6 us (3%)
  between operations  14.5 us (2%)
    reduce_scatter x1, waiting for transfers between devices, per_device(): lax.psum_scatter(term.reshape(lax.axis_size('grid') * (D // lax.axis_size...  372 us
    reduce_scatter x1, waiting for transfers between devices, per_device(): lax.psum_scatter(wout_term, 'grid', scatter_dimension=1, tiled=True)  316 us
    ppermute x16, starting transfers between devices, passed_along(): lax.ppermute(value, axis, [(source, source + steps) for source in range(i...  61.8 us
    reduce_scatter x1, waiting for transfers between devices, per_device(): lax.psum_scatter(lax.dot_general(piece, w_qkv, (((2, 3), (1, 2)), ((), ()...  20.1 us
  transfers between devices with their start and end apart: 21, of which 5 were waited for; matrix products, arithmetic and copies ran while one was open for 13% of the time, Pallas kernels for 0%

commit v1 on v0

v1 whole, which is shorter than its diff:
```python
import jax
import jax.numpy as jnp
from jax import lax
from jax.experimental import pallas as pl
from jax.experimental.pallas import tpu as pltpu
from jax.sharding import Mesh
from jax.sharding import PartitionSpec as P

D = 1024
HD = 64
HEADS_HERE = 4
FEAT = HD * HEADS_HERE
TH = 32
TW = 16
TOKENS = TH * TW
DEPTH = 3
IMG_H = 256
IMG_W = 128
PAD_H = TH + 2 * DEPTH
CENTER = PAD_H * TW
EDGE = DEPTH * TW
SLOTS = 4
BAND = 40 * SLOTS
BLOCKS = 4
BLK = TOKENS // BLOCKS
BLK_ROWS = TH // BLOCKS
K_MID = (BLK_ROWS + 2 * DEPTH) * TW
K_BAND = 16 * SLOTS
K_ALL = K_MID + 2 * K_BAND
Z, YH, X, YL, CORE = 8, 2, 4, 2, 2
GRID = ("z", "yh", "x")
YX = ("yh", "x")
HEAD = ("yl", "core")
F32 = jnp.float32
BF16 = jnp.bfloat16
VMEM_LIMIT = 40 * 1024 * 1024


def dot(a, b, ca, cb):
    return lax.dot_general(a, b, (((ca,), (cb,)), ((), ())), preferred_element_type=F32)


def call(body, out_shape, scratch=(), n_smem=0, n_in=0):
    specs = [pl.BlockSpec(memory_space=pltpu.SMEM)] * n_smem
    specs += [pl.BlockSpec(memory_space=pltpu.VMEM)] * (n_in - n_smem)
    outs = jax.tree.map(lambda _: pl.BlockSpec(memory_space=pltpu.VMEM), out_shape)
    return pl.pallas_call(
        body,
        out_shape=out_shape,
        in_specs=specs,
        out_specs=outs,
        scratch_shapes=list(scratch),
        compiler_params=pltpu.CompilerParams(vmem_limit_bytes=VMEM_LIMIT),
    )


def shaped(shape, dtype=BF16):
    return jax.ShapeDtypeStruct(shape, dtype)


def pick(first_col, token_axis):
    shape = (CENTER, BAND) if token_axis == 0 else (BAND, CENTER)
    token = lax.broadcasted_iota(jnp.int32, shape, token_axis)
    slot = lax.broadcasted_iota(jnp.int32, shape, 1 - token_axis)
    lane = slot & (SLOTS - 1)
    wanted = (slot // SLOTS) * TW + first_col + lane
    return jnp.where((token == wanted) & (lane < DEPTH), 1.0, 0.0).astype(BF16)


def bands_kernel(k, v, above, below, to_left, to_right):
    left = pick(0, 1)
    right = pick(TW - DEPTH, 1)
    for i, own in enumerate((k, v)):
        mid = jnp.concatenate([above[i], own[...], below[i]], axis=0)
        to_left[i] = dot(left, mid, 1, 0).astype(BF16)
        to_right[i] = dot(right, mid, 1, 0).astype(BF16)


def stacked(x):
    lane = lax.broadcasted_iota(jnp.int32, x.shape, 1) // HD
    zero = jnp.zeros_like(x)
    return jnp.concatenate([jnp.where(lane == h, x, zero) for h in range(HEADS_HERE)], axis=0)


def unstacked(x):
    lane = lax.broadcasted_iota(jnp.int32, (BLK, FEAT), 1) // HD
    out = x[:BLK]
    for h in range(1, HEADS_HERE):
        out = jnp.where(lane == h, x[h * BLK : (h + 1) * BLK], out)
    return out


def attention_kernel(
    place, q, og0, og1, og2, og3, w_out, k, v, above, below, from_left, from_right,
    attn_out, grad_q, grad_mid, band_left, band_right,
    mid, ga, gl, gr,
):
    head = place[0]
    tile_row = place[1]
    tile_col = place[2]
    for i, own in enumerate((k, v)):
        mid[i, :EDGE] = above[i]
        mid[i, EDGE : EDGE + TOKENS] = own[...]
        mid[i, EDGE + TOKENS :] = below[i]
    for i, piece in enumerate((og0, og1, og2, og3)):
        at = pl.multiple_of((head ^ i) * BLK, BLK)
        ga[pl.ds(at, BLK), :] = dot(piece[...], w_out[...], 1, 1).astype(BF16)
    grad_mid[...] = jnp.zeros_like(grad_mid)
    gl[...] = jnp.zeros_like(gl)
    gr[...] = jnp.zeros_like(gr)

    key = lax.broadcasted_iota(jnp.int32, (1, K_ALL), 1)
    in_mid = key < K_MID
    in_left = key < K_MID + K_BAND
    slot = key & (SLOTS - 1)
    key_row = jnp.where(
        in_mid,
        key // TW,
        jnp.where(in_left, (key - K_MID) // SLOTS, (key - K_MID - K_BAND) // SLOTS),
    )
    band_col = jnp.where(in_left, slot, TW + DEPTH + slot)
    key_col = jnp.where(in_mid, (key & (TW - 1)) + DEPTH, jnp.where(slot < DEPTH, band_col, 1000))
    col_image = tile_col * TW + key_col - DEPTH
    key_col = jnp.where((col_image >= 0) & (col_image < IMG_W), key_col, 1000)
    token = lax.broadcasted_iota(jnp.int32, (BLK, 1), 0)
    row_off = key_row - token // TW
    col_off = key_col - (token & (TW - 1))
    near = (row_off >= 0) & (row_off < 7) & (col_off >= 0) & (col_off < 7)
    row_image = tile_row * TH + key_row - DEPTH

    for b in range(BLOCKS):
        row_here = row_image + b * BLK_ROWS
        valid = near & (row_here >= 0) & (row_here < IMG_H)
        bias = jnp.where(valid, 0.0, -jnp.inf).astype(F32)
        rows = slice(b * BLK, (b + 1) * BLK)
        m_rows = slice(b * BLK, b * BLK + K_MID)
        b_rows = slice(b * BLK_ROWS * SLOTS, b * BLK_ROWS * SLOTS + K_BAND)
        kk = jnp.concatenate([mid[0, m_rows], from_left[0, b_rows], from_right[0, b_rows]], axis=0)
        vv = jnp.concatenate([mid[1, m_rows], from_left[1, b_rows], from_right[1, b_rows]], axis=0)
        qs = stacked(q[rows, :] * jnp.asarray(HD**-0.5, BF16))
        gs = stacked(ga[rows, :])
        s = dot(qs, kk, 1, 1).reshape(HEADS_HERE, BLK, K_ALL) + bias[None]
        s = s.reshape(HEADS_HERE * BLK, K_ALL)
        e = jnp.exp(s - jnp.max(s, axis=1, keepdims=True))
        p = e * (1.0 / jnp.sum(e, axis=1, keepdims=True))
        p16 = p.astype(BF16)
        attn = dot(p16, vv, 1, 0).astype(BF16)
        attn_out[rows, :] = unstacked(attn)
        delta = jnp.sum(gs.astype(F32) * attn.astype(F32), axis=1, keepdims=True)
        ds = (p * (dot(gs, vv, 1, 1) - delta)).astype(BF16)
        grad_q[rows, :] = unstacked(dot(ds, kk, 1, 0) * (HD**-0.5)).astype(BF16)
        for i, g in enumerate((dot(ds, qs, 0, 0), dot(p16, gs, 0, 0))):
            grad_mid[i, m_rows] += g[:K_MID]
            gl[i, b_rows] += g[K_MID : K_MID + K_BAND]
            gr[i, b_rows] += g[K_MID + K_BAND :]
    band_left[...] = gl[...].astype(BF16)
    band_right[...] = gr[...].astype(BF16)


def put_term(out, cols, term):
    term = term.astype(BF16)
    for yx in range(YH * X):
        for z in range(Z):
            at = (z * YH * X + yx) * 16
            out[yx, z, :, cols] = term[at : at + 16]


def first_terms_kernel(place, hidden, grad_q, og0, og1, og2, og3, attn, out, og):
    head = place[0]
    for i, piece in enumerate((og0, og1, og2, og3)):
        og[pl.ds(pl.multiple_of((head ^ i) * BLK, BLK), BLK), :] = piece[...]
    put_term(out, slice(0, FEAT), dot(hidden[...], grad_q[...], 0, 0))
    put_term(out, slice(FEAT, 2 * FEAT), dot(og[...], attn[...], 0, 0))


def columns_kernel(grad_mid, from_left, from_right, inner, to_above, to_below):
    left = pick(0, 0)
    right = pick(TW - DEPTH, 0)
    for i in range(2):
        g = grad_mid[i] + dot(left, from_left[i], 1, 0) + dot(right, from_right[i], 1, 0)
        to_above[i] = g[:EDGE].astype(BF16)
        inner[i] = g[EDGE : EDGE + TOKENS]
        to_below[i] = g[EDGE + TOKENS :].astype(BF16)


def second_terms_kernel(
    place, inner, from_above, from_below, grad_q, hidden, w_qkv, terms, keep, send, grads
):
    core = place[3]
    grads[0] = grad_q[...]
    for i in range(2):
        grads[1 + i, :EDGE] = (inner[i, :EDGE] + from_above[i].astype(F32)).astype(BF16)
        grads[1 + i, EDGE : TOKENS - EDGE] = inner[i, EDGE : TOKENS - EDGE].astype(BF16)
        last = inner[i, TOKENS - EDGE :] + from_below[i].astype(F32)
        grads[1 + i, TOKENS - EDGE :] = last.astype(BF16)
    for yl in range(YL):
        for out, c in ((send, 1 - core), (keep, core)):
            at = pl.ds(pl.multiple_of((yl * CORE + c) * BLK, BLK), BLK)
            total = dot(grads[0, at, :], w_qkv[0], 1, 1)
            for j in (1, 2):
                total += dot(grads[j, at, :], w_qkv[j], 1, 1)
            out[yl] = total.astype(BF16)
    for i in range(2):
        put_term(terms, slice(i * FEAT, (i + 1) * FEAT), dot(hidden[...], grads[1 + i], 0, 0))


def halve_kernel(place, keep, got, stay, send):
    yl = place[4]
    stay[...] = keep[yl].astype(F32) + got[yl].astype(F32)
    send[...] = (keep[1 - yl].astype(F32) + got[1 - yl].astype(F32)).astype(BF16)


def add_terms_kernel(first, second, out):
    for i, terms in enumerate((first, second)):
        total = terms[0].astype(F32)
        for yx in range(1, YH * X):
            total += terms[yx].astype(F32)
        out[:, :, i * 2 * FEAT : (i + 1) * 2 * FEAT] = total.astype(BF16)


def ring(size, step):
    return [(i, (i + step) % size) for i in range(size)]


SWAP = [(0, 1), (1, 0)]


def per_device(hidden_in, queries, keys, values, w_qkv, w_out, out_grad):
    yl = lax.axis_index("yl")
    core = lax.axis_index("core")
    place = jnp.stack(
        [yl * CORE + core, lax.axis_index("z"), lax.axis_index(YX), core, yl]
    ).astype(jnp.int32)
    q = queries.reshape(TOKENS, FEAT)
    k = keys.reshape(TOKENS, FEAT)
    v = values.reshape(TOKENS, FEAT)
    w3 = w_qkv.transpose(1, 0, 2)

    og0 = out_grad.reshape(BLK, D)
    og2 = lax.ppermute(og0, "yl", SWAP)
    og1 = lax.ppermute(og0, "core", SWAP)
    og3 = lax.ppermute(og2, "core", SWAP)
    pieces = (og0, og1, og2, og3)

    below = lax.ppermute(jnp.stack([k[:EDGE], v[:EDGE]]), "z", ring(Z, -1))
    above = lax.ppermute(jnp.stack([k[-EDGE:], v[-EDGE:]]), "z", ring(Z, 1))
    band = shaped((2, BAND, FEAT))
    to_left, to_right = call(bands_kernel, (band, band), n_in=4)(k, v, above, below)
    from_right = lax.ppermute(to_left, YX, ring(YH * X, -1))
    from_left = lax.ppermute(to_right, YX, ring(YH * X, 1))
    hidden = lax.all_gather(hidden_in, HEAD, axis=1, tiled=True).reshape(TOKENS, D)

    flat = shaped((TOKENS, FEAT))
    attn, grad_q, grad_mid, band_left, band_right = call(
        attention_kernel,
        (flat, flat, shaped((2, CENTER, FEAT), F32), band, band),
        scratch=[
            pltpu.VMEM((2, CENTER, FEAT), BF16),
            pltpu.VMEM((TOKENS, FEAT), BF16),
            pltpu.VMEM((2, BAND, FEAT), F32),
            pltpu.VMEM((2, BAND, FEAT), F32),
        ],
        n_smem=1,
        n_in=13,
    )(place, q, *pieces, w_out, k, v, above, below, from_left, from_right)

    got_right = lax.ppermute(band_left, YX, ring(YH * X, -1))
    got_left = lax.ppermute(band_right, YX, ring(YH * X, 1))
    terms = shaped((YH * X, Z, 16, 2 * FEAT))
    first = call(
        first_terms_kernel, terms, scratch=[pltpu.VMEM((TOKENS, D), BF16)], n_smem=1, n_in=8
    )(place, hidden, grad_q, *pieces, attn)
    edge = shaped((2, EDGE, FEAT))
    inner, to_above, to_below = call(
        columns_kernel, (shaped((2, TOKENS, FEAT), F32), edge, edge), n_in=3
    )(grad_mid, got_left, got_right)
    got_below = lax.ppermute(to_above, "z", ring(Z, -1))
    got_above = lax.ppermute(to_below, "z", ring(Z, 1))
    first, inner = lax.optimization_barrier((first, inner))
    first = lax.all_to_all(first, YX, 0, 0, tiled=True)

    half = shaped((YL, BLK, D))
    second, keep, send = call(
        second_terms_kernel,
        (terms, half, half),
        scratch=[pltpu.VMEM((3, TOKENS, FEAT), BF16)],
        n_smem=1,
        n_in=7,
    )(place, inner, got_above, got_below, grad_q, hidden, w3)
    got = lax.ppermute(send, "core", SWAP)
    stay, send = call(halve_kernel, (shaped((BLK, D), F32), shaped((BLK, D))), n_smem=1, n_in=3)(
        place, keep, got
    )
    got = lax.ppermute(send, "yl", SWAP)
    second, stay = lax.optimization_barrier((second, stay))
    second = lax.all_to_all(second, YX, 0, 0, tiled=True)
    grad_hidden = (stay + got.astype(F32)).astype(BF16).reshape(1, 8, TW, D)

    partial = call(add_terms_kernel, shaped((Z, 16, 4 * FEAT)), n_in=2)(first, second)
    partial = lax.all_to_all(partial, "z", 0, 0, tiled=True)
    total = jnp.sum(partial.astype(F32), axis=0)
    grad_wout = total[:, FEAT : 2 * FEAT].T
    grad_wqkv = jnp.stack(
        [total[:, :FEAT], total[:, 2 * FEAT : 3 * FEAT], total[:, 3 * FEAT :]], axis=1
    )
    return grad_hidden, grad_wqkv, grad_wout


def solution(mesh):
    fine = Mesh(mesh.devices.reshape(Z, YH, X, YL, CORE), GRID + HEAD)
    return jax.shard_map(
        per_device,
        mesh=fine,
        in_specs=(
            P(GRID, HEAD, None, None),
            P(GRID, None, None, HEAD),
            P(GRID, None, None, HEAD),
            P(GRID, None, None, HEAD),
            P(None, None, HEAD),
            P(HEAD, None),
            P(GRID, HEAD, None, None),
        ),
        out_specs=(P(GRID, HEAD, None, None), P(GRID, None, HEAD), P(HEAD, GRID)),
        check_vma=False,
    )
```

time: 924 us -> 131 us (0.14)
  waiting for transfers between devices: 720 us -> 46.3 us
  local copies, waits for them, and re-layouts: 65.6 us -> 10.6 us
  matrix products: 30.4 us -> 0 us
  other arithmetic: 29.6 us -> 1.43 us
  starting transfers between devices: 62 us -> 42.7 us
  Pallas kernels: 0 us -> 15 us
    reduce_scatter x3 -> x0, waiting for transfers between devices: 707 us -> none  [the longest x1 372 us: per_device(): lax.psum_scatter(term.reshape(lax.axis_size('grid') * (D // lax.axis_size...]
    ppermute x16 -> x13, starting transfers between devices: 61.8 us -> 24 us  [the longest x1 5.93 us: per_device(): below = lax.ppermute(jnp.stack([k[:EDGE], v[:EDGE]]), 'z', ring(Z, -1))]
    all_to_all x0 -> x3, waiting for transfers between devices: none -> 28.7 us  [the longest x1 16.9 us: per_device(): second = lax.all_to_all(second, YX, 0, 0, tiled=True)]
    dot_general x9 -> x0, matrix products: 23.9 us -> none  [the longest x1 4.23 us: neighbour_pass(): jnp.einsum('htk,the->khe', probs16, grad_attn, preferred_element_type=jnp...]
    all_to_all x0 -> x3, starting transfers between devices: none -> 18.6 us  [the longest x1 7.04 us: per_device(): first = lax.all_to_all(first, YX, 0, 0, tiled=True)]
    pallas_call x0 -> x7, Pallas kernels: none -> 15 us  [the longest x1 5.88 us: per_device(): call(attention_kernel, (flat, flat, shaped((2, CENTER, FEAT), F32), band,...]
    scatter-add x6 -> x0, local copies, waits for them, and re-layouts: 14.7 us -> none  [per_device(): inner = inner.at[:, put_r[0]:put_r[1], put_c[0]:put_c[1]].add(got)]
    another operation x12 -> x1, local copies, waits for them, and re-layouts: 12.1 us -> 0.08 us  [per_device(): jnp.stack([yl * CORE + core, lax.axis_index('z'), lax.axis_index(YX), cor...]
  transfers between devices with their start and end apart: 21 -> 17, of which waited for: 5 -> 9; matrix products, arithmetic and copies ran while one was open for 13% -> 2% of each run, Pallas kernels for 0% -> 10%
where the time goes in v1:
time: 131 us; the launch traced here: 130 us
  waiting for transfers between devices  46.3 us (35%)
  starting transfers between devices  42.7 us (33%)
  Pallas kernels  15 us (11%)
  between operations  14.2 us (11%)
  local copies, waits for them, and re-layouts  10.6 us (8%)
  other arithmetic  1.43 us (1%)
    all_to_all x1, waiting for transfers between devices, per_device(): second = lax.all_to_all(second, YX, 0, 0, tiled=True)  16.9 us
    all_to_all x1, waiting for transfers between devices, per_device(): partial = lax.all_to_all(partial, 'z', 0, 0, tiled=True)  10.9 us
    unnamed x22, local copies, waits for them, and re-layouts  8.34 us
    all_to_all x1, starting transfers between devices, per_device(): first = lax.all_to_all(first, YX, 0, 0, tiled=True)  7.04 us
    all_to_all x1, starting transfers between devices, per_device(): second = lax.all_to_all(second, YX, 0, 0, tiled=True)  6.38 us
    ppermute x1, starting transfers between devices, per_device(): below = lax.ppermute(jnp.stack([k[:EDGE], v[:EDGE]]), 'z', ring(Z, -1))  5.93 us
    pallas_call x1, Pallas kernels, per_device(): call(attention_kernel, (flat, flat, shaped((2, CENTER, FEAT), F32), band,...  5.88 us
    ppermute x1, starting transfers between devices, per_device(): got_right = lax.ppermute(band_left, YX, ring(YH * X, -1))  5.63 us
  transfers between devices with their start and end apart: 17, of which 9 were waited for; matrix products, arithmetic and copies ran while one was open for 2% of the time, Pallas kernels for 10%

profile of v1, /device:TPU:8, one launch (start us, length us, event | category | flops | bytes accessed | tf_op | source)
XLA Modules:
  0.0 130.1 jit_solution(1809536612695010331)
XLA Ops:
  7.9 2.3 %collective-permute-start.1 = (bf16[128,1024]{1,0:T(8,128)(2,1)}, bf16[128,1024]{1,0:T(8,128)(2,1)S(1)}, u32[]{:S(2)}, u32[]{:S(2)}) collective-permute-start(bf16[128,1024]{1,0:T(8,128)(2,1)} %bitcast.32), channel_id=1, source_target_pairs={{0,2},{2,0},{1,3},{3,1},{4,6},{6,4},{5,7},{7,5},{8,10},{10,8},{9,1... | collective-permute-start | bytes 786440 | tf_op jit(solution)/shard_map/ppermute | solution.py:240
  12.0 4.3 %collective-permute-done.1.og2 = bf16[128,1024]{1,0:T(8,128)(2,1)S(1)} collective-permute-done((bf16[128,1024]{1,0:T(8,128)(2,1)}, bf16[128,1024]{1,0:T(8,128)(2,1)S(1)}, u32[]{:S(2)}, u32[]{:S(2)}) %collective-permute-start.1) | collective-permute-done | bytes 262176 | tf_op jit(solution)/shard_map/ppermute | solution.py:240
  16.3 5.9 %collective-permute-start.4 = (bf16[2,48,256]{2,1,0:T(8,128)(2,1)S(1)}, bf16[2,48,256]{2,1,0:T(8,128)(2,1)S(1)}, u32[]{:S(2)}, u32[]{:S(2)}) collective-permute-start(bf16[2,48,256]{2,1,0:T(8,128)(2,1)S(1)} %pad_maximum_fusion.1), channel_id=1, source_target_pairs={{0,224},{32,0},{64,32},{96,64},{128,96},{160,128},{192,160},{224,1... | collective-permute-start | bytes 147464 | tf_op jit(solution)/shard_map/ppermute | solution.py:245
  22.2 1.7 %collective-permute-done.4.below = bf16[2,48,256]{2,1,0:T(8,128)(2,1)S(1)} collective-permute-done((bf16[2,48,256]{2,1,0:T(8,128)(2,1)S(1)}, bf16[2,48,256]{2,1,0:T(8,128)(2,1)S(1)}, u32[]{:S(2)}, u32[]{:S(2)}) %collective-permute-start.4) | collective-permute-done | bytes 49184 | tf_op jit(solution)/shard_map/ppermute | solution.py:245
  24.0 1.0 copy-done.3
  26.3 1.6 %collective-permute-start.5 = (bf16[2,160,256]{2,1,0:T(8,128)(2,1)S(1)}, bf16[2,160,256]{2,1,0:T(8,128)(2,1)S(1)}, u32[]{:S(2)}, u32[]{:S(2)}) collective-permute-start(bf16[2,160,256]{2,1,0:T(8,128)(2,1)S(1)} %get-tuple-element.22), channel_id=1, source_target_pairs={{0,4},{4,8},{8,12},{12,16},{16,20},{20,24},{24,28},{28,0},{1,5},{5... | collective-permute-start | bytes 491528 | tf_op jit(solution)/shard_map/ppermute | solution.py:250
  27.9 4.2 %collective-permute-start.6 = (bf16[2,160,256]{2,1,0:T(8,128)(2,1)S(1)}, bf16[2,160,256]{2,1,0:T(8,128)(2,1)S(1)}, u32[]{:S(2)}, u32[]{:S(2)}) collective-permute-start(bf16[2,160,256]{2,1,0:T(8,128)(2,1)S(1)} %get-tuple-element.23), channel_id=1, source_target_pairs={{0,28},{4,0},{8,4},{12,8},{16,12},{20,16},{24,20},{28,24},{1,29},{... | collective-permute-start | bytes 491528 | tf_op jit(solution)/shard_map/ppermute | solution.py:249
  32.1 3.7 %collective-permute-done.5.from_left = bf16[2,160,256]{2,1,0:T(8,128)(2,1)S(1)} collective-permute-done((bf16[2,160,256]{2,1,0:T(8,128)(2,1)S(1)}, bf16[2,160,256]{2,1,0:T(8,128)(2,1)S(1)}, u32[]{:S(2)}, u32[]{:S(2)}) %collective-permute-start.5) | collective-permute-done | bytes 163872 | tf_op jit(solution)/shard_map/ppermute | solution.py:250
  39.6 5.9 %shard_map.95 = (bf16[512,256]{1,0:T(8,128)(2,1)S(1)}, bf16[512,256]{1,0:T(8,128)(2,1)S(1)}, f32[2,608,256]{2,1,0:T(8,128)S(1)}, bf16[2,160,256]{2,1,0:T(8,128)(2,1)S(1)}, bf16[2,160,256]{2,1,0:T(8,128)(2,1)S(1)}) custom-call(s32[5]{0:T(128)S(1)} %stack.53.place, bf16[512,256]{1,0:T(8,128)(2,1)S(1)} %bitcast.36, bf16[128,1024]{1,0:T(8,128)(2,1)S(1)} %bitcast.34, ...), custom_call_target="tpu_custom_call" | custom-call | tf_op jit(solution)/shard_map/pallas_call | solution.py:254
  45.6 5.6 %collective-permute-start.8 = (bf16[2,160,256]{2,1,0:T(8,128)(2,1)S(1)}, bf16[2,160,256]{2,1,0:T(8,128)(2,1)S(1)}, u32[]{:S(2)}, u32[]{:S(2)}) collective-permute-start(bf16[2,160,256]{2,1,0:T(8,128)(2,1)S(1)} %get-tuple-element.28), channel_id=1, source_target_pairs={{0,28},{4,0},{8,4},{12,8},{16,12},{20,16},{24,20},{28,24},{1,29},{... | collective-permute-start | bytes 491528 | tf_op jit(solution)/shard_map/ppermute | solution.py:267
  51.2 3.3 %collective-permute-done.7.from_left = bf16[2,160,256]{2,1,0:T(8,128)(2,1)S(1)} collective-permute-done((bf16[2,160,256]{2,1,0:T(8,128)(2,1)S(1)}, bf16[2,160,256]{2,1,0:T(8,128)(2,1)S(1)}, u32[]{:S(2)}, u32[]{:S(2)}) %collective-permute-start.7) | collective-permute-done | bytes 163872 | tf_op jit(solution)/shard_map/ppermute | solution.py:268
  55.1 1.2 copy-done
  56.3 2.4 %shard_map.96 = bf16[8,8,16,512]{3,2,1,0:T(8,128)(2,1)} custom-call(s32[5]{0:T(128)S(1)} %stack.53.place, bf16[512,1024]{1,0:T(8,128)(2,1)S(1)} %bitcast.25, bf16[512,256]{1,0:T(8,128)(2,1)S(1)} %get-tuple-element.24.grad_q, bf16[128,1024]{1,0:T(8,128)(2,1)S(1)} %bitcast.35, bf16[128,1024]{1,0:T(8,128)(2,1)S(1)} %collective-permute-done.og1, ...), custom_call_target="tpu_custom_call" | custom-call | tf_op jit(solution)/shard_map/pallas_call | solution.py:270
  58.6 7.0 %all-to-all-start = ((bf16[8,8,16,512]{3,2,1,0:T(8,128)(2,1)}), bf16[8,8,16,512]{3,2,1,0:T(8,128)(2,1)S(1)}, u32[]{:S(2)}, u32[]{:S(2)}) async-start(bf16[8,8,16,512]{3,2,1,0:T(8,128)(2,1)} %shard_map.96), calls=%async_computation | async-start | bytes 2097152 | tf_op jit(solution)/shard_map/all_to_all | solution.py:280
  65.7 3.5 %collective-permute-start.10 = (bf16[2,48,256]{2,1,0:T(8,128)(2,1)S(1)}, bf16[2,48,256]{2,1,0:T(8,128)(2,1)S(1)}, u32[]{:S(2)}, u32[]{:S(2)}) collective-permute-start(bf16[2,48,256]{2,1,0:T(8,128)(2,1)S(1)} %get-tuple-element.32), channel_id=1, source_target_pairs={{0,224},{32,0},{64,32},{96,64},{128,96},{160,128},{192,160},{224,1... | collective-permute-start | bytes 147464 | tf_op jit(solution)/shard_map/ppermute | solution.py:277
  69.2 2.0 %collective-permute-done.9.from_above = bf16[2,48,256]{2,1,0:T(8,128)(2,1)S(1)} collective-permute-done((bf16[2,48,256]{2,1,0:T(8,128)(2,1)S(1)}, bf16[2,48,256]{2,1,0:T(8,128)(2,1)S(1)}, u32[]{:S(2)}, u32[]{:S(2)}) %collective-permute-start.9) | collective-permute-done | bytes 49184 | tf_op jit(solution)/shard_map/ppermute | solution.py:278
  71.2 1.4 %copy-done.2 = bf16[1024,3,256]{2,0,1:T(8,128)(2,1)S(1)} copy-done((bf16[1024,3,256]{2,0,1:T(8,128)(2,1)S(1)}, bf16[1024,3,256]{2,0,1:T(8,128)(2,1)}, u32[]{:S(2)}) %copy-start.2) | copy-done | bytes 1572888
  72.6 4.2 %shard_map.98 = (bf16[8,8,16,512]{3,2,1,0:T(8,128)(2,1)}, bf16[2,128,1024]{2,1,0:T(8,128)(2,1)S(1)}, bf16[2,128,1024]{2,1,0:T(8,128)(2,1)S(1)}) custom-call(s32[5]{0:T(128)S(1)} %stack.53.place, f32[2,512,256]{2,1,0:T(8,128)S(1)} %get-tuple-element.30.inner, bf16[2,48,256]{2,1,0:T(8,128)(2,1)S(1)} %collective-permute-done.9.from_above, ...), custom_call_target="tpu_custom_call" | custom-call | tf_op jit(solution)/shard_map/pallas_call | solution.py:283
  76.8 1.9 %collective-permute-done.11.got = bf16[2,128,1024]{2,1,0:T(8,128)(2,1)S(1)} collective-permute-done((bf16[2,128,1024]{2,1,0:T(8,128)(2,1)S(1)}, bf16[2,128,1024]{2,1,0:T(8,128)(2,1)S(1)}, u32[]{:S(2)}, u32[]{:S(2)}) %collective-permute-start.11) | collective-permute-done | bytes 524320 | tf_op jit(solution)/shard_map/ppermute | solution.py:290
  80.2 6.4 %all-to-all-start.1 = ((bf16[8,8,16,512]{3,2,1,0:T(8,128)(2,1)}), bf16[8,8,16,512]{3,2,1,0:T(8,128)(2,1)S(1)}, u32[]{:S(2)}, u32[]{:S(2)}) async-start(bf16[8,8,16,512]{3,2,1,0:T(8,128)(2,1)} %get-tuple-element.40), calls=%async_computation.1 | async-start | bytes 2097152 | tf_op jit(solution)/shard_map/all_to_all | solution.py:296
  87.3 16.9 %all-to-all-done.1.second = bf16[8,8,16,512]{3,2,1,0:T(8,128)(2,1)S(1)} async-done(((bf16[8,8,16,512]{3,2,1,0:T(8,128)(2,1)}), bf16[8,8,16,512]{3,2,1,0:T(8,128)(2,1)S(1)}, u32[]{:S(2)}, u32[]{:S(2)}) %all-to-all-start.1) | async-done | bytes 1048608 | tf_op jit(solution)/shard_map/all_to_all | solution.py:296
  104.2 1.0 shard_map.100
  105.2 5.2 %all-to-all-start.2 = ((bf16[8,16,1024]{2,1,0:T(8,128)(2,1)}), bf16[8,16,1024]{2,1,0:T(8,128)(2,1)S(1)}, u32[]{:S(2)}, u32[]{:S(2)}) async-start(bf16[8,16,1024]{2,1,0:T(8,128)(2,1)} %shard_map.100), calls=%async_computation.2 | async-start | bytes 524288 | tf_op jit(solution)/shard_map/all_to_all | solution.py:300
  111.1 10.9 %all-to-all-done.2 = bf16[8,16,1024]{2,1,0:T(8,128)(2,1)S(1)} async-done(((bf16[8,16,1024]{2,1,0:T(8,128)(2,1)}), bf16[8,16,1024]{2,1,0:T(8,128)(2,1)S(1)}, u32[]{:S(2)}, u32[]{:S(2)}) %all-to-all-start.2) | async-done | bytes 262176 | tf_op jit(solution)/shard_map/all_to_all | solution.py:300
  (49 shorter events, 12.6 us)
Async XLA Ops:
  7.2 28.6 %copy-start.9 = (bf16[256,1024]{1,0:T(8,128)(2,1)S(1)}, bf16[256,1024]{1,0:T(8,128)(2,1)}, u32[]{:S(2)}) copy-start(bf16[256,1024]{1,0:T(8,128)(2,1)} %w_out.1) | copy-start | bytes 1572868
  7.2 47.9 %all-gather.2.cloned.1.call-start = ((), (), s32[]{:S(2)}) async-start(), calls=%async_computation.3 | async-start | bytes 1310720 | tf_op jit(solution)/shard_map/all_gather | solution.py:251
  7.9 8.3 %collective-permute-start.1 = (bf16[128,1024]{1,0:T(8,128)(2,1)}, bf16[128,1024]{1,0:T(8,128)(2,1)S(1)}, u32[]{:S(2)}, u32[]{:S(2)}) collective-permute-start(bf16[128,1024]{1,0:T(8,128)(2,1)} %bitcast.32), channel_id=1, source_target_pairs={{0,2},{2,0},{1,3},{3,1},{4,6},{6,4},{5,7},{7,5},{8,10},{10,8},{9,1... | collective-permute-start | bytes 786440 | tf_op jit(solution)/shard_map/ppermute | solution.py:240
  10.2 25.6 %collective-permute-start = (bf16[128,1024]{1,0:T(8,128)(2,1)}, bf16[128,1024]{1,0:T(8,128)(2,1)S(1)}, u32[]{:S(2)}, u32[]{:S(2)}) collective-permute-start(bf16[128,1024]{1,0:T(8,128)(2,1)} %bitcast.33), channel_id=1, source_target_pairs={{0,1},{1,0},{2,3},{3,2},{4,5},{5,4},{6,7},{7,6},{8,9},{9,8},{10,11... | collective-permute-start | bytes 786440 | tf_op jit(solution)/shard_map/ppermute | solution.py:241
  11.7 10.5 %collective-permute-start.3 = (bf16[2,48,256]{2,1,0:T(8,128)(2,1)S(1)}, bf16[2,48,256]{2,1,0:T(8,128)(2,1)S(1)}, u32[]{:S(2)}, u32[]{:S(2)}) collective-permute-start(bf16[2,48,256]{2,1,0:T(8,128)(2,1)S(1)} %pad_maximum_fusion), channel_id=1, source_target_pairs={{0,32},{32,64},{64,96},{96,128},{128,160},{160,192},{192,224},{224... | collective-permute-start | bytes 147464 | tf_op jit(solution)/shard_map/ppermute | solution.py:246
  16.3 19.6 %collective-permute-start.2 = (bf16[128,1024]{1,0:T(8,128)(2,1)S(1)}, bf16[128,1024]{1,0:T(8,128)(2,1)S(1)}, u32[]{:S(2)}, u32[]{:S(2)}) collective-permute-start(bf16[128,1024]{1,0:T(8,128)(2,1)S(1)} %collective-permute-done.1.og2), channel_id=1, source_target_pairs={{0,1},{1,0},{2,3},{3,2},{4,5},{5,4},{6,7},{7,6},{8,9},{9,8},{10,11... | collective-permute-start | bytes 786440 | tf_op jit(solution)/shard_map/ppermute | solution.py:242
  16.3 7.7 %collective-permute-start.4 = (bf16[2,48,256]{2,1,0:T(8,128)(2,1)S(1)}, bf16[2,48,256]{2,1,0:T(8,128)(2,1)S(1)}, u32[]{:S(2)}, u32[]{:S(2)}) collective-permute-start(bf16[2,48,256]{2,1,0:T(8,128)(2,1)S(1)} %pad_maximum_fusion.1), channel_id=1, source_target_pairs={{0,224},{32,0},{64,32},{96,64},{128,96},{160,128},{192,160},{224,1... | collective-permute-start | bytes 147464 | tf_op jit(solution)/shard_map/ppermute | solution.py:245
  23.9 1.0 copy-start.3
  26.3 9.5 %collective-permute-start.5 = (bf16[2,160,256]{2,1,0:T(8,128)(2,1)S(1)}, bf16[2,160,256]{2,1,0:T(8,128)(2,1)S(1)}, u32[]{:S(2)}, u32[]{:S(2)}) collective-permute-start(bf16[2,160,256]{2,1,0:T(8,128)(2,1)S(1)} %get-tuple-element.22), channel_id=1, source_target_pairs={{0,4},{4,8},{8,12},{12,16},{16,20},{20,24},{24,28},{28,0},{1,5},{5... | collective-permute-start | bytes 491528 | tf_op jit(solution)/shard_map/ppermute | solution.py:250
  27.9 7.9 %collective-permute-start.6 = (bf16[2,160,256]{2,1,0:T(8,128)(2,1)S(1)}, bf16[2,160,256]{2,1,0:T(8,128)(2,1)S(1)}, u32[]{:S(2)}, u32[]{:S(2)}) collective-permute-start(bf16[2,160,256]{2,1,0:T(8,128)(2,1)S(1)} %get-tuple-element.23), channel_id=1, source_target_pairs={{0,28},{4,0},{8,4},{12,8},{16,12},{20,16},{24,20},{28,24},{1,29},{... | collective-permute-start | bytes 491528 | tf_op jit(solution)/shard_map/ppermute | solution.py:249
  35.8 1.0 copy-start.4
  39.6 15.4 %copy-start.8 = (bf16[1,8,16,1024]{3,2,1,0:T(8,128)(2,1)S(1)}, bf16[1,8,16,1024]{3,2,1,0:T(8,128)(2,1)}, u32[]{:S(2)}) copy-start(bf16[1,8,16,1024]{3,2,1,0:T(8,128)(2,1)} %param.13) | copy-start | bytes 786436
  45.5 9.0 %collective-permute-start.7 = (bf16[2,160,256]{2,1,0:T(8,128)(2,1)S(1)}, bf16[2,160,256]{2,1,0:T(8,128)(2,1)S(1)}, u32[]{:S(2)}, u32[]{:S(2)}) collective-permute-start(bf16[2,160,256]{2,1,0:T(8,128)(2,1)S(1)} %get-tuple-element.27), channel_id=1, source_target_pairs={{0,4},{4,8},{8,12},{12,16},{16,20},{20,24},{24,28},{28,0},{1,5},{5... | collective-permute-start | bytes 491528 | tf_op jit(solution)/shard_map/ppermute | solution.py:268
  45.6 8.9 %collective-permute-start.8 = (bf16[2,160,256]{2,1,0:T(8,128)(2,1)S(1)}, bf16[2,160,256]{2,1,0:T(8,128)(2,1)S(1)}, u32[]{:S(2)}, u32[]{:S(2)}) collective-permute-start(bf16[2,160,256]{2,1,0:T(8,128)(2,1)S(1)} %get-tuple-element.28), channel_id=1, source_target_pairs={{0,28},{4,0},{8,4},{12,8},{16,12},{20,16},{24,20},{28,24},{1,29},{... | collective-permute-start | bytes 491528 | tf_op jit(solution)/shard_map/ppermute | solution.py:267
  55.1 1.2 copy-start
  58.6 12.5 %copy-start.1 = (bf16[1,32,16,1024]{3,2,0,1:T(8,128)(2,1)S(1)}, bf16[1,32,16,1024]{3,2,0,1:T(8,128)(2,1)}, u32[]{:S(2)}) copy-start(bf16[1,32,16,1024]{3,2,0,1:T(8,128)(2,1)} %all-gather.2.cloned.1.call-done) | copy-start | bytes 3145732
  58.6 21.6 %all-to-all-start = ((bf16[8,8,16,512]{3,2,1,0:T(8,128)(2,1)}), bf16[8,8,16,512]{3,2,1,0:T(8,128)(2,1)S(1)}, u32[]{:S(2)}, u32[]{:S(2)}) async-start(bf16[8,8,16,512]{3,2,1,0:T(8,128)(2,1)} %shard_map.96), calls=%async_computation | async-start | bytes 2097152 | tf_op jit(solution)/shard_map/all_to_all | solution.py:280
  65.7 5.5 %collective-permute-start.9 = (bf16[2,48,256]{2,1,0:T(8,128)(2,1)S(1)}, bf16[2,48,256]{2,1,0:T(8,128)(2,1)S(1)}, u32[]{:S(2)}, u32[]{:S(2)}) collective-permute-start(bf16[2,48,256]{2,1,0:T(8,128)(2,1)S(1)} %get-tuple-element.31), channel_id=1, source_target_pairs={{0,32},{32,64},{64,96},{96,128},{128,160},{160,192},{192,224},{224... | collective-permute-start | bytes 147464 | tf_op jit(solution)/shard_map/ppermute | solution.py:278
  65.7 5.5 %collective-permute-start.10 = (bf16[2,48,256]{2,1,0:T(8,128)(2,1)S(1)}, bf16[2,48,256]{2,1,0:T(8,128)(2,1)S(1)}, u32[]{:S(2)}, u32[]{:S(2)}) collective-permute-start(bf16[2,48,256]{2,1,0:T(8,128)(2,1)S(1)} %get-tuple-element.32), channel_id=1, source_target_pairs={{0,224},{32,0},{64,32},{96,64},{128,96},{160,128},{192,160},{224,1... | collective-permute-start | bytes 147464 | tf_op jit(solution)/shard_map/ppermute | solution.py:277
  71.1 1.4 %copy-start.2 = (bf16[1024,3,256]{2,0,1:T(8,128)(2,1)S(1)}, bf16[1024,3,256]{2,0,1:T(8,128)(2,1)}, u32[]{:S(2)}) copy-start(bf16[1024,3,256]{2,0,1:T(8,128)(2,1)} %param.11) | copy-start | bytes 4718596
  76.8 1.9 %collective-permute-start.11 = (bf16[2,128,1024]{2,1,0:T(8,128)(2,1)S(1)}, bf16[2,128,1024]{2,1,0:T(8,128)(2,1)S(1)}, u32[]{:S(2)}, u32[]{:S(2)}) collective-permute-start(bf16[2,128,1024]{2,1,0:T(8,128)(2,1)S(1)} %get-tuple-element.35), channel_id=1, source_target_pairs={{0,1},{1,0},{2,3},{3,2},{4,5},{5,4},{6,7},{7,6},{8,9},{9,8},{10,11... | collective-permute-start | bytes 1572872 | tf_op jit(solution)/shard_map/ppermute | solution.py:290
  80.2 24.0 %all-to-all-start.1 = ((bf16[8,8,16,512]{3,2,1,0:T(8,128)(2,1)}), bf16[8,8,16,512]{3,2,1,0:T(8,128)(2,1)S(1)}, u32[]{:S(2)}, u32[]{:S(2)}) async-start(bf16[8,8,16,512]{3,2,1,0:T(8,128)(2,1)} %get-tuple-element.40), calls=%async_computation.1 | async-start | bytes 2097152 | tf_op jit(solution)/shard_map/all_to_all | solution.py:296
  86.6 23.8 %collective-permute-start.12 = (bf16[128,1024]{1,0:T(8,128)(2,1)S(1)}, bf16[128,1024]{1,0:T(8,128)(2,1)S(1)}, u32[]{:S(2)}, u32[]{:S(2)}) collective-permute-start(bf16[128,1024]{1,0:T(8,128)(2,1)S(1)} %get-tuple-element.38), channel_id=1, source_target_pairs={{0,2},{2,0},{1,3},{3,1},{4,6},{6,4},{5,7},{7,5},{8,10},{10,8},{9,1... | collective-permute-start | bytes 786440 | tf_op jit(solution)/shard_map/ppermute | solution.py:294
  105.2 16.8 %all-to-all-start.2 = ((bf16[8,16,1024]{2,1,0:T(8,128)(2,1)}), bf16[8,16,1024]{2,1,0:T(8,128)(2,1)S(1)}, u32[]{:S(2)}, u32[]{:S(2)}) async-start(bf16[8,16,1024]{2,1,0:T(8,128)(2,1)} %shard_map.100), calls=%async_computation.2 | async-start | bytes 524288 | tf_op jit(solution)/shard_map/all_to_all | solution.py:300
  (4 other events, 3.8 us)
Sparse Core Ops, SparseCore 0:
  9.8 28.9 all-gather.1

commit v2 on v1

v2 whole, which is shorter than its diff:
```python
import jax
import jax.numpy as jnp
from jax import lax
from jax.experimental import pallas as pl
from jax.experimental.pallas import tpu as pltpu
from jax.sharding import Mesh
from jax.sharding import PartitionSpec as P

D = 1024
HD = 64
HEADS_HERE = 4
FEAT = HD * HEADS_HERE
TH = 32
TW = 16
TOKENS = TH * TW
DEPTH = 3
IMG_H = 256
IMG_W = 128
PAD_H = TH + 2 * DEPTH
CENTER = PAD_H * TW
EDGE = DEPTH * TW
SLOTS = 4
BAND = 40 * SLOTS
BLOCKS = 4
BLK = TOKENS // BLOCKS
BLK_ROWS = TH // BLOCKS
K_MID = (BLK_ROWS + 2 * DEPTH) * TW
K_BAND = 16 * SLOTS
K_ALL = K_MID + 2 * K_BAND
Z, YH, X, YL, CORE = 8, 2, 4, 2, 2
GRID = ("z", "yh", "x")
YX = ("yh", "x")
HEAD = ("yl", "core")
F32 = jnp.float32
BF16 = jnp.bfloat16
VMEM_LIMIT = 24 * 1024 * 1024


def dot(a, b, ca, cb):
    return lax.dot_general(a, b, (((ca,), (cb,)), ((), ())), preferred_element_type=F32)


def call(body, out_shape, scratch=(), n_in=0, hbm=(), hbm_out=(), flops=0):
    specs = [pl.BlockSpec(memory_space=pltpu.HBM if i in hbm else pltpu.VMEM) for i in range(n_in)]
    outs = [
        pl.BlockSpec(memory_space=pltpu.HBM if i in hbm_out else pltpu.VMEM)
        for i in range(len(out_shape))
    ]
    out_shape = [
        pltpu.HBM(o.shape, o.dtype) if i in hbm_out else o for i, o in enumerate(out_shape)
    ]
    run = pl.pallas_call(
        body,
        out_shape=out_shape,
        in_specs=specs,
        out_specs=outs,
        scratch_shapes=list(scratch),
        compiler_params=pltpu.CompilerParams(vmem_limit_bytes=VMEM_LIMIT),
        cost_estimate=pl.CostEstimate(flops=flops, bytes_accessed=0, transcendentals=0),
    )

    def on(*args):
        hold = pltpu.with_memory_space_constraint
        return run(*(hold(a, pltpu.HBM) if i in hbm else a for i, a in enumerate(args)))

    return on


def head_index():
    return lax.axis_index("yl") * CORE + lax.axis_index("core")


def shaped(shape, dtype=BF16):
    return jax.ShapeDtypeStruct(shape, dtype)


def pick(first_col, token_axis):
    shape = (CENTER, BAND) if token_axis == 0 else (BAND, CENTER)
    token = lax.broadcasted_iota(jnp.int32, shape, token_axis)
    slot = lax.broadcasted_iota(jnp.int32, shape, 1 - token_axis)
    lane = slot & (SLOTS - 1)
    wanted = (slot // SLOTS) * TW + first_col + lane
    return jnp.where((token == wanted) & (lane < DEPTH), 1.0, 0.0).astype(BF16)


def load_kernel(
    q, k, v, w_out, out_grad, hidden,
    q_out, kv, w_out_out, own_grad, own_hidden, to_above, to_below, sems,
):
    first, last = pl.ds(0, EDGE), pl.ds(TOKENS - EDGE, EDGE)
    pairs = [(k.at[first], to_above.at[0]), (v.at[first], to_above.at[1])]
    pairs += [(k.at[last], to_below.at[0]), (v.at[last], to_below.at[1])]
    pairs += [(out_grad, own_grad), (hidden, own_hidden)]
    pairs += [(k, kv.at[0]), (v, kv.at[1]), (q, q_out), (w_out, w_out_out)]
    copies = [pltpu.make_async_copy(a, b, sems.at[i]) for i, (a, b) in enumerate(pairs)]
    for copy in copies:
        copy.start()
    for copy in copies:
        copy.wait()


def bands_kernel(kv, above, below, mid, to_left, to_right):
    left = pick(0, 1)
    right = pick(TW - DEPTH, 1)
    for i in range(2):
        mid[i, :EDGE] = above[i]
        mid[i, EDGE : EDGE + TOKENS] = kv[i]
        mid[i, EDGE + TOKENS :] = below[i]
        to_left[i] = dot(left, mid[i], 1, 0).astype(BF16)
        to_right[i] = dot(right, mid[i], 1, 0).astype(BF16)


def stacked(x):
    lane = lax.broadcasted_iota(jnp.int32, x.shape, 1) // HD
    zero = jnp.zeros_like(x)
    return jnp.concatenate([jnp.where(lane == h, x, zero) for h in range(HEADS_HERE)], axis=0)


def unstacked(x):
    lane = lax.broadcasted_iota(jnp.int32, (BLK, FEAT), 1) // HD
    out = x[:BLK]
    for h in range(1, HEADS_HERE):
        out = jnp.where(lane == h, x[h * BLK : (h + 1) * BLK], out)
    return out


def attention_kernel(
    q, og0, og1, og2, og3, w_out, mid, from_left, from_right,
    attn_out, grad_q, grad_mid, band_left, band_right,
    ga, gl, gr,
):
    head = head_index()
    tile_row = lax.axis_index("z")
    tile_col = lax.axis_index("yh") * X + lax.axis_index("x")
    for i, piece in enumerate((og0, og1, og2, og3)):
        at = pl.multiple_of((head ^ i) * BLK, BLK)
        ga[pl.ds(at, BLK), :] = dot(piece[...], w_out[...], 1, 1).astype(BF16)
    grad_mid[...] = jnp.zeros_like(grad_mid)
    gl[...] = jnp.zeros_like(gl)
    gr[...] = jnp.zeros_like(gr)

    key = lax.broadcasted_iota(jnp.int32, (1, K_ALL), 1)
    in_mid = key < K_MID
    in_left = key < K_MID + K_BAND
    slot = key & (SLOTS - 1)
    key_row = jnp.where(
        in_mid,
        key // TW,
        jnp.where(in_left, (key - K_MID) // SLOTS, (key - K_MID - K_BAND) // SLOTS),
    )
    band_col = jnp.where(in_left, slot, TW + DEPTH + slot)
    key_col = jnp.where(in_mid, (key & (TW - 1)) + DEPTH, jnp.where(slot < DEPTH, band_col, 1000))
    col_image = tile_col * TW + key_col - DEPTH
    key_col = jnp.where((col_image >= 0) & (col_image < IMG_W), key_col, 1000)
    token = lax.broadcasted_iota(jnp.int32, (BLK, 1), 0)
    row_off = key_row - token // TW
    col_off = key_col - (token & (TW - 1))
    near = (row_off >= 0) & (row_off < 7) & (col_off >= 0) & (col_off < 7)
    row_image = tile_row * TH + key_row - DEPTH

    for b in range(BLOCKS):
        row_here = row_image + b * BLK_ROWS
        valid = near & (row_here >= 0) & (row_here < IMG_H)
        bias = jnp.where(valid, 0.0, -jnp.inf).astype(F32)
        rows = slice(b * BLK, (b + 1) * BLK)
        m_rows = slice(b * BLK, b * BLK + K_MID)
        b_rows = slice(b * BLK_ROWS * SLOTS, b * BLK_ROWS * SLOTS + K_BAND)
        kk = jnp.concatenate([mid[0, m_rows], from_left[0, b_rows], from_right[0, b_rows]], axis=0)
        vv = jnp.concatenate([mid[1, m_rows], from_left[1, b_rows], from_right[1, b_rows]], axis=0)
        qs = stacked(q[rows, :] * jnp.asarray(HD**-0.5, BF16))
        gs = stacked(ga[rows, :])
        s = dot(qs, kk, 1, 1).reshape(HEADS_HERE, BLK, K_ALL) + bias[None]
        s = s.reshape(HEADS_HERE * BLK, K_ALL)
        e = jnp.exp(s - jnp.max(s, axis=1, keepdims=True))
        p = e * (1.0 / jnp.sum(e, axis=1, keepdims=True))
        p16 = p.astype(BF16)
        attn = dot(p16, vv, 1, 0).astype(BF16)
        attn_out[rows, :] = unstacked(attn)
        delta = jnp.sum(gs.astype(F32) * attn.astype(F32), axis=1, keepdims=True)
        ds = (p * (dot(gs, vv, 1, 1) - delta)).astype(BF16)
        grad_q[rows, :] = unstacked(dot(ds, kk, 1, 0) * (HD**-0.5)).astype(BF16)
        for i, g in enumerate((dot(ds, qs, 0, 0), dot(p16, gs, 0, 0))):
            grad_mid[i, m_rows] += g[:K_MID]
            gl[i, b_rows] += g[K_MID : K_MID + K_BAND]
            gr[i, b_rows] += g[K_MID + K_BAND :]
    band_left[...] = gl[...].astype(BF16)
    band_right[...] = gr[...].astype(BF16)


def put_term(out, term):
    term = term.astype(BF16)
    for yx in range(YH * X):
        for z in range(Z):
            at = (z * YH * X + yx) * 16
            out[yx, z] = term[at : at + 16]


def first_terms_kernel(
    grad_q, attn, g0, g1, g2, g3, h0, h1, h2, h3, out, hidden_out, hidden, og, terms, sems
):
    head = head_index()
    for i, (g, h) in enumerate(((g0, h0), (g1, h1), (g2, h2), (g3, h3))):
        at = pl.ds(pl.multiple_of((head ^ i) * BLK, BLK), BLK)
        og[at, :] = g[...]
        hidden[at, :] = h[...]
    copies = [pltpu.make_async_copy(hidden, hidden_out, sems.at[0])]
    copies[0].start()
    for i, (left, right) in enumerate(((hidden, grad_q), (og, attn))):
        put_term(terms.at[i], dot(left[...], right[...], 0, 0))
        copies.append(pltpu.make_async_copy(terms.at[i], out.at[i], sems.at[1 + i]))
        copies[-1].start()
    for copy in copies:
        copy.wait()


def columns_kernel(grad_mid, from_left, from_right, inner, to_above, to_below):
    left = pick(0, 0)
    right = pick(TW - DEPTH, 0)
    for i in range(2):
        g = grad_mid[i] + dot(left, from_left[i], 1, 0) + dot(right, from_right[i], 1, 0)
        to_above[i] = g[:EDGE].astype(BF16)
        inner[i] = g[EDGE : EDGE + TOKENS]
        to_below[i] = g[EDGE + TOKENS :].astype(BF16)


def second_terms_kernel(
    inner, from_above, from_below, first, hidden_in, terms, grads, hidden, sems
):
    copies = [pltpu.make_async_copy(hidden_in, hidden, sems.at[0])]
    for i in range(2):
        copies.append(pltpu.make_async_copy(first.at[i], terms.at[:, i], sems.at[1 + i]))
    for copy in copies:
        copy.start()
    for i in range(2):
        grads[i, :EDGE] = (inner[i, :EDGE] + from_above[i].astype(F32)).astype(BF16)
        grads[i, EDGE : TOKENS - EDGE] = inner[i, EDGE : TOKENS - EDGE].astype(BF16)
        last = inner[i, TOKENS - EDGE :] + from_below[i].astype(F32)
        grads[i, TOKENS - EDGE :] = last.astype(BF16)
    copies[0].wait()
    for i in range(2):
        put_term(terms.at[:, 2 + i], dot(hidden[...], grads[i], 0, 0))
    copies[1].wait()
    copies[2].wait()


def hidden_grad_kernel(grad_q, grads, w_qkv, keep, send):
    core = lax.axis_index("core")
    for yl in range(YL):
        for out, c in ((send, 1 - core), (keep, core)):
            at = pl.ds(pl.multiple_of((yl * CORE + c) * BLK, BLK), BLK)
            total = dot(grad_q[at, :], w_qkv[0], 1, 1)
            for j in range(2):
                total += dot(grads[j, at, :], w_qkv[1 + j], 1, 1)
            out[yl] = total.astype(BF16)


def halve_kernel(keep, got, stay, send):
    yl = lax.axis_index("yl")
    stay[...] = keep[yl].astype(F32) + got[yl].astype(F32)
    send[...] = (keep[1 - yl].astype(F32) + got[1 - yl].astype(F32)).astype(BF16)


def summed(terms):
    total = terms[0].astype(F32)
    for i in range(1, 8):
        total += terms[i].astype(F32)
    return total


def sum_kernel(terms, out):
    for j in range(4):
        total = terms[0, j].astype(F32)
        for i in range(1, YH * X):
            total += terms[i, j].astype(F32)
        out[:, :, j * FEAT : (j + 1) * FEAT] = total.astype(BF16)


def last_kernel(parts, grad_wqkv, grad_wout):
    total = summed(parts)
    grad_wqkv[0] = total[:, :FEAT]
    grad_wout[...] = total[:, FEAT : 2 * FEAT]
    grad_wqkv[1] = total[:, 2 * FEAT : 3 * FEAT]
    grad_wqkv[2] = total[:, 3 * FEAT :]


def ring(size, step):
    return [(i, (i + step) % size) for i in range(size)]


SWAP = [(0, 1), (1, 0)]


def per_device(hidden_in, queries, keys, values, w_qkv, w_out, out_grad):
    q = queries.reshape(TOKENS, FEAT)
    k = keys.reshape(TOKENS, FEAT)
    v = values.reshape(TOKENS, FEAT)
    w3 = w_qkv.transpose(1, 0, 2)

    flat = shaped((TOKENS, FEAT))
    edge = shaped((2, EDGE, FEAT))
    band = shaped((2, BAND, FEAT))
    mids = shaped((2, CENTER, FEAT))
    own = shaped((BLK, D))
    q, kv, w_out, g0, h0, to_above, to_below = call(
        load_kernel,
        (flat, shaped((2, TOKENS, FEAT)), shaped((FEAT, D)), own, own, edge, edge),
        scratch=[pltpu.SemaphoreType.DMA((10,))],
        n_in=6,
        hbm=range(6),
    )(q, k, v, w_out, out_grad.reshape(BLK, D), hidden_in.reshape(BLK, D))

    below = lax.ppermute(to_above, "z", ring(Z, -1))
    above = lax.ppermute(to_below, "z", ring(Z, 1))
    g2 = lax.ppermute(g0, "yl", SWAP)
    g1 = lax.ppermute(g0, "core", SWAP)
    h2 = lax.ppermute(h0, "yl", SWAP)
    h1 = lax.ppermute(h0, "core", SWAP)

    mid, to_left, to_right = call(bands_kernel, (mids, band, band), n_in=3)(kv, above, below)
    from_right = lax.ppermute(to_left, YX, ring(YH * X, -1))
    from_left = lax.ppermute(to_right, YX, ring(YH * X, 1))
    g3 = lax.ppermute(g2, "core", SWAP)
    h2, _ = lax.optimization_barrier((h2, from_left))
    h3 = lax.ppermute(h2, "core", SWAP)

    attn, grad_q, grad_mid, band_left, band_right = call(
        attention_kernel,
        (flat, flat, shaped((2, CENTER, FEAT), F32), band, band),
        scratch=[
            pltpu.VMEM((TOKENS, FEAT), BF16),
            pltpu.VMEM((2, BAND, FEAT), F32),
            pltpu.VMEM((2, BAND, FEAT), F32),
        ],
        n_in=9,
    )(q, g0, g1, g2, g3, w_out, mid, from_left, from_right)

    got_right = lax.ppermute(band_left, YX, ring(YH * X, -1))
    got_left = lax.ppermute(band_right, YX, ring(YH * X, 1))
    inner, to_above, to_below = call(
        columns_kernel, (shaped((2, TOKENS, FEAT), F32), edge, edge), n_in=3
    )(grad_mid, got_left, got_right)
    got_below = lax.ppermute(to_above, "z", ring(Z, -1))
    got_above = lax.ppermute(to_below, "z", ring(Z, 1))

    first, hidden = call(
        first_terms_kernel,
        (shaped((2, YH * X, Z, 16, FEAT)), shaped((TOKENS, D))),
        scratch=[
            pltpu.VMEM((TOKENS, D), BF16),
            pltpu.VMEM((TOKENS, D), BF16),
            pltpu.VMEM((2, YH * X, Z, 16, FEAT), BF16),
            pltpu.SemaphoreType.DMA((3,)),
        ],
        n_in=10,
        hbm_out=(0, 1),
        flops=10_000_000_000,
    )(grad_q, attn, g0, g1, g2, g3, h0, h1, h2, h3)
    terms, grads = call(
        second_terms_kernel,
        (shaped((YH * X, 4, Z, 16, FEAT)), shaped((2, TOKENS, FEAT))),
        scratch=[pltpu.VMEM((TOKENS, D), BF16), pltpu.SemaphoreType.DMA((3,))],
        n_in=5,
        hbm=(3, 4),
    )(inner, got_above, got_below, first, hidden)
    terms = lax.all_to_all(terms, YX, 0, 0, tiled=True)

    half = shaped((YL, BLK, D))
    keep, send = call(hidden_grad_kernel, (half, half), n_in=3)(grad_q, grads, w3)
    got = lax.ppermute(send, "core", SWAP)
    stay, send = call(halve_kernel, (shaped((BLK, D), F32), shaped((BLK, D))), n_in=2)(keep, got)
    got = lax.ppermute(send, "yl", SWAP)
    grad_hidden = (stay + got.astype(F32)).astype(BF16).reshape(1, 8, TW, D)

    (parts,) = call(sum_kernel, (shaped((Z, 16, 4 * FEAT)),), n_in=1)(terms)
    parts = lax.all_to_all(parts, "z", 0, 0, tiled=True)
    grad_wqkv, grad_wout = call(
        last_kernel, (shaped((3, 16, FEAT), F32), shaped((16, FEAT), F32)), n_in=1
    )(parts)
    return grad_hidden, grad_wqkv.transpose(1, 0, 2), grad_wout.T


def solution(mesh):
    fine = Mesh(mesh.devices.reshape(Z, YH, X, YL, CORE), GRID + HEAD)
    return jax.shard_map(
        per_device,
        mesh=fine,
        in_specs=(
            P(GRID, HEAD, None, None),
            P(GRID, None, None, HEAD),
            P(GRID, None, None, HEAD),
            P(GRID, None, None, HEAD),
            P(None, None, HEAD),
            P(HEAD, None),
            P(GRID, HEAD, None, None),
        ),
        out_specs=(P(GRID, HEAD, None, None), P(GRID, None, HEAD), P(HEAD, GRID)),
        check_vma=False,
    )
```

time: 131 us -> 103 us (0.79)
  between operations: 14.2 us -> 0.74 us
  local copies, waits for them, and re-layouts: 10.6 us -> 2.75 us
  waiting for transfers between devices: 46.3 us -> 42.8 us
  starting transfers between devices: 42.7 us -> 40 us
    unnamed x22 -> x4, local copies, waits for them, and re-layouts: 8.34 us -> 2.75 us
    all_to_all x3 -> x2, starting transfers between devices: 18.6 us -> 13.2 us  [the longest x1 6.63 us: per_device(): terms = lax.all_to_all(terms, YX, 0, 0, tiled=True)]
    ppermute x5 -> x8, waiting for transfers between devices: 6.04 us -> 2.07 us  [the longest x1 1.49 us: per_device(): g2 = lax.ppermute(g0, 'yl', SWAP)]
    all_to_all x3 -> x2, waiting for transfers between devices: 28.7 us -> 30.6 us  [the longest x1 20.8 us: per_device(): terms = lax.all_to_all(terms, YX, 0, 0, tiled=True)]
    ppermute x1, waiting for transfers between devices: 1.98 us -> 0.08 us  [per_device(): got_above = lax.ppermute(to_below, 'z', ring(Z, 1))]
    ppermute x1, starting transfers between devices: 0.01 us -> 1.81 us  [per_device(): got_above = lax.ppermute(to_below, 'z', ring(Z, 1))]
    slice x2 -> x0, local copies, waits for them, and re-layouts: 1.52 us -> none  [per_device(): below = lax.ppermute(jnp.stack([k[:EDGE], v[:EDGE]]), 'z', ring(Z, -1))]
    pallas_call x7 -> x10, Pallas kernels: 15 us -> 15.6 us  [on(): run(*(hold(a, pltpu.HBM) if i in hbm else a for i, a in enumerate(args)))]
  transfers between devices with their start and end apart: 17 -> 18, of which waited for: 9 -> 8; matrix products, arithmetic and copies ran while one was open for 2% -> 1% of each run, Pallas kernels for 10% -> 11%
where the time goes in v2:
time: 103 us
  waiting for transfers between devices  42.8 us (42%)
  starting transfers between devices  40 us (39%)
  Pallas kernels  15.6 us (15%)
  local copies, waits for them, and re-layouts  2.75 us (3%)
    all_to_all x1, waiting for transfers between devices, per_device(): terms = lax.all_to_all(terms, YX, 0, 0, tiled=True)  20.8 us
    pallas_call x10, Pallas kernels, on(): run(*(hold(a, pltpu.HBM) if i in hbm else a for i, a in enumerate(args)))  15.6 us
    all_to_all x1, waiting for transfers between devices, per_device(): parts = lax.all_to_all(parts, 'z', 0, 0, tiled=True)  9.81 us
    all_to_all x1, starting transfers between devices, per_device(): terms = lax.all_to_all(terms, YX, 0, 0, tiled=True)  6.63 us
    all_to_all x1, starting transfers between devices, per_device(): parts = lax.all_to_all(parts, 'z', 0, 0, tiled=True)  6.56 us
    ppermute x1, starting transfers between devices, per_device(): got_right = lax.ppermute(band_left, YX, ring(YH * X, -1))  5.63 us
    ppermute x1, starting transfers between devices, per_device(): from_right = lax.ppermute(to_left, YX, ring(YH * X, -1))  4.15 us
    ppermute x1, waiting for transfers between devices, per_device(): got_left = lax.ppermute(band_right, YX, ring(YH * X, 1))  4.1 us
  transfers between devices with their start and end apart: 18, of which 8 were waited for; matrix products, arithmetic and copies ran while one was open for 1% of the time, Pallas kernels for 11%

profile of v2, /device:TPU:8, one launch (start us, length us, event | category | flops | bytes accessed | tf_op | source)
XLA Modules:
  0.0 102.6 jit_solution(16516504361072400956)
XLA Ops:
  0.6 1.6 %shard_map.94 = (bf16[512,256]{1,0:T(8,128)(2,1)S(1)}, bf16[2,512,256]{2,1,0:T(8,128)(2,1)S(1)}, bf16[256,1024]{1,0:T(8,128)(2,1)S(1)}, bf16[128,1024]{1,0:T(8,1...) custom-call(bf16[512,256]{1,0:T(8,128)(2,1)} %bitcast.10, ...), custom_call_target="tpu_custom_call" | custom-call | tf_op jit(solution)/shard_map/pallas_call | solution.py:64
  2.2 2.3 %collective-permute-start.1 = (bf16[128,1024]{1,0:T(8,128)(2,1)S(1)}, bf16[128,1024]{1,0:T(8,128)(2,1)S(1)}, u32[]{:S(2)}, u32[]{:S(2)}) collective-permute-start(bf16[128,1024]{1,0:T(8,128)(2,1)S(1)} %get-tuple-element.33.og0.g0), channel_id=1, source_target_pairs={{0,2},{2,0},{1,3},{3,1},{4,6},{6,4},{5,7},{7,5},{8,10},{10,8},{9,1... | collective-permute-start | bytes 786440 | tf_op jit(solution)/shard_map/ppermute | solution.py:314
  4.6 1.7 %collective-permute-start.3 = (bf16[2,48,256]{2,1,0:T(8,128)(2,1)S(1)}, bf16[2,48,256]{2,1,0:T(8,128)(2,1)S(1)}, u32[]{:S(2)}, u32[]{:S(2)}) collective-permute-start(bf16[2,48,256]{2,1,0:T(8,128)(2,1)S(1)} %get-tuple-element.36), channel_id=1, source_target_pairs={{0,32},{32,64},{64,96},{96,128},{128,160},{160,192},{192,224},{224... | collective-permute-start | bytes 147464 | tf_op jit(solution)/shard_map/ppermute | solution.py:313
  6.3 3.9 %collective-permute-start.4 = (bf16[2,48,256]{2,1,0:T(8,128)(2,1)S(1)}, bf16[2,48,256]{2,1,0:T(8,128)(2,1)S(1)}, u32[]{:S(2)}, u32[]{:S(2)}) collective-permute-start(bf16[2,48,256]{2,1,0:T(8,128)(2,1)S(1)} %get-tuple-element.37), channel_id=1, source_target_pairs={{0,224},{32,0},{64,32},{96,64},{128,96},{160,128},{192,160},{224,1... | collective-permute-start | bytes 147464 | tf_op jit(solution)/shard_map/ppermute | solution.py:312
  10.2 1.5 %collective-permute-done.1.og2.g2 = bf16[128,1024]{1,0:T(8,128)(2,1)S(1)} collective-permute-done((bf16[128,1024]{1,0:T(8,128)(2,1)S(1)}, bf16[128,1024]{1,0:T(8,128)(2,1)S(1)}, u32[]{:S(2)}, u32[]{:S(2)}) %collective-permute-start.1) | collective-permute-done | bytes 262176 | tf_op jit(solution)/shard_map/ppermute | solution.py:314
  12.7 1.6 %collective-permute-start.5 = (bf16[2,160,256]{2,1,0:T(8,128)(2,1)S(1)}, bf16[2,160,256]{2,1,0:T(8,128)(2,1)S(1)}, u32[]{:S(2)}, u32[]{:S(2)}) collective-permute-start(bf16[2,160,256]{2,1,0:T(8,128)(2,1)S(1)} %get-tuple-element.39), channel_id=1, source_target_pairs={{0,4},{4,8},{8,12},{12,16},{16,20},{20,24},{24,28},{28,0},{1,5},{5... | collective-permute-start | bytes 491528 | tf_op jit(solution)/shard_map/ppermute | solution.py:321
  14.3 4.2 %collective-permute-start.6 = (bf16[2,160,256]{2,1,0:T(8,128)(2,1)S(1)}, bf16[2,160,256]{2,1,0:T(8,128)(2,1)S(1)}, u32[]{:S(2)}, u32[]{:S(2)}) collective-permute-start(bf16[2,160,256]{2,1,0:T(8,128)(2,1)S(1)} %get-tuple-element.40), channel_id=1, source_target_pairs={{0,28},{4,0},{8,4},{12,8},{16,12},{20,16},{24,20},{28,24},{1,29},{... | collective-permute-start | bytes 491528 | tf_op jit(solution)/shard_map/ppermute | solution.py:320
  18.4 4.0 %collective-permute-done.5.from_left = bf16[2,160,256]{2,1,0:T(8,128)(2,1)S(1)} collective-permute-done((bf16[2,160,256]{2,1,0:T(8,128)(2,1)S(1)}, bf16[2,160,256]{2,1,0:T(8,128)(2,1)S(1)}, u32[]{:S(2)}, u32[]{:S(2)}) %collective-permute-start.5) | collective-permute-done | bytes 163872 | tf_op jit(solution)/shard_map/ppermute | solution.py:321
  23.0 5.3 %shard_map.96 = (bf16[512,256]{1,0:T(8,128)(2,1)S(1)}, bf16[512,256]{1,0:T(8,128)(2,1)S(1)}, f32[2,608,256]{2,1,0:T(8,128)S(1)}, bf16[2,160,256]{2,1,0:T(8,128)(2,1)S(1)}, bf16[2,160,256]{2,1,0:T(8,128)(2,1)S(1)}) custom-call(bf16[512,256]{1,0:T(8,128)(2,1)S(1)} %get-tuple-element.32.q, bf16[128,1024]{1,0:T(8,128)(2,1)S(1)} %get-tuple-element.33.og0.g0, ...), custom_call_target="tpu_custom_call" | custom-call | tf_op jit(solution)/shard_map/pallas_call | solution.py:64
  28.6 5.6 %collective-permute-start.8 = (bf16[2,160,256]{2,1,0:T(8,128)(2,1)S(1)}, bf16[2,160,256]{2,1,0:T(8,128)(2,1)S(1)}, u32[]{:S(2)}, u32[]{:S(2)}) collective-permute-start(bf16[2,160,256]{2,1,0:T(8,128)(2,1)S(1)} %get-tuple-element.44), channel_id=1, source_target_pairs={{0,28},{4,0},{8,4},{12,8},{16,12},{20,16},{24,20},{28,24},{1,29},{... | collective-permute-start | bytes 491528 | tf_op jit(solution)/shard_map/ppermute | solution.py:337
  34.2 4.1 %collective-permute-done.7.from_left = bf16[2,160,256]{2,1,0:T(8,128)(2,1)S(1)} collective-permute-done((bf16[2,160,256]{2,1,0:T(8,128)(2,1)S(1)}, bf16[2,160,256]{2,1,0:T(8,128)(2,1)S(1)}, u32[]{:S(2)}, u32[]{:S(2)}) %collective-permute-start.7) | collective-permute-done | bytes 163872 | tf_op jit(solution)/shard_map/ppermute | solution.py:338
  38.8 1.8 %collective-permute-start.9 = (bf16[2,48,256]{2,1,0:T(8,128)(2,1)S(1)}, bf16[2,48,256]{2,1,0:T(8,128)(2,1)S(1)}, u32[]{:S(2)}, u32[]{:S(2)}) collective-permute-start(bf16[2,48,256]{2,1,0:T(8,128)(2,1)S(1)} %get-tuple-element.46), channel_id=1, source_target_pairs={{0,32},{32,64},{64,96},{96,128},{128,160},{160,192},{192,224},{224... | collective-permute-start | bytes 147464 | tf_op jit(solution)/shard_map/ppermute | solution.py:343
  40.6 4.0 %collective-permute-start.10 = (bf16[2,48,256]{2,1,0:T(8,128)(2,1)S(1)}, bf16[2,48,256]{2,1,0:T(8,128)(2,1)S(1)}, u32[]{:S(2)}, u32[]{:S(2)}) collective-permute-start(bf16[2,48,256]{2,1,0:T(8,128)(2,1)S(1)} %get-tuple-element.47), channel_id=1, source_target_pairs={{0,224},{32,0},{64,32},{96,64},{128,96},{160,128},{192,160},{224,1... | collective-permute-start | bytes 147464 | tf_op jit(solution)/shard_map/ppermute | solution.py:342
  44.7 1.9 %shard_map.98 = (bf16[2,8,8,16,256]{4,3,2,1,0:T(8,128)(2,1)}, bf16[512,1024]{1,0:T(8,128)(2,1)}) custom-call(bf16[512,256]{1,0:T(8,128)(2,1)S(1)} %get-tuple-element.41.grad_q, bf16[512,256]{1,0:T(8,128)(2,1)S(1)} %get-tuple-element.48.attn, bf16[128,1024]{1,0:T(8,128)(2,1)S(1)} %get-tuple-element.33.og0.g0, ...), custom_call_target="tpu_custom_call" | custom-call | flops 10000000000 | tf_op jit(solution)/shard_map/pallas_call | solution.py:64
  46.6 2.0 %shard_map.99 = (bf16[8,4,8,16,256]{4,3,2,1,0:T(8,128)(2,1)S(1)}, bf16[2,512,256]{2,1,0:T(8,128)(2,1)S(1)}) custom-call(f32[2,512,256]{2,1,0:T(8,128)S(1)} %get-tuple-element.45.inner, bf16[2,48,256]{2,1,0:T(8,128)(2,1)S(1)} %collective-permute-done.9.from_above, bf16[2,48,256]{2,1,0:T(8,128)(2,1)S(1)} %collective-permute-done.10.from_below, ...), custom_call_target="tpu_custom_call" | custom-call | tf_op jit(solution)/shard_map/pallas_call | solution.py:64
  48.7 1.3 %copy-done = bf16[8,4,8,16,256]{4,3,2,1,0:T(8,128)(2,1)} copy-done((bf16[8,4,8,16,256]{4,3,2,1,0:T(8,128)(2,1)}, bf16[8,4,8,16,256]{4,3,2,1,0:T(8,128)(2,1)S(1)}, u32[]{:S(2)}) %copy-start) | copy-done | bytes 2097176
  50.0 6.6 %all-to-all-start = ((bf16[8,4,8,16,256]{4,3,2,1,0:T(8,128)(2,1)}), bf16[8,4,8,16,256]{4,3,2,1,0:T(8,128)(2,1)S(1)}, u32[]{:S(2)}, u32[]{:S(2)}) async-start(bf16[8,4,8,16,256]{4,3,2,1,0:T(8,128)(2,1)} %copy-done), calls=%async_computation | async-start | bytes 4194304 | tf_op jit(solution)/shard_map/all_to_all | solution.py:365
  56.6 1.4 %copy-done.1 = bf16[1024,3,256]{2,0,1:T(8,128)(2,1)S(1)} copy-done((bf16[1024,3,256]{2,0,1:T(8,128)(2,1)S(1)}, bf16[1024,3,256]{2,0,1:T(8,128)(2,1)}, u32[]{:S(2)}) %copy-start.1) | copy-done | bytes 1572888
  58.1 2.1 %shard_map.100 = (bf16[2,128,1024]{2,1,0:T(8,128)(2,1)S(1)}, bf16[2,128,1024]{2,1,0:T(8,128)(2,1)S(1)}) custom-call(bf16[512,256]{1,0:T(8,128)(2,1)S(1)} %get-tuple-element.41.grad_q, bf16[2,512,256]{2,1,0:T(8,128)(2,1)S(1)} %get-tuple-element.53.grads, bf16[3,1024,256]{2,1,0:T(8,128)(2,1)S(1)} %bitcast.9), custom_call_target="tpu_custom_call" | custom-call | tf_op jit(solution)/shard_map/pallas_call | solution.py:64
  60.3 1.9 %collective-permute-done.14.got = bf16[2,128,1024]{2,1,0:T(8,128)(2,1)S(1)} collective-permute-done((bf16[2,128,1024]{2,1,0:T(8,128)(2,1)S(1)}, bf16[2,128,1024]{2,1,0:T(8,128)(2,1)S(1)}, u32[]{:S(2)}, u32[]{:S(2)}) %collective-permute-start.14) | collective-permute-done | bytes 524320 | tf_op jit(solution)/shard_map/ppermute | solution.py:369
  63.1 20.8 %all-to-all-done.terms = bf16[8,4,8,16,256]{4,3,2,1,0:T(8,128)(2,1)S(1)} async-done(((bf16[8,4,8,16,256]{4,3,2,1,0:T(8,128)(2,1)}), bf16[8,4,8,16,256]{4,3,2,1,0:T(8,128)(2,1)S(1)}, u32[]{:S(2)}, u32[]{:S(2)}) %all-to-all-start) | async-done | bytes 2097184 | tf_op jit(solution)/shard_map/all_to_all | solution.py:365
  83.9 1.0 shard_map.102
  84.8 6.6 %all-to-all-start.1 = ((bf16[8,16,1024]{2,1,0:T(8,128)(2,1)}), bf16[8,16,1024]{2,1,0:T(8,128)(2,1)S(1)}, u32[]{:S(2)}, u32[]{:S(2)}) async-start(bf16[8,16,1024]{2,1,0:T(8,128)(2,1)} %shard_map.102), calls=%async_computation.1 | async-start | bytes 524288 | tf_op jit(solution)/shard_map/all_to_all | solution.py:375
  92.2 9.8 %all-to-all-done.1.parts = bf16[8,16,1024]{2,1,0:T(8,128)(2,1)S(1)} async-done(((bf16[8,16,1024]{2,1,0:T(8,128)(2,1)}), bf16[8,16,1024]{2,1,0:T(8,128)(2,1)S(1)}, u32[]{:S(2)}, u32[]{:S(2)}) %all-to-all-start.1) | async-done | bytes 262176 | tf_op jit(solution)/shard_map/all_to_all | solution.py:375
  (27 shorter events, 4.9 us)
Async XLA Ops:
  2.2 9.5 %collective-permute-start.1 = (bf16[128,1024]{1,0:T(8,128)(2,1)S(1)}, bf16[128,1024]{1,0:T(8,128)(2,1)S(1)}, u32[]{:S(2)}, u32[]{:S(2)}) collective-permute-start(bf16[128,1024]{1,0:T(8,128)(2,1)S(1)} %get-tuple-element.33.og0.g0), channel_id=1, source_target_pairs={{0,2},{2,0},{1,3},{3,1},{4,6},{6,4},{5,7},{7,5},{8,10},{10,8},{9,1... | collective-permute-start | bytes 786440 | tf_op jit(solution)/shard_map/ppermute | solution.py:314
  4.5 18.0 %collective-permute-start.12 = (bf16[128,1024]{1,0:T(8,128)(2,1)S(1)}, bf16[128,1024]{1,0:T(8,128)(2,1)S(1)}, u32[]{:S(2)}, u32[]{:S(2)}) collective-permute-start(bf16[128,1024]{1,0:T(8,128)(2,1)S(1)} %get-tuple-element.49.h0), channel_id=1, source_target_pairs={{0,2},{2,0},{1,3},{3,1},{4,6},{6,4},{5,7},{7,5},{8,10},{10,8},{9,1... | collective-permute-start | bytes 786440 | tf_op jit(solution)/shard_map/ppermute | solution.py:316
  4.6 7.7 %collective-permute-start.3 = (bf16[2,48,256]{2,1,0:T(8,128)(2,1)S(1)}, bf16[2,48,256]{2,1,0:T(8,128)(2,1)S(1)}, u32[]{:S(2)}, u32[]{:S(2)}) collective-permute-start(bf16[2,48,256]{2,1,0:T(8,128)(2,1)S(1)} %get-tuple-element.36), channel_id=1, source_target_pairs={{0,32},{32,64},{64,96},{96,128},{128,160},{160,192},{192,224},{224... | collective-permute-start | bytes 147464 | tf_op jit(solution)/shard_map/ppermute | solution.py:313
  6.3 6.0 %collective-permute-start.4 = (bf16[2,48,256]{2,1,0:T(8,128)(2,1)S(1)}, bf16[2,48,256]{2,1,0:T(8,128)(2,1)S(1)}, u32[]{:S(2)}, u32[]{:S(2)}) collective-permute-start(bf16[2,48,256]{2,1,0:T(8,128)(2,1)S(1)} %get-tuple-element.37), channel_id=1, source_target_pairs={{0,224},{32,0},{64,32},{96,64},{128,96},{160,128},{192,160},{224,1... | collective-permute-start | bytes 147464 | tf_op jit(solution)/shard_map/ppermute | solution.py:312
  10.2 12.8 %collective-permute-start = (bf16[128,1024]{1,0:T(8,128)(2,1)S(1)}, bf16[128,1024]{1,0:T(8,128)(2,1)S(1)}, u32[]{:S(2)}, u32[]{:S(2)}) collective-permute-start(bf16[128,1024]{1,0:T(8,128)(2,1)S(1)} %get-tuple-element.33.og0.g0), channel_id=1, source_target_pairs={{0,1},{1,0},{2,3},{3,2},{4,5},{5,4},{6,7},{7,6},{8,9},{9,8},{10,11... | collective-permute-start | bytes 786440 | tf_op jit(solution)/shard_map/ppermute | solution.py:315
  11.7 11.3 %collective-permute-start.2 = (bf16[128,1024]{1,0:T(8,128)(2,1)S(1)}, bf16[128,1024]{1,0:T(8,128)(2,1)S(1)}, u32[]{:S(2)}, u32[]{:S(2)}) collective-permute-start(bf16[128,1024]{1,0:T(8,128)(2,1)S(1)} %collective-permute-done.1.og2.g2), channel_id=1, source_target_pairs={{0,1},{1,0},{2,3},{3,2},{4,5},{5,4},{6,7},{7,6},{8,9},{9,8},{10,11... | collective-permute-start | bytes 786440 | tf_op jit(solution)/shard_map/ppermute | solution.py:322
  12.7 9.7 %collective-permute-start.5 = (bf16[2,160,256]{2,1,0:T(8,128)(2,1)S(1)}, bf16[2,160,256]{2,1,0:T(8,128)(2,1)S(1)}, u32[]{:S(2)}, u32[]{:S(2)}) collective-permute-start(bf16[2,160,256]{2,1,0:T(8,128)(2,1)S(1)} %get-tuple-element.39), channel_id=1, source_target_pairs={{0,4},{4,8},{8,12},{12,16},{16,20},{20,24},{24,28},{28,0},{1,5},{5... | collective-permute-start | bytes 491528 | tf_op jit(solution)/shard_map/ppermute | solution.py:321
  14.3 8.7 %collective-permute-start.6 = (bf16[2,160,256]{2,1,0:T(8,128)(2,1)S(1)}, bf16[2,160,256]{2,1,0:T(8,128)(2,1)S(1)}, u32[]{:S(2)}, u32[]{:S(2)}) collective-permute-start(bf16[2,160,256]{2,1,0:T(8,128)(2,1)S(1)} %get-tuple-element.40), channel_id=1, source_target_pairs={{0,28},{4,0},{8,4},{12,8},{16,12},{20,16},{24,20},{28,24},{1,29},{... | collective-permute-start | bytes 491528 | tf_op jit(solution)/shard_map/ppermute | solution.py:320
  22.5 22.2 %collective-permute-start.11 = (bf16[128,1024]{1,0:T(8,128)(2,1)S(1)}, bf16[128,1024]{1,0:T(8,128)(2,1)S(1)}, u32[]{:S(2)}, u32[]{:S(2)}) collective-permute-start(bf16[128,1024]{1,0:T(8,128)(2,1)S(1)} %get-tuple-element.49.h0), channel_id=1, source_target_pairs={{0,1},{1,0},{2,3},{3,2},{4,5},{5,4},{6,7},{7,6},{8,9},{9,8},{10,11... | collective-permute-start | bytes 786440 | tf_op jit(solution)/shard_map/ppermute | solution.py:317
  22.5 22.2 %collective-permute-start.13 = (bf16[128,1024]{1,0:T(8,128)(2,1)S(1)}, bf16[128,1024]{1,0:T(8,128)(2,1)S(1)}, u32[]{:S(2)}, u32[]{:S(2)}) collective-permute-start(bf16[128,1024]{1,0:T(8,128)(2,1)S(1)} %collective-permute-done.12.h2), channel_id=1, source_target_pairs={{0,1},{1,0},{2,3},{3,2},{4,5},{5,4},{6,7},{7,6},{8,9},{9,8},{10,11... | collective-permute-start | bytes 786440 | tf_op jit(solution)/shard_map/ppermute | solution.py:324
  28.3 10.0 %collective-permute-start.7 = (bf16[2,160,256]{2,1,0:T(8,128)(2,1)S(1)}, bf16[2,160,256]{2,1,0:T(8,128)(2,1)S(1)}, u32[]{:S(2)}, u32[]{:S(2)}) collective-permute-start(bf16[2,160,256]{2,1,0:T(8,128)(2,1)S(1)} %get-tuple-element.43), channel_id=1, source_target_pairs={{0,4},{4,8},{8,12},{12,16},{16,20},{20,24},{24,28},{28,0},{1,5},{5... | collective-permute-start | bytes 491528 | tf_op jit(solution)/shard_map/ppermute | solution.py:338
  28.6 9.7 %collective-permute-start.8 = (bf16[2,160,256]{2,1,0:T(8,128)(2,1)S(1)}, bf16[2,160,256]{2,1,0:T(8,128)(2,1)S(1)}, u32[]{:S(2)}, u32[]{:S(2)}) collective-permute-start(bf16[2,160,256]{2,1,0:T(8,128)(2,1)S(1)} %get-tuple-element.44), channel_id=1, source_target_pairs={{0,28},{4,0},{8,4},{12,8},{16,12},{20,16},{24,20},{28,24},{1,29},{... | collective-permute-start | bytes 491528 | tf_op jit(solution)/shard_map/ppermute | solution.py:337
  38.8 7.8 %collective-permute-start.9 = (bf16[2,48,256]{2,1,0:T(8,128)(2,1)S(1)}, bf16[2,48,256]{2,1,0:T(8,128)(2,1)S(1)}, u32[]{:S(2)}, u32[]{:S(2)}) collective-permute-start(bf16[2,48,256]{2,1,0:T(8,128)(2,1)S(1)} %get-tuple-element.46), channel_id=1, source_target_pairs={{0,32},{32,64},{64,96},{96,128},{128,160},{160,192},{192,224},{224... | collective-permute-start | bytes 147464 | tf_op jit(solution)/shard_map/ppermute | solution.py:343
  40.6 6.0 %collective-permute-start.10 = (bf16[2,48,256]{2,1,0:T(8,128)(2,1)S(1)}, bf16[2,48,256]{2,1,0:T(8,128)(2,1)S(1)}, u32[]{:S(2)}, u32[]{:S(2)}) collective-permute-start(bf16[2,48,256]{2,1,0:T(8,128)(2,1)S(1)} %get-tuple-element.47), channel_id=1, source_target_pairs={{0,224},{32,0},{64,32},{96,64},{128,96},{160,128},{192,160},{224,1... | collective-permute-start | bytes 147464 | tf_op jit(solution)/shard_map/ppermute | solution.py:342
  48.7 1.4 %copy-start = (bf16[8,4,8,16,256]{4,3,2,1,0:T(8,128)(2,1)}, bf16[8,4,8,16,256]{4,3,2,1,0:T(8,128)(2,1)S(1)}, u32[]{:S(2)}) copy-start(bf16[8,4,8,16,256]{4,3,2,1,0:T(8,128)(2,1)S(1)} %get-tuple-element.58) | copy-start | bytes 6291460
  50.0 33.8 %all-to-all-start = ((bf16[8,4,8,16,256]{4,3,2,1,0:T(8,128)(2,1)}), bf16[8,4,8,16,256]{4,3,2,1,0:T(8,128)(2,1)S(1)}, u32[]{:S(2)}, u32[]{:S(2)}) async-start(bf16[8,4,8,16,256]{4,3,2,1,0:T(8,128)(2,1)} %copy-done), calls=%async_computation | async-start | bytes 4194304 | tf_op jit(solution)/shard_map/all_to_all | solution.py:365
  56.6 1.4 %copy-start.1 = (bf16[1024,3,256]{2,0,1:T(8,128)(2,1)S(1)}, bf16[1024,3,256]{2,0,1:T(8,128)(2,1)}, u32[]{:S(2)}) copy-start(bf16[1024,3,256]{2,0,1:T(8,128)(2,1)} %param.11) | copy-start | bytes 4718596
  60.2 2.0 %collective-permute-start.14 = (bf16[2,128,1024]{2,1,0:T(8,128)(2,1)S(1)}, bf16[2,128,1024]{2,1,0:T(8,128)(2,1)S(1)}, u32[]{:S(2)}, u32[]{:S(2)}) collective-permute-start(bf16[2,128,1024]{2,1,0:T(8,128)(2,1)S(1)} %get-tuple-element.55), channel_id=1, source_target_pairs={{0,1},{1,0},{2,3},{3,2},{4,5},{5,4},{6,7},{7,6},{8,9},{9,8},{10,11... | collective-permute-start | bytes 1572872 | tf_op jit(solution)/shard_map/ppermute | solution.py:369
  62.3 29.1 %collective-permute-start.15 = (bf16[128,1024]{1,0:T(8,128)(2,1)S(1)}, bf16[128,1024]{1,0:T(8,128)(2,1)S(1)}, u32[]{:S(2)}, u32[]{:S(2)}) collective-permute-start(bf16[128,1024]{1,0:T(8,128)(2,1)S(1)} %get-tuple-element.57), channel_id=1, source_target_pairs={{0,2},{2,0},{1,3},{3,1},{4,6},{6,4},{5,7},{7,5},{8,10},{10,8},{9,1... | collective-permute-start | bytes 786440 | tf_op jit(solution)/shard_map/ppermute | solution.py:371
  84.8 17.1 %all-to-all-start.1 = ((bf16[8,16,1024]{2,1,0:T(8,128)(2,1)}), bf16[8,16,1024]{2,1,0:T(8,128)(2,1)S(1)}, u32[]{:S(2)}, u32[]{:S(2)}) async-start(bf16[8,16,1024]{2,1,0:T(8,128)(2,1)} %shard_map.102), calls=%async_computation.1 | async-start | bytes 524288 | tf_op jit(solution)/shard_map/all_to_all | solution.py:375

commit v3 on v2

--- a/solution.py
+++ b/solution.py
@@ -40,7 +40,7 @@
     return lax.dot_general(a, b, (((ca,), (cb,)), ((), ())), preferred_element_type=F32)
 
 
-def call(body, out_shape, scratch=(), n_in=0, hbm=(), hbm_out=(), flops=0):
+def call(body, out_shape, scratch=(), n_in=0, hbm=(), hbm_out=(), flops=0, alias=None):
     specs = [pl.BlockSpec(memory_space=pltpu.HBM if i in hbm else pltpu.VMEM) for i in range(n_in)]
     outs = [
         pl.BlockSpec(memory_space=pltpu.HBM if i in hbm_out else pltpu.VMEM)
@@ -55,6 +55,7 @@
         in_specs=specs,
         out_specs=outs,
         scratch_shapes=list(scratch),
+        input_output_aliases=alias or {},
         compiler_params=pltpu.CompilerParams(vmem_limit_bytes=VMEM_LIMIT),
         cost_estimate=pl.CostEstimate(flops=flops, bytes_accessed=0, transcendentals=0),
     )
@@ -83,20 +84,26 @@
     return jnp.where((token == wanted) & (lane < DEPTH), 1.0, 0.0).astype(BF16)
 
 
-def load_kernel(
-    q, k, v, w_out, out_grad, hidden,
-    q_out, kv, w_out_out, own_grad, own_hidden, to_above, to_below, sems,
-):
-    first, last = pl.ds(0, EDGE), pl.ds(TOKENS - EDGE, EDGE)
-    pairs = [(k.at[first], to_above.at[0]), (v.at[first], to_above.at[1])]
-    pairs += [(k.at[last], to_below.at[0]), (v.at[last], to_below.at[1])]
-    pairs += [(out_grad, own_grad), (hidden, own_hidden)]
-    pairs += [(k, kv.at[0]), (v, kv.at[1]), (q, q_out), (w_out, w_out_out)]
+def copy_all(pairs, sems):
     copies = [pltpu.make_async_copy(a, b, sems.at[i]) for i, (a, b) in enumerate(pairs)]
     for copy in copies:
         copy.start()
     for copy in copies:
         copy.wait()
+
+
+def edges_kernel(k, v, to_above, to_below, sems):
+    first, last = pl.ds(0, EDGE), pl.ds(TOKENS - EDGE, EDGE)
+    pairs = [(k.at[first], to_above.at[0]), (v.at[first], to_above.at[1])]
+    pairs += [(k.at[last], to_below.at[0]), (v.at[last], to_below.at[1])]
+    copy_all(pairs, sems)
+
+
+def load_kernel(
+    after, q, k, v, w_out, out_grad, hidden, q_out, kv, w_out_out, own_grad, own_hidden, sems
+):
+    pairs = [(out_grad, own_grad), (hidden, own_hidden), (k, kv.at[0]), (v, kv.at[1])]
+    copy_all(pairs + [(q, q_out), (w_out, w_out_out)], sems)
 
 
 def bands_kernel(kv, above, below, mid, to_left, to_right):
@@ -195,56 +202,64 @@
             out[yx, z] = term[at : at + 16]
 
 
-def first_terms_kernel(
-    grad_q, attn, g0, g1, g2, g3, h0, h1, h2, h3, out, hidden_out, hidden, og, terms, sems
-):
+def hidden_kernel(after, h0, h1, h2, h3, hidden, to_above, to_below):
     head = head_index()
-    for i, (g, h) in enumerate(((g0, h0), (g1, h1), (g2, h2), (g3, h3))):
-        at = pl.ds(pl.multiple_of((head ^ i) * BLK, BLK), BLK)
-        og[at, :] = g[...]
-        hidden[at, :] = h[...]
-    copies = [pltpu.make_async_copy(hidden, hidden_out, sems.at[0])]
-    copies[0].start()
+    for i, piece in enumerate((h0, h1, h2, h3)):
+        hidden[pl.ds(pl.multiple_of((head ^ i) * BLK, BLK), BLK), :] = piece[...]
+    to_above[...] = hidden[:EDGE, :]
+    to_below[...] = hidden[TOKENS - EDGE :, :]
+
+
+def first_terms_kernel(grad_q, attn, g0, g1, g2, g3, hidden, out, og, terms, sems):
+    head = head_index()
+    for i, piece in enumerate((g0, g1, g2, g3)):
+        og[pl.ds(pl.multiple_of((head ^ i) * BLK, BLK), BLK), :] = piece[...]
+    copies = []
     for i, (left, right) in enumerate(((hidden, grad_q), (og, attn))):
         put_term(terms.at[i], dot(left[...], right[...], 0, 0))
-        copies.append(pltpu.make_async_copy(terms.at[i], out.at[i], sems.at[1 + i]))
+        copies.append(pltpu.make_async_copy(terms.at[i], out.at[:, i], sems.at[i]))
         copies[-1].start()
     for copy in copies:
         copy.wait()
 
 
-def columns_kernel(grad_mid, from_left, from_right, inner, to_above, to_below):
+def second_terms_kernel(
+    grad_mid, from_left, from_right, hidden, hid_above, hid_below, first,
+    out, grads, top, bottom, to_above, to_below,
+    hid_mid, terms, sems,
+):
+    hid_mid[:EDGE] = hid_above[...]
+    hid_mid[EDGE : EDGE + TOKENS] = hidden[...]
+    hid_mid[EDGE + TOKENS :] = hid_below[...]
     left = pick(0, 0)
     right = pick(TW - DEPTH, 0)
+    copies = []
     for i in range(2):
         g = grad_mid[i] + dot(left, from_left[i], 1, 0) + dot(right, from_right[i], 1, 0)
-        to_above[i] = g[:EDGE].astype(BF16)
-        inner[i] = g[EDGE : EDGE + TOKENS]
-        to_below[i] = g[EDGE + TOKENS :].astype(BF16)
-
-
-def second_terms_kernel(
-    inner, from_above, from_below, first, hidden_in, terms, grads, hidden, sems
+        g16 = g.astype(BF16)
+        put_term(terms.at[i], dot(hid_mid[...], g16, 0, 0))
+        copies.append(pltpu.make_async_copy(terms.at[i], out.at[:, 2 + i], sems.at[i]))
+        copies[-1].start()
+        to_above[i] = g16[:EDGE]
+        grads[i] = g16[EDGE : EDGE + TOKENS]
+        top[i] = g[EDGE : 2 * EDGE]
+        bottom[i] = g[TOKENS : TOKENS + EDGE]
+        to_below[i] = g16[EDGE + TOKENS :]
+    for copy in copies:
+        copy.wait()
+
+
+def hidden_grad_kernel(
+    grad_q, inner, top, bottom, from_above, from_below, w_qkv_in, keep, send, grads, w_qkv, sem
 ):
-    copies = [pltpu.make_async_copy(hidden_in, hidden, sems.at[0])]
+    copy = pltpu.make_async_copy(w_qkv_in, w_qkv, sem)
+    copy.start()
+    core = lax.axis_index("core")
     for i in range(2):
-        copies.append(pltpu.make_async_copy(first.at[i], terms.at[:, i], sems.at[1 + i]))
-    for copy in copies:
-        copy.start()
-    for i in range(2):
-        grads[i, :EDGE] = (inner[i, :EDGE] + from_above[i].astype(F32)).astype(BF16)
-        grads[i, EDGE : TOKENS - EDGE] = inner[i, EDGE : TOKENS - EDGE].astype(BF16)
-        last = inner[i, TOKENS - EDGE :] + from_below[i].astype(F32)
-        grads[i, TOKENS - EDGE :] = last.astype(BF16)
-    copies[0].wait()
-    for i in range(2):
-        put_term(terms.at[:, 2 + i], dot(hidden[...], grads[i], 0, 0))
-    copies[1].wait()
-    copies[2].wait()
-
-
-def hidden_grad_kernel(grad_q, grads, w_qkv, keep, send):
-    core = lax.axis_index("core")
+        grads[i, :EDGE] = (top[i] + from_above[i].astype(F32)).astype(BF16)
+        grads[i, EDGE : TOKENS - EDGE] = inner[i, EDGE : TOKENS - EDGE]
+        grads[i, TOKENS - EDGE :] = (bottom[i] + from_below[i].astype(F32)).astype(BF16)
+    copy.wait()
     for yl in range(YL):
         for out, c in ((send, 1 - core), (keep, core)):
             at = pl.ds(pl.multiple_of((yl * CORE + c) * BLK, BLK), BLK)
@@ -288,6 +303,17 @@
 
 
 SWAP = [(0, 1), (1, 0)]
+COLS = ("yh", "x", "yl")
+
+
+def columns(step):
+    pairs = []
+    for col in range(YH * X):
+        for yl in range(YL):
+            to = col + step
+            to_yl = yl if 0 <= to < YH * X else 1 - yl
+            pairs.append((col * YL + yl, (to % (YH * X)) * YL + to_yl))
+    return pairs
 
 
 def per_device(hidden_in, queries, keys, values, w_qkv, w_out, out_grad):
@@ -301,26 +327,32 @@
     band = shaped((2, BAND, FEAT))
     mids = shaped((2, CENTER, FEAT))
     own = shaped((BLK, D))
-    q, kv, w_out, g0, h0, to_above, to_below = call(
-        load_kernel,
-        (flat, shaped((2, TOKENS, FEAT)), shaped((FEAT, D)), own, own, edge, edge),
-        scratch=[pltpu.SemaphoreType.DMA((10,))],
-        n_in=6,
-        hbm=range(6),
-    )(q, k, v, w_out, out_grad.reshape(BLK, D), hidden_in.reshape(BLK, D))
-
+    own_grad = out_grad.reshape(BLK, D)
+    own_hidden = hidden_in.reshape(BLK, D)
+    to_above, to_below = call(
+        edges_kernel, (edge, edge), scratch=[pltpu.SemaphoreType.DMA((4,))], n_in=2, hbm=(0, 1)
+    )(k, v)
     below = lax.ppermute(to_above, "z", ring(Z, -1))
     above = lax.ppermute(to_below, "z", ring(Z, 1))
-    g2 = lax.ppermute(g0, "yl", SWAP)
-    g1 = lax.ppermute(g0, "core", SWAP)
+    q, kv, w_out, g0, h0 = call(
+        load_kernel,
+        (flat, shaped((2, TOKENS, FEAT)), shaped((FEAT, D)), own, own),
+        scratch=[pltpu.SemaphoreType.DMA((6,))],
+        n_in=7,
+        hbm=range(1, 7),
+        flops=10_000_000_000,
+    )(to_above, q, k, v, w_out, own_grad, own_hidden)
+    g2 = lax.ppermute(own_grad, "yl", SWAP)
+    g1 = lax.ppermute(own_grad, "core", SWAP)
     h2 = lax.ppermute(h0, "yl", SWAP)
     h1 = lax.ppermute(h0, "core", SWAP)
 
     mid, to_left, to_right = call(bands_kernel, (mids, band, band), n_in=3)(kv, above, below)
-    from_right = lax.ppermute(to_left, YX, ring(YH * X, -1))
-    from_left = lax.ppermute(to_right, YX, ring(YH * X, 1))
+    from_right = lax.ppermute(to_left, COLS, columns(-1))
+    from_left = lax.ppermute(to_right, COLS, columns(1))
+    g2, _ = lax.optimization_barrier((g2, to_left))
     g3 = lax.ppermute(g2, "core", SWAP)
-    h2, _ = lax.optimization_barrier((h2, from_left))
+    h2, _, _ = lax.optimization_barrier((h2, from_left, from_right))
     h3 = lax.ppermute(h2, "core", SWAP)
 
     attn, grad_q, grad_mid, band_left, band_right = call(
@@ -334,38 +366,57 @@
         n_in=9,
     )(q, g0, g1, g2, g3, w_out, mid, from_left, from_right)
 
-    got_right = lax.ppermute(band_left, YX, ring(YH * X, -1))
-    got_left = lax.ppermute(band_right, YX, ring(YH * X, 1))
-    inner, to_above, to_below = call(
-        columns_kernel, (shaped((2, TOKENS, FEAT), F32), edge, edge), n_in=3
-    )(grad_mid, got_left, got_right)
+    got_right = lax.ppermute(band_left, COLS, columns(-1))
+    got_left = lax.ppermute(band_right, COLS, columns(1))
+    hid_edge = shaped((EDGE, D))
+    hidden, to_above, to_below = call(
+        hidden_kernel, (shaped((TOKENS, D)), hid_edge, hid_edge), n_in=5
+    )(band_left, h0, h1, h2, h3)
+    hid_below = lax.ppermute(to_above, "z", ring(Z, -1))
+    hid_above = lax.ppermute(to_below, "z", ring(Z, 1))
+    all_terms = shaped((YH * X, 4, Z, 16, FEAT))
+    (terms,) = call(
+        first_terms_kernel,
+        (all_terms,),
+        scratch=[
+            pltpu.VMEM((TOKENS, D), BF16),
+            pltpu.VMEM((2, YH * X, Z, 16, FEAT), BF16),
+            pltpu.SemaphoreType.DMA((2,)),
+        ],
+        n_in=7,
+        hbm_out=(0,),
+        flops=10_000_000_000,
+    )(grad_q, attn, g0, g1, g2, g3, hidden)
+    edge32 = shaped((2, EDGE, FEAT), F32)
+    terms, grads, top, bottom, to_above, to_below = call(
+        second_terms_kernel,
+        (all_terms, shaped((2, TOKENS, FEAT)), edge32, edge32, edge, edge),
+        scratch=[
+            pltpu.VMEM((CENTER, D), BF16),
+            pltpu.VMEM((2, YH * X, Z, 16, FEAT), BF16),
+            pltpu.SemaphoreType.DMA((2,)),
+        ],
+        n_in=7,
+        hbm=(6,),
+        hbm_out=(0,),
+        alias={6: 0},
+    )(grad_mid, got_left, got_right, hidden, hid_above, hid_below, terms)
     got_below = lax.ppermute(to_above, "z", ring(Z, -1))
     got_above = lax.ppermute(to_below, "z", ring(Z, 1))
-
-    first, hidden = call(
-        first_terms_kernel,
-        (shaped((2, YH * X, Z, 16, FEAT)), shaped((TOKENS, D))),
+    terms = lax.all_to_all(terms, YX, 0, 0, tiled=True)
+
+    half = shaped((YL, BLK, D))
+    keep, send = call(
+        hidden_grad_kernel,
+        (half, half),
         scratch=[
-            pltpu.VMEM((TOKENS, D), BF16),
-            pltpu.VMEM((TOKENS, D), BF16),
-            pltpu.VMEM((2, YH * X, Z, 16, FEAT), BF16),
-            pltpu.SemaphoreType.DMA((3,)),
+            pltpu.VMEM((2, TOKENS, FEAT), BF16),
+            pltpu.VMEM((3, D, FEAT), BF16),
+            pltpu.SemaphoreType.DMA,
         ],
-        n_in=10,
-        hbm_out=(0, 1),
-        flops=10_000_000_000,
-    )(grad_q, attn, g0, g1, g2, g3, h0, h1, h2, h3)
-    terms, grads = call(
-        second_terms_kernel,
-        (shaped((YH * X, 4, Z, 16, FEAT)), shaped((2, TOKENS, FEAT))),
-        scratch=[pltpu.VMEM((TOKENS, D), BF16), pltpu.SemaphoreType.DMA((3,))],
-        n_in=5,
-        hbm=(3, 4),
-    )(inner, got_above, got_below, first, hidden)
-    terms = lax.all_to_all(terms, YX, 0, 0, tiled=True)
-
-    half = shaped((YL, BLK, D))
-    keep, send = call(hidden_grad_kernel, (half, half), n_in=3)(grad_q, grads, w3)
+        n_in=7,
+        hbm=(6,),
+    )(grad_q, grads, top, bottom, got_above, got_below, w3)
     got = lax.ppermute(send, "core", SWAP)
     stay, send = call(halve_kernel, (shaped((BLK, D), F32), shaped((BLK, D))), n_in=2)(keep, got)
     got = lax.ppermute(send, "yl", SWAP)

time: 103 us -> 95.2 us (0.924)
  waiting for transfers between devices: 42.8 us -> 36 us
  local copies, waits for them, and re-layouts: 2.75 us -> 0.01 us
  Pallas kernels: 15.6 us -> 17.7 us
    all_to_all x1, waiting for transfers between devices: 20.8 us -> 14.6 us  [per_device(): terms = lax.all_to_all(terms, YX, 0, 0, tiled=True)]
    ppermute x6 -> x8, waiting for transfers between devices: 9.63 us -> 3.67 us  [the longest x1 2.77 us: per_device(): from_left = lax.ppermute(to_right, COLS, columns(1))]
    ppermute x1, starting transfers between devices: 4.02 us -> 1.12 us  [per_device(): got_below = lax.ppermute(to_above, 'z', ring(Z, -1))]
    unnamed x4 -> x2, local copies, waits for them, and re-layouts: 2.75 us -> 0.01 us
    pallas_call x10 -> x11, Pallas kernels: 15.6 us -> 17.7 us  [on(): run(*(hold(a, pltpu.HBM) if i in hbm else a for i, a in enumerate(args)))]
    ppermute x1, waiting for transfers between devices: 0.08 us -> 1.98 us  [per_device(): got_above = lax.ppermute(to_below, 'z', ring(Z, 1))]
    ppermute x1, waiting for transfers between devices: 0.56 us -> 2.06 us  [per_device(): above = lax.ppermute(to_below, 'z', ring(Z, 1))]
    all_to_all x1, waiting for transfers between devices: 9.81 us -> 10.9 us  [per_device(): parts = lax.all_to_all(parts, 'z', 0, 0, tiled=True)]
  transfers between devices with their start and end apart: 18 -> 20, of which waited for: 8 -> 8; matrix products, arithmetic and copies ran while one was open for 1% -> 1% of each run, Pallas kernels for 11% -> 15%
where the time goes in v3:
time: 95.2 us; the launch traced here: 94.8 us
  starting transfers between devices  39.5 us (41%)
  waiting for transfers between devices  36 us (38%)
  Pallas kernels  17.7 us (19%)
    pallas_call x11, Pallas kernels, on(): run(*(hold(a, pltpu.HBM) if i in hbm else a for i, a in enumerate(args)))  17.7 us
    all_to_all x1, waiting for transfers between devices, per_device(): terms = lax.all_to_all(terms, YX, 0, 0, tiled=True)  14.6 us
    all_to_all x1, waiting for transfers between devices, per_device(): parts = lax.all_to_all(parts, 'z', 0, 0, tiled=True)  10.9 us
    all_to_all x1, starting transfers between devices, per_device(): terms = lax.all_to_all(terms, YX, 0, 0, tiled=True)  7.24 us
    all_to_all x1, starting transfers between devices, per_device(): parts = lax.all_to_all(parts, 'z', 0, 0, tiled=True)  6.39 us
    ppermute x1, starting transfers between devices, per_device(): below = lax.ppermute(to_above, 'z', ring(Z, -1))  3.94 us
    ppermute x1, starting transfers between devices, per_device(): got_right = lax.ppermute(band_left, COLS, columns(-1))  3.76 us
    ppermute x1, starting transfers between devices, per_device(): hid_below = lax.ppermute(to_above, 'z', ring(Z, -1))  3.3 us
  transfers between devices with their start and end apart: 20, of which 8 were waited for; matrix products, arithmetic and copies ran while one was open for 1% of the time, Pallas kernels for 15%

profile of v3, /device:TPU:8, one launch (start us, length us, event | category | flops | bytes accessed | tf_op | source)
XLA Modules:
  0.0 94.8 jit_solution(1757893163788578364)
XLA Ops:
  0.6 2.3 %collective-permute-start.1 = (bf16[128,1024]{1,0:T(8,128)(2,1)}, bf16[128,1024]{1,0:T(8,128)(2,1)S(1)}, u32[]{:S(2)}, u32[]{:S(2)}) collective-permute-start(bf16[128,1024]{1,0:T(8,128)(2,1)} %bitcast.17), channel_id=1, source_target_pairs={{0,2},{2,0},{1,3},{3,1},{4,6},{6,4},{5,7},{7,5},{8,10},{10,8},{9,1... | collective-permute-start | bytes 786440 | tf_op jit(solution)/shard_map/ppermute | solution.py:345
  3.7 1.5 %shard_map.95 = (bf16[512,256]{1,0:T(8,128)(2,1)S(1)}, bf16[2,512,256]{2,1,0:T(8,128)(2,1)S(1)}, bf16[256,1024]{1,0:T(8,128)(2,1)S(1)}, bf16[128,1024]{1,0:T(8,128)(2,1)S(1)}, bf16[128,1024]{1,0:T(8,128)(2,1)S(1)}) custom-call(bf16[2,48,256]{2,1,0:T(8,128)(2,1)S(1)} %get-tuple-element.35.after, bf16[512,256]{1,0:T(8,128)(2,1)} %bitcast.15, ...), custom_call_target="tpu_custom_call" | custom-call | flops 10000000000 | tf_op jit(solution)/shard_map/pallas_call | solution.py:65
  5.4 1.7 %collective-permute-start.2 = (bf16[2,48,256]{2,1,0:T(8,128)(2,1)S(1)}, bf16[2,48,256]{2,1,0:T(8,128)(2,1)S(1)}, u32[]{:S(2)}, u32[]{:S(2)}) collective-permute-start(bf16[2,48,256]{2,1,0:T(8,128)(2,1)S(1)} %get-tuple-element.39), channel_id=1, source_target_pairs={{0,32},{32,64},{64,96},{96,128},{128,160},{160,192},{192,224},{224... | collective-permute-start | bytes 147464 | tf_op jit(solution)/shard_map/ppermute | solution.py:336
  7.1 3.9 %collective-permute-start.3 = (bf16[2,48,256]{2,1,0:T(8,128)(2,1)S(1)}, bf16[2,48,256]{2,1,0:T(8,128)(2,1)S(1)}, u32[]{:S(2)}, u32[]{:S(2)}) collective-permute-start(bf16[2,48,256]{2,1,0:T(8,128)(2,1)S(1)} %get-tuple-element.35.after), channel_id=1, source_target_pairs={{0,224},{32,0},{64,32},{96,64},{128,96},{160,128},{192,160},{224,1... | collective-permute-start | bytes 147464 | tf_op jit(solution)/shard_map/ppermute | solution.py:335
  11.1 2.1 %collective-permute-done.2.above = bf16[2,48,256]{2,1,0:T(8,128)(2,1)S(1)} collective-permute-done((bf16[2,48,256]{2,1,0:T(8,128)(2,1)S(1)}, bf16[2,48,256]{2,1,0:T(8,128)(2,1)S(1)}, u32[]{:S(2)}, u32[]{:S(2)}) %collective-permute-start.2) | collective-permute-done | bytes 49184 | tf_op jit(solution)/shard_map/ppermute | solution.py:336
  13.6 1.6 %collective-permute-start.5 = (bf16[2,160,256]{2,1,0:T(8,128)(2,1)S(1)}, bf16[2,160,256]{2,1,0:T(8,128)(2,1)S(1)}, u32[]{:S(2)}, u32[]{:S(2)}) collective-permute-start(bf16[2,160,256]{2,1,0:T(8,128)(2,1)S(1)} %get-tuple-element.44), channel_id=1, source_target_pairs={{0,4},{2,6},{4,8},{6,10},{8,12},{10,14},{12,16},{14,18},{16,20},{1... | collective-permute-start | bytes 491528 | tf_op jit(solution)/shard_map/ppermute | solution.py:352
  15.2 2.6 %collective-permute-start.6 = (bf16[2,160,256]{2,1,0:T(8,128)(2,1)S(1)}, bf16[2,160,256]{2,1,0:T(8,128)(2,1)S(1)}, u32[]{:S(2)}, u32[]{:S(2)}) collective-permute-start(bf16[2,160,256]{2,1,0:T(8,128)(2,1)S(1)} %get-tuple-element.40), channel_id=1, source_target_pairs={{0,30},{2,28},{4,0},{6,2},{8,4},{10,6},{12,8},{14,10},{16,12},{18,... | collective-permute-start | bytes 491528 | tf_op jit(solution)/shard_map/ppermute | solution.py:351
  18.3 2.8 %collective-permute-done.5.from_left = bf16[2,160,256]{2,1,0:T(8,128)(2,1)S(1)} collective-permute-done((bf16[2,160,256]{2,1,0:T(8,128)(2,1)S(1)}, bf16[2,160,256]{2,1,0:T(8,128)(2,1)S(1)}, u32[]{:S(2)}, u32[]{:S(2)}) %collective-permute-start.5) | collective-permute-done | bytes 163872 | tf_op jit(solution)/shard_map/ppermute | solution.py:352
  21.6 5.3 %shard_map.97 = (bf16[512,256]{1,0:T(8,128)(2,1)S(1)}, bf16[512,256]{1,0:T(8,128)(2,1)S(1)}, f32[2,608,256]{2,1,0:T(8,128)S(1)}, bf16[2,160,256]{2,1,0:T(8,128)(2,1)S(1)}, bf16[2,160,256]{2,1,0:T(8,128)(2,1)S(1)}) custom-call(bf16[512,256]{1,0:T(8,128)(2,1)S(1)} %get-tuple-element.36.q, bf16[128,1024]{1,0:T(8,128)(2,1)S(1)} %get-tuple-element.37.og0.g0, ...), custom_call_target="tpu_custom_call" | custom-call | tf_op jit(solution)/shard_map/pallas_call | solution.py:65
  27.6 3.8 %collective-permute-start.8 = (bf16[2,160,256]{2,1,0:T(8,128)(2,1)S(1)}, bf16[2,160,256]{2,1,0:T(8,128)(2,1)S(1)}, u32[]{:S(2)}, u32[]{:S(2)}) collective-permute-start(bf16[2,160,256]{2,1,0:T(8,128)(2,1)S(1)} %get-tuple-element.48.after), channel_id=1, source_target_pairs={{0,30},{2,28},{4,0},{6,2},{8,4},{10,6},{12,8},{14,10},{16,12},{18,... | collective-permute-start | bytes 491528 | tf_op jit(solution)/shard_map/ppermute | solution.py:369
  31.6 3.3 %collective-permute-start.13 = (bf16[48,1024]{1,0:T(8,128)(2,1)S(1)}, bf16[48,1024]{1,0:T(8,128)(2,1)S(1)}, u32[]{:S(2)}, u32[]{:S(2)}) collective-permute-start(bf16[48,1024]{1,0:T(8,128)(2,1)S(1)} %get-tuple-element.53), channel_id=1, source_target_pairs={{0,224},{32,0},{64,32},{96,64},{128,96},{160,128},{192,160},{224,1... | collective-permute-start | bytes 294920 | tf_op jit(solution)/shard_map/ppermute | solution.py:375
  34.9 1.8 %shard_map.99.first = bf16[8,4,8,16,256]{4,3,2,1,0:T(8,128)(2,1)} custom-call(bf16[512,256]{1,0:T(8,128)(2,1)S(1)} %get-tuple-element.45.grad_q, bf16[512,256]{1,0:T(8,128)(2,1)S(1)} %get-tuple-element.54.attn, bf16[128,1024]{1,0:T(8,128)(2,1)S(1)} %get-tuple-element.37.og0.g0, bf16[128,1024]{1,0:T(8,128)(2,1)S(1)} %collective-permute-done.og1.g1, ...), custom_call_target="tpu_custom_call" | custom-call | flops 10000000000 | tf_op jit(solution)/shard_map/pallas_call | solution.py:65
  37.5 2.4 %shard_map.100 = (bf16[8,4,8,16,256]{4,3,2,1,0:T(8,128)(2,1)}, bf16[2,512,256]{2,1,0:T(8,128)(2,1)S(1)}, f32[2,48,256]{2,1,0:T(8,128)S(1)}, f32[2,48,256]{2,1,0:...) custom-call(f32[2,608,256]{2,1,0:T(8,128)S(1)} %get-tuple-element.46, ...), custom_call_target="tpu_custom_call", output_to_operand_aliasing={{0}: (6, {})} | custom-call | tf_op jit(solution)/shard_map/pallas_call | solution.py:65
  40.0 7.2 %all-to-all-start = ((bf16[8,4,8,16,256]{4,3,2,1,0:T(8,128)(2,1)}), bf16[8,4,8,16,256]{4,3,2,1,0:T(8,128)(2,1)S(1)}, u32[]{:S(2)}, u32[]{:S(2)}) async-start(bf16[8,4,8,16,256]{4,3,2,1,0:T(8,128)(2,1)} %get-tuple-element.64), calls=%async_computation | async-start | bytes 4194304 | tf_op jit(solution)/shard_map/all_to_all | solution.py:406
  47.2 2.2 %collective-permute-start.14 = (bf16[2,48,256]{2,1,0:T(8,128)(2,1)S(1)}, bf16[2,48,256]{2,1,0:T(8,128)(2,1)S(1)}, u32[]{:S(2)}, u32[]{:S(2)}) collective-permute-start(bf16[2,48,256]{2,1,0:T(8,128)(2,1)S(1)} %get-tuple-element.58), channel_id=1, source_target_pairs={{0,32},{32,64},{64,96},{96,128},{128,160},{160,192},{192,224},{224... | collective-permute-start | bytes 147464 | tf_op jit(solution)/shard_map/ppermute | solution.py:405
  49.4 1.1 %collective-permute-start.15 = (bf16[2,48,256]{2,1,0:T(8,128)(2,1)S(1)}, bf16[2,48,256]{2,1,0:T(8,128)(2,1)S(1)}, u32[]{:S(2)}, u32[]{:S(2)}) collective-permute-start(bf16[2,48,256]{2,1,0:T(8,128)(2,1)S(1)} %get-tuple-element.59), channel_id=1, source_target_pairs={{0,224},{32,0},{64,32},{96,64},{128,96},{160,128},{192,160},{224,1... | collective-permute-start | bytes 147464 | tf_op jit(solution)/shard_map/ppermute | solution.py:404
  50.5 2.0 %collective-permute-done.14.from_above = bf16[2,48,256]{2,1,0:T(8,128)(2,1)S(1)} collective-permute-done((bf16[2,48,256]{2,1,0:T(8,128)(2,1)S(1)}, bf16[2,48,256]{2,1,0:T(8,128)(2,1)S(1)}, u32[]{:S(2)}, u32[]{:S(2)}) %collective-permute-start.14) | collective-permute-done | bytes 49184 | tf_op jit(solution)/shard_map/ppermute | solution.py:405
  52.5 1.0 %collective-permute-done.15.from_below = bf16[2,48,256]{2,1,0:T(8,128)(2,1)S(1)} collective-permute-done((bf16[2,48,256]{2,1,0:T(8,128)(2,1)S(1)}, bf16[2,48,256]{2,1,0:T(8,128)(2,1)S(1)}, u32[]{:S(2)}, u32[]{:S(2)}) %collective-permute-start.15) | collective-permute-done | bytes 49184 | tf_op jit(solution)/shard_map/ppermute | solution.py:404
  53.5 3.6 %shard_map.101 = (bf16[2,128,1024]{2,1,0:T(8,128)(2,1)S(1)}, bf16[2,128,1024]{2,1,0:T(8,128)(2,1)S(1)}) custom-call(bf16[512,256]{1,0:T(8,128)(2,1)S(1)} %get-tuple-element.45.grad_q, bf16[2,512,256]{2,1,0:T(8,128)(2,1)S(1)} %get-tuple-element.55.inner, f32[2,48,256]{2,1,0:T(8,128)S(1)} %get-tuple-element.56.top, ...), custom_call_target="tpu_custom_call" | custom-call | tf_op jit(solution)/shard_map/pallas_call | solution.py:65
  57.2 1.9 %collective-permute-done.16.got = bf16[2,128,1024]{2,1,0:T(8,128)(2,1)S(1)} collective-permute-done((bf16[2,128,1024]{2,1,0:T(8,128)(2,1)S(1)}, bf16[2,128,1024]{2,1,0:T(8,128)(2,1)S(1)}, u32[]{:S(2)}, u32[]{:S(2)}) %collective-permute-start.16) | collective-permute-done | bytes 524320 | tf_op jit(solution)/shard_map/ppermute | solution.py:420
  59.2 1.4 %collective-permute-start.17 = (bf16[128,1024]{1,0:T(8,128)(2,1)S(1)}, bf16[128,1024]{1,0:T(8,128)(2,1)S(1)}, u32[]{:S(2)}, u32[]{:S(2)}) collective-permute-start(bf16[128,1024]{1,0:T(8,128)(2,1)S(1)} %get-tuple-element.63), channel_id=1, source_target_pairs={{0,2},{2,0},{1,3},{3,1},{4,6},{6,4},{5,7},{7,5},{8,10},{10,8},{9,1... | collective-permute-start | bytes 786440 | tf_op jit(solution)/shard_map/ppermute | solution.py:422
  60.6 14.6 %all-to-all-done.terms = bf16[8,4,8,16,256]{4,3,2,1,0:T(8,128)(2,1)S(1)} async-done(((bf16[8,4,8,16,256]{4,3,2,1,0:T(8,128)(2,1)}), bf16[8,4,8,16,256]{4,3,2,1,0:T(8,128)(2,1)S(1)}, u32[]{:S(2)}, u32[]{:S(2)}) %all-to-all-start) | async-done | bytes 2097184 | tf_op jit(solution)/shard_map/all_to_all | solution.py:406
  76.1 6.4 %all-to-all-start.1 = ((bf16[8,16,1024]{2,1,0:T(8,128)(2,1)}), bf16[8,16,1024]{2,1,0:T(8,128)(2,1)S(1)}, u32[]{:S(2)}, u32[]{:S(2)}) async-start(bf16[8,16,1024]{2,1,0:T(8,128)(2,1)} %shard_map.103), calls=%async_computation.1 | async-start | bytes 524288 | tf_op jit(solution)/shard_map/all_to_all | solution.py:426
  83.3 10.9 %all-to-all-done.1.parts = bf16[8,16,1024]{2,1,0:T(8,128)(2,1)S(1)} async-done(((bf16[8,16,1024]{2,1,0:T(8,128)(2,1)}), bf16[8,16,1024]{2,1,0:T(8,128)(2,1)S(1)}, u32[]{:S(2)}, u32[]{:S(2)}) %all-to-all-start.1) | async-done | bytes 262176 | tf_op jit(solution)/shard_map/all_to_all | solution.py:426
  (30 shorter events, 6.7 us)
Async XLA Ops:
  0.6 17.2 %collective-permute-start.1 = (bf16[128,1024]{1,0:T(8,128)(2,1)}, bf16[128,1024]{1,0:T(8,128)(2,1)S(1)}, u32[]{:S(2)}, u32[]{:S(2)}) collective-permute-start(bf16[128,1024]{1,0:T(8,128)(2,1)} %bitcast.17), channel_id=1, source_target_pairs={{0,2},{2,0},{1,3},{3,1},{4,6},{6,4},{5,7},{7,5},{8,10},{10,8},{9,1... | collective-permute-start | bytes 786440 | tf_op jit(solution)/shard_map/ppermute | solution.py:345
  3.7 14.1 %copy-start = (bf16[1,8,16,1024]{3,2,1,0:T(8,128)(2,1)S(1)}, bf16[1,8,16,1024]{3,2,1,0:T(8,128)(2,1)}, u32[]{:S(2)}) copy-start(bf16[1,8,16,1024]{3,2,1,0:T(8,128)(2,1)} %param.13) | copy-start | bytes 786436
  5.3 15.8 %collective-permute-start.10 = (bf16[128,1024]{1,0:T(8,128)(2,1)S(1)}, bf16[128,1024]{1,0:T(8,128)(2,1)S(1)}, u32[]{:S(2)}, u32[]{:S(2)}) collective-permute-start(bf16[128,1024]{1,0:T(8,128)(2,1)S(1)} %get-tuple-element.49.h0), channel_id=1, source_target_pairs={{0,2},{2,0},{1,3},{3,1},{4,6},{6,4},{5,7},{7,5},{8,10},{10,8},{9,1... | collective-permute-start | bytes 786440 | tf_op jit(solution)/shard_map/ppermute | solution.py:347
  5.4 7.7 %collective-permute-start.2 = (bf16[2,48,256]{2,1,0:T(8,128)(2,1)S(1)}, bf16[2,48,256]{2,1,0:T(8,128)(2,1)S(1)}, u32[]{:S(2)}, u32[]{:S(2)}) collective-permute-start(bf16[2,48,256]{2,1,0:T(8,128)(2,1)S(1)} %get-tuple-element.39), channel_id=1, source_target_pairs={{0,32},{32,64},{64,96},{96,128},{128,160},{160,192},{192,224},{224... | collective-permute-start | bytes 147464 | tf_op jit(solution)/shard_map/ppermute | solution.py:336
  7.1 6.0 %collective-permute-start.3 = (bf16[2,48,256]{2,1,0:T(8,128)(2,1)S(1)}, bf16[2,48,256]{2,1,0:T(8,128)(2,1)S(1)}, u32[]{:S(2)}, u32[]{:S(2)}) collective-permute-start(bf16[2,48,256]{2,1,0:T(8,128)(2,1)S(1)} %get-tuple-element.35.after), channel_id=1, source_target_pairs={{0,224},{32,0},{64,32},{96,64},{128,96},{160,128},{192,160},{224,1... | collective-permute-start | bytes 147464 | tf_op jit(solution)/shard_map/ppermute | solution.py:335
  13.6 7.5 %collective-permute-start.5 = (bf16[2,160,256]{2,1,0:T(8,128)(2,1)S(1)}, bf16[2,160,256]{2,1,0:T(8,128)(2,1)S(1)}, u32[]{:S(2)}, u32[]{:S(2)}) collective-permute-start(bf16[2,160,256]{2,1,0:T(8,128)(2,1)S(1)} %get-tuple-element.44), channel_id=1, source_target_pairs={{0,4},{2,6},{4,8},{6,10},{8,12},{10,14},{12,16},{14,18},{16,20},{1... | collective-permute-start | bytes 491528 | tf_op jit(solution)/shard_map/ppermute | solution.py:352
  15.2 5.9 %collective-permute-start.6 = (bf16[2,160,256]{2,1,0:T(8,128)(2,1)S(1)}, bf16[2,160,256]{2,1,0:T(8,128)(2,1)S(1)}, u32[]{:S(2)}, u32[]{:S(2)}) collective-permute-start(bf16[2,160,256]{2,1,0:T(8,128)(2,1)S(1)} %get-tuple-element.40), channel_id=1, source_target_pairs={{0,30},{2,28},{4,0},{6,2},{8,4},{10,6},{12,8},{14,10},{16,12},{18,... | collective-permute-start | bytes 491528 | tf_op jit(solution)/shard_map/ppermute | solution.py:351
  17.8 3.8 %collective-permute-start = (bf16[128,1024]{1,0:T(8,128)(2,1)S(1)}, bf16[128,1024]{1,0:T(8,128)(2,1)S(1)}, u32[]{:S(2)}, u32[]{:S(2)}) collective-permute-start(bf16[128,1024]{1,0:T(8,128)(2,1)S(1)} %bitcast.19), channel_id=1, source_target_pairs={{0,1},{1,0},{2,3},{3,2},{4,5},{5,4},{6,7},{7,6},{8,9},{9,8},{10,11... | collective-permute-start | bytes 786440 | tf_op jit(solution)/shard_map/ppermute | solution.py:346
  17.8 3.8 %collective-permute-start.4 = (bf16[128,1024]{1,0:T(8,128)(2,1)S(1)}, bf16[128,1024]{1,0:T(8,128)(2,1)S(1)}, u32[]{:S(2)}, u32[]{:S(2)}) collective-permute-start(bf16[128,1024]{1,0:T(8,128)(2,1)S(1)} %collective-permute-done.1.og2.g2), channel_id=1, source_target_pairs={{0,1},{1,0},{2,3},{3,2},{4,5},{5,4},{6,7},{7,6},{8,9},{9,8},{10,11... | collective-permute-start | bytes 786440 | tf_op jit(solution)/shard_map/ppermute | solution.py:354
  21.1 10.3 %collective-permute-start.9 = (bf16[128,1024]{1,0:T(8,128)(2,1)S(1)}, bf16[128,1024]{1,0:T(8,128)(2,1)S(1)}, u32[]{:S(2)}, u32[]{:S(2)}) collective-permute-start(bf16[128,1024]{1,0:T(8,128)(2,1)S(1)} %get-tuple-element.49.h0), channel_id=1, source_target_pairs={{0,1},{1,0},{2,3},{3,2},{4,5},{5,4},{6,7},{7,6},{8,9},{9,8},{10,11... | collective-permute-start | bytes 786440 | tf_op jit(solution)/shard_map/ppermute | solution.py:348
  21.1 10.3 %collective-permute-start.11 = (bf16[128,1024]{1,0:T(8,128)(2,1)S(1)}, bf16[128,1024]{1,0:T(8,128)(2,1)S(1)}, u32[]{:S(2)}, u32[]{:S(2)}) collective-permute-start(bf16[128,1024]{1,0:T(8,128)(2,1)S(1)} %collective-permute-done.10.h2), channel_id=1, source_target_pairs={{0,1},{1,0},{2,3},{3,2},{4,5},{5,4},{6,7},{7,6},{8,9},{9,8},{10,11... | collective-permute-start | bytes 786440 | tf_op jit(solution)/shard_map/ppermute | solution.py:356
  27.0 10.6 %collective-permute-start.7 = (bf16[2,160,256]{2,1,0:T(8,128)(2,1)S(1)}, bf16[2,160,256]{2,1,0:T(8,128)(2,1)S(1)}, u32[]{:S(2)}, u32[]{:S(2)}) collective-permute-start(bf16[2,160,256]{2,1,0:T(8,128)(2,1)S(1)} %get-tuple-element.47), channel_id=1, source_target_pairs={{0,4},{2,6},{4,8},{6,10},{8,12},{10,14},{12,16},{14,18},{16,20},{1... | collective-permute-start | bytes 491528 | tf_op jit(solution)/shard_map/ppermute | solution.py:370
  27.6 9.9 %collective-permute-start.8 = (bf16[2,160,256]{2,1,0:T(8,128)(2,1)S(1)}, bf16[2,160,256]{2,1,0:T(8,128)(2,1)S(1)}, u32[]{:S(2)}, u32[]{:S(2)}) collective-permute-start(bf16[2,160,256]{2,1,0:T(8,128)(2,1)S(1)} %get-tuple-element.48.after), channel_id=1, source_target_pairs={{0,30},{2,28},{4,0},{6,2},{8,4},{10,6},{12,8},{14,10},{16,12},{18,... | collective-permute-start | bytes 491528 | tf_op jit(solution)/shard_map/ppermute | solution.py:369
  31.5 6.1 %collective-permute-start.12 = (bf16[48,1024]{1,0:T(8,128)(2,1)S(1)}, bf16[48,1024]{1,0:T(8,128)(2,1)S(1)}, u32[]{:S(2)}, u32[]{:S(2)}) collective-permute-start(bf16[48,1024]{1,0:T(8,128)(2,1)S(1)} %get-tuple-element.52), channel_id=1, source_target_pairs={{0,32},{32,64},{64,96},{96,128},{128,160},{160,192},{192,224},{224... | collective-permute-start | bytes 294920 | tf_op jit(solution)/shard_map/ppermute | solution.py:376
  31.6 6.0 %collective-permute-start.13 = (bf16[48,1024]{1,0:T(8,128)(2,1)S(1)}, bf16[48,1024]{1,0:T(8,128)(2,1)S(1)}, u32[]{:S(2)}, u32[]{:S(2)}) collective-permute-start(bf16[48,1024]{1,0:T(8,128)(2,1)S(1)} %get-tuple-element.53), channel_id=1, source_target_pairs={{0,224},{32,0},{64,32},{96,64},{128,96},{160,128},{192,160},{224,1... | collective-permute-start | bytes 294920 | tf_op jit(solution)/shard_map/ppermute | solution.py:375
  40.0 35.2 %all-to-all-start = ((bf16[8,4,8,16,256]{4,3,2,1,0:T(8,128)(2,1)}), bf16[8,4,8,16,256]{4,3,2,1,0:T(8,128)(2,1)S(1)}, u32[]{:S(2)}, u32[]{:S(2)}) async-start(bf16[8,4,8,16,256]{4,3,2,1,0:T(8,128)(2,1)} %get-tuple-element.64), calls=%async_computation | async-start | bytes 4194304 | tf_op jit(solution)/shard_map/all_to_all | solution.py:406
  47.2 5.3 %collective-permute-start.14 = (bf16[2,48,256]{2,1,0:T(8,128)(2,1)S(1)}, bf16[2,48,256]{2,1,0:T(8,128)(2,1)S(1)}, u32[]{:S(2)}, u32[]{:S(2)}) collective-permute-start(bf16[2,48,256]{2,1,0:T(8,128)(2,1)S(1)} %get-tuple-element.58), channel_id=1, source_target_pairs={{0,32},{32,64},{64,96},{96,128},{128,160},{160,192},{192,224},{224... | collective-permute-start | bytes 147464 | tf_op jit(solution)/shard_map/ppermute | solution.py:405
  49.4 4.1 %collective-permute-start.15 = (bf16[2,48,256]{2,1,0:T(8,128)(2,1)S(1)}, bf16[2,48,256]{2,1,0:T(8,128)(2,1)S(1)}, u32[]{:S(2)}, u32[]{:S(2)}) collective-permute-start(bf16[2,48,256]{2,1,0:T(8,128)(2,1)S(1)} %get-tuple-element.59), channel_id=1, source_target_pairs={{0,224},{32,0},{64,32},{96,64},{128,96},{160,128},{192,160},{224,1... | collective-permute-start | bytes 147464 | tf_op jit(solution)/shard_map/ppermute | solution.py:404
  57.1 2.0 %collective-permute-start.16 = (bf16[2,128,1024]{2,1,0:T(8,128)(2,1)S(1)}, bf16[2,128,1024]{2,1,0:T(8,128)(2,1)S(1)}, u32[]{:S(2)}, u32[]{:S(2)}) collective-permute-start(bf16[2,128,1024]{2,1,0:T(8,128)(2,1)S(1)} %get-tuple-element.61), channel_id=1, source_target_pairs={{0,1},{1,0},{2,3},{3,2},{4,5},{5,4},{6,7},{7,6},{8,9},{9,8},{10,11... | collective-permute-start | bytes 1572872 | tf_op jit(solution)/shard_map/ppermute | solution.py:420
  59.2 23.3 %collective-permute-start.17 = (bf16[128,1024]{1,0:T(8,128)(2,1)S(1)}, bf16[128,1024]{1,0:T(8,128)(2,1)S(1)}, u32[]{:S(2)}, u32[]{:S(2)}) collective-permute-start(bf16[128,1024]{1,0:T(8,128)(2,1)S(1)} %get-tuple-element.63), channel_id=1, source_target_pairs={{0,2},{2,0},{1,3},{3,1},{4,6},{6,4},{5,7},{7,5},{8,10},{10,8},{9,1... | collective-permute-start | bytes 786440 | tf_op jit(solution)/shard_map/ppermute | solution.py:422
  76.1 18.0 %all-to-all-start.1 = ((bf16[8,16,1024]{2,1,0:T(8,128)(2,1)}), bf16[8,16,1024]{2,1,0:T(8,128)(2,1)S(1)}, u32[]{:S(2)}, u32[]{:S(2)}) async-start(bf16[8,16,1024]{2,1,0:T(8,128)(2,1)} %shard_map.103), calls=%async_computation.1 | async-start | bytes 524288 | tf_op jit(solution)/shard_map/all_to_all | solution.py:426

commit v4 on v3

--- a/solution.py
+++ b/solution.py
@@ -21,6 +21,7 @@
 EDGE = DEPTH * TW
 SLOTS = 4
 BAND = 40 * SLOTS
+SENT = 128
 BLOCKS = 4
 BLK = TOKENS // BLOCKS
 BLK_ROWS = TH // BLOCKS
@@ -76,12 +77,21 @@
 
 
 def pick(first_col, token_axis):
-    shape = (CENTER, BAND) if token_axis == 0 else (BAND, CENTER)
+    shape = (CENTER, SENT) if token_axis == 0 else (SENT, CENTER)
     token = lax.broadcasted_iota(jnp.int32, shape, token_axis)
-    slot = lax.broadcasted_iota(jnp.int32, shape, 1 - token_axis)
+    sent = lax.broadcasted_iota(jnp.int32, shape, 1 - token_axis)
+    row = (sent * 171) >> 9
+    wanted = row * TW + first_col + sent - DEPTH * row
+    return jnp.where((token == wanted) & (row < PAD_H), 1.0, 0.0).astype(BF16)
+
+
+def spread(band_axis):
+    shape = (BAND, SENT) if band_axis == 0 else (SENT, BAND)
+    slot = lax.broadcasted_iota(jnp.int32, shape, band_axis)
+    sent = lax.broadcasted_iota(jnp.int32, shape, 1 - band_axis)
     lane = slot & (SLOTS - 1)
-    wanted = (slot // SLOTS) * TW + first_col + lane
-    return jnp.where((token == wanted) & (lane < DEPTH), 1.0, 0.0).astype(BF16)
+    wanted = (slot // SLOTS) * DEPTH + lane
+    return jnp.where((sent == wanted) & (lane < DEPTH) & (slot < PAD_H * SLOTS), 1.0, 0.0).astype(BF16)
 
 
 def copy_all(pairs, sems):
@@ -132,9 +142,9 @@
 
 
 def attention_kernel(
-    q, og0, og1, og2, og3, w_out, mid, from_left, from_right,
+    q, og0, og1, og2, og3, w_out, mid, sent_left, sent_right,
     attn_out, grad_q, grad_mid, band_left, band_right,
-    ga, gl, gr,
+    ga, gl, gr, from_left, from_right,
 ):
     head = head_index()
     tile_row = lax.axis_index("z")
@@ -142,6 +152,10 @@
     for i, piece in enumerate((og0, og1, og2, og3)):
         at = pl.multiple_of((head ^ i) * BLK, BLK)
         ga[pl.ds(at, BLK), :] = dot(piece[...], w_out[...], 1, 1).astype(BF16)
+    spreading = spread(0)
+    for i in range(2):
+        from_left[i] = dot(spreading, sent_left[i], 1, 0).astype(BF16)
+        from_right[i] = dot(spreading, sent_right[i], 1, 0).astype(BF16)
     grad_mid[...] = jnp.zeros_like(grad_mid)
     gl[...] = jnp.zeros_like(gl)
     gr[...] = jnp.zeros_like(gr)
@@ -190,8 +204,10 @@
             grad_mid[i, m_rows] += g[:K_MID]
             gl[i, b_rows] += g[K_MID : K_MID + K_BAND]
             gr[i, b_rows] += g[K_MID + K_BAND :]
-    band_left[...] = gl[...].astype(BF16)
-    band_right[...] = gr[...].astype(BF16)
+    joining = spread(1)
+    for i in range(2):
+        band_left[i] = dot(joining, gl[i].astype(BF16), 1, 0).astype(BF16)
+        band_right[i] = dot(joining, gr[i].astype(BF16), 1, 0).astype(BF16)
 
 
 def put_term(out, term):
@@ -324,7 +340,7 @@
 
     flat = shaped((TOKENS, FEAT))
     edge = shaped((2, EDGE, FEAT))
-    band = shaped((2, BAND, FEAT))
+    band = shaped((2, SENT, FEAT))
     mids = shaped((2, CENTER, FEAT))
     own = shaped((BLK, D))
     own_grad = out_grad.reshape(BLK, D)
@@ -343,15 +359,16 @@
         flops=10_000_000_000,
     )(to_above, q, k, v, w_out, own_grad, own_hidden)
     g2 = lax.ppermute(own_grad, "yl", SWAP)
-    g1 = lax.ppermute(own_grad, "core", SWAP)
-    h2 = lax.ppermute(h0, "yl", SWAP)
-    h1 = lax.ppermute(h0, "core", SWAP)
+    late, _ = lax.optimization_barrier((own_hidden, below))
+    h2 = lax.ppermute(late, "yl", SWAP)
 
     mid, to_left, to_right = call(bands_kernel, (mids, band, band), n_in=3)(kv, above, below)
     from_right = lax.ppermute(to_left, COLS, columns(-1))
     from_left = lax.ppermute(to_right, COLS, columns(1))
     g2, _ = lax.optimization_barrier((g2, to_left))
     g3 = lax.ppermute(g2, "core", SWAP)
+    g1 = lax.ppermute(g0, "core", SWAP)
+    h1 = lax.ppermute(h0, "core", SWAP)
     h2, _, _ = lax.optimization_barrier((h2, from_left, from_right))
     h3 = lax.ppermute(h2, "core", SWAP)
 
@@ -362,6 +379,8 @@
             pltpu.VMEM((TOKENS, FEAT), BF16),
             pltpu.VMEM((2, BAND, FEAT), F32),
             pltpu.VMEM((2, BAND, FEAT), F32),
+            pltpu.VMEM((2, BAND, FEAT), BF16),
+            pltpu.VMEM((2, BAND, FEAT), BF16),
         ],
         n_in=9,
     )(q, g0, g1, g2, g3, w_out, mid, from_left, from_right)

time: 95.2 us -> 93.7 us (0.984)
  starting transfers between devices: 39.5 us -> 32.6 us
  waiting for transfers between devices: 36 us -> 41.1 us
    ppermute x2, waiting for transfers between devices: 0.01 us -> 3.53 us  [the longest x1 3.53 us: per_device(): h2 = lax.ppermute(late, 'yl', SWAP)]
    all_to_all x1, starting transfers between devices: 7.24 us -> 4.92 us  [per_device(): terms = lax.all_to_all(terms, YX, 0, 0, tiled=True)]
    ppermute x1, starting transfers between devices: 2.2 us -> 0.01 us  [per_device(): got_above = lax.ppermute(to_below, 'z', ring(Z, 1))]
    ppermute x1, starting transfers between devices: 1.12 us -> 3.23 us  [per_device(): got_below = lax.ppermute(to_above, 'z', ring(Z, -1))]
    all_to_all x1, waiting for transfers between devices: 14.6 us -> 16.6 us  [per_device(): terms = lax.all_to_all(terms, YX, 0, 0, tiled=True)]
    all_to_all x1, starting transfers between devices: 6.39 us -> 4.35 us  [per_device(): parts = lax.all_to_all(parts, 'z', 0, 0, tiled=True)]
    ppermute x1, starting transfers between devices: 3.94 us -> 5.93 us  [per_device(): below = lax.ppermute(to_above, 'z', ring(Z, -1))]
    ppermute x1, starting transfers between devices: 2.27 us -> 0.45 us  [per_device(): g2 = lax.ppermute(own_grad, 'yl', SWAP)]
  transfers between devices with their start and end apart: 20 -> 20, of which waited for: 8 -> 9; matrix products, arithmetic and copies ran while one was open for 1% -> 1% of each run, Pallas kernels for 15% -> 15%
where the time goes in v4:
time: 93.7 us; the launch traced here: 93.3 us
  waiting for transfers between devices  41.1 us (44%)
  starting transfers between devices  32.6 us (35%)
  Pallas kernels  18.1 us (19%)
    pallas_call x11, Pallas kernels, on(): run(*(hold(a, pltpu.HBM) if i in hbm else a for i, a in enumerate(args)))  18.1 us
    all_to_all x1, waiting for transfers between devices, per_device(): terms = lax.all_to_all(terms, YX, 0, 0, tiled=True)  16.6 us
    all_to_all x1, waiting for transfers between devices, per_device(): parts = lax.all_to_all(parts, 'z', 0, 0, tiled=True)  10.9 us
    ppermute x1, starting transfers between devices, per_device(): below = lax.ppermute(to_above, 'z', ring(Z, -1))  5.93 us
    all_to_all x1, starting transfers between devices, per_device(): terms = lax.all_to_all(terms, YX, 0, 0, tiled=True)  4.92 us
    all_to_all x1, starting transfers between devices, per_device(): parts = lax.all_to_all(parts, 'z', 0, 0, tiled=True)  4.35 us
    ppermute x1, starting transfers between devices, per_device(): got_right = lax.ppermute(band_left, COLS, columns(-1))  4.12 us
    ppermute x1, waiting for transfers between devices, per_device(): h2 = lax.ppermute(late, 'yl', SWAP)  3.53 us
  transfers between devices with their start and end apart: 20, of which 9 were waited for; matrix products, arithmetic and copies ran while one was open for 1% of the time, Pallas kernels for 15%

profile of v4, /device:TPU:8, one launch (start us, length us, event | category | flops | bytes accessed | tf_op | source)
XLA Modules:
  0.0 93.3 jit_solution(7911993198446236397)
XLA Ops:
  0.6 0.8 shard_map.94
  1.5 5.9 %collective-permute-start.3 = (bf16[2,48,256]{2,1,0:T(8,128)(2,1)S(1)}, bf16[2,48,256]{2,1,0:T(8,128)(2,1)S(1)}, u32[]{:S(2)}, u32[]{:S(2)}) collective-permute-start(bf16[2,48,256]{2,1,0:T(8,128)(2,1)S(1)} %get-tuple-element.36.after), channel_id=1, source_target_pairs={{0,224},{32,0},{64,32},{96,64},{128,96},{160,128},{192,160},{224,1... | collective-permute-start | bytes 147464 | tf_op jit(solution)/shard_map/ppermute | solution.py:351
  7.9 1.3 %collective-permute-done.3.below = bf16[2,48,256]{2,1,0:T(8,128)(2,1)S(1)} collective-permute-done((bf16[2,48,256]{2,1,0:T(8,128)(2,1)S(1)}, bf16[2,48,256]{2,1,0:T(8,128)(2,1)S(1)}, u32[]{:S(2)}, u32[]{:S(2)}) %collective-permute-start.3) | collective-permute-done | bytes 49184 | tf_op jit(solution)/shard_map/ppermute | solution.py:351
  9.6 1.5 %shard_map.95 = (bf16[512,256]{1,0:T(8,128)(2,1)S(1)}, bf16[2,512,256]{2,1,0:T(8,128)(2,1)S(1)}, bf16[256,1024]{1,0:T(8,128)(2,1)S(1)}, bf16[128,1024]{1,0:T(8,128)(2,1)S(1)}, bf16[128,1024]{1,0:T(8,128)(2,1)S(1)}) custom-call(bf16[2,48,256]{2,1,0:T(8,128)(2,1)S(1)} %get-tuple-element.36.after, bf16[512,256]{1,0:T(8,128)(2,1)} %bitcast.15, ...), custom_call_target="tpu_custom_call" | custom-call | flops 10000000000 | tf_op jit(solution)/shard_map/pallas_call | solution.py:66
  11.1 1.6 %collective-permute-done.2.above = bf16[2,48,256]{2,1,0:T(8,128)(2,1)S(1)} collective-permute-done((bf16[2,48,256]{2,1,0:T(8,128)(2,1)S(1)}, bf16[2,48,256]{2,1,0:T(8,128)(2,1)S(1)}, u32[]{:S(2)}, u32[]{:S(2)}) %collective-permute-start.2) | collective-permute-done | bytes 49184 | tf_op jit(solution)/shard_map/ppermute | solution.py:352
  13.1 1.6 %collective-permute-start.5 = (bf16[2,128,256]{2,1,0:T(8,128)(2,1)S(1)}, bf16[2,128,256]{2,1,0:T(8,128)(2,1)S(1)}, u32[]{:S(2)}, u32[]{:S(2)}) collective-permute-start(bf16[2,128,256]{2,1,0:T(8,128)(2,1)S(1)} %get-tuple-element.45), channel_id=1, source_target_pairs={{0,4},{2,6},{4,8},{6,10},{8,12},{10,14},{12,16},{14,18},{16,20},{1... | collective-permute-start | bytes 393224 | tf_op jit(solution)/shard_map/ppermute | solution.py:367
  14.7 2.6 %collective-permute-start.6 = (bf16[2,128,256]{2,1,0:T(8,128)(2,1)S(1)}, bf16[2,128,256]{2,1,0:T(8,128)(2,1)S(1)}, u32[]{:S(2)}, u32[]{:S(2)}) collective-permute-start(bf16[2,128,256]{2,1,0:T(8,128)(2,1)S(1)} %get-tuple-element.41), channel_id=1, source_target_pairs={{0,30},{2,28},{4,0},{6,2},{8,4},{10,6},{12,8},{14,10},{16,12},{18,... | collective-permute-start | bytes 393224 | tf_op jit(solution)/shard_map/ppermute | solution.py:366
  17.8 2.4 %collective-permute-done.5.sent_left = bf16[2,128,256]{2,1,0:T(8,128)(2,1)S(1)} collective-permute-done((bf16[2,128,256]{2,1,0:T(8,128)(2,1)S(1)}, bf16[2,128,256]{2,1,0:T(8,128)(2,1)S(1)}, u32[]{:S(2)}, u32[]{:S(2)}) %collective-permute-start.5) | collective-permute-done | bytes 131104 | tf_op jit(solution)/shard_map/ppermute | solution.py:367
  20.3 3.5 %collective-permute-done.10.h2 = bf16[128,1024]{1,0:T(8,128)(2,1)S(1)} collective-permute-done((bf16[128,1024]{1,0:T(8,128)(2,1)}, bf16[128,1024]{1,0:T(8,128)(2,1)S(1)}, u32[]{:S(2)}, u32[]{:S(2)}) %collective-permute-start.10) | collective-permute-done | bytes 262176 | tf_op jit(solution)/shard_map/ppermute | solution.py:363
  23.8 5.6 %shard_map.97 = (bf16[512,256]{1,0:T(8,128)(2,1)S(1)}, bf16[512,256]{1,0:T(8,128)(2,1)S(1)}, f32[2,608,256]{2,1,0:T(8,128)S(1)}, bf16[2,128,256]{2,1,0:T(8,128)(2,1)S(1)}, bf16[2,128,256]{2,1,0:T(8,128)(2,1)S(1)}) custom-call(bf16[512,256]{1,0:T(8,128)(2,1)S(1)} %get-tuple-element.37.q, bf16[128,1024]{1,0:T(8,128)(2,1)S(1)} %get-tuple-element.38.og0.g0, ...), custom_call_target="tpu_custom_call" | custom-call | tf_op jit(solution)/shard_map/pallas_call | solution.py:66
  29.7 4.1 %collective-permute-start.8 = (bf16[2,128,256]{2,1,0:T(8,128)(2,1)S(1)}, bf16[2,128,256]{2,1,0:T(8,128)(2,1)S(1)}, u32[]{:S(2)}, u32[]{:S(2)}) collective-permute-start(bf16[2,128,256]{2,1,0:T(8,128)(2,1)S(1)} %get-tuple-element.49.after), channel_id=1, source_target_pairs={{0,30},{2,28},{4,0},{6,2},{8,4},{10,6},{12,8},{14,10},{16,12},{18,... | collective-permute-start | bytes 393224 | tf_op jit(solution)/shard_map/ppermute | solution.py:388
  34.1 3.2 %collective-permute-start.13 = (bf16[48,1024]{1,0:T(8,128)(2,1)S(1)}, bf16[48,1024]{1,0:T(8,128)(2,1)S(1)}, u32[]{:S(2)}, u32[]{:S(2)}) collective-permute-start(bf16[48,1024]{1,0:T(8,128)(2,1)S(1)} %get-tuple-element.55), channel_id=1, source_target_pairs={{0,224},{32,0},{64,32},{96,64},{128,96},{160,128},{192,160},{224,1... | collective-permute-start | bytes 294920 | tf_op jit(solution)/shard_map/ppermute | solution.py:394
  37.3 1.8 %shard_map.99.first = bf16[8,4,8,16,256]{4,3,2,1,0:T(8,128)(2,1)} custom-call(bf16[512,256]{1,0:T(8,128)(2,1)S(1)} %get-tuple-element.46.grad_q, bf16[512,256]{1,0:T(8,128)(2,1)S(1)} %get-tuple-element.56.attn, bf16[128,1024]{1,0:T(8,128)(2,1)S(1)} %get-tuple-element.38.og0.g0, bf16[128,1024]{1,0:T(8,128)(2,1)S(1)} %collective-permute-done.og1.g1, ...), custom_call_target="tpu_custom_call" | custom-call | flops 10000000000 | tf_op jit(solution)/shard_map/pallas_call | solution.py:66
  39.1 0.8 collective-permute-done.12.hid_above
  39.9 2.5 %shard_map.100 = (bf16[8,4,8,16,256]{4,3,2,1,0:T(8,128)(2,1)}, bf16[2,512,256]{2,1,0:T(8,128)(2,1)S(1)}, f32[2,48,256]{2,1,0:T(8,128)S(1)}, f32[2,48,256]{2,1,0:...) custom-call(f32[2,608,256]{2,1,0:T(8,128)S(1)} %get-tuple-element.47, ...), custom_call_target="tpu_custom_call", output_to_operand_aliasing={{0}: (6, {})} | custom-call | tf_op jit(solution)/shard_map/pallas_call | solution.py:66
  42.4 4.9 %all-to-all-start = ((bf16[8,4,8,16,256]{4,3,2,1,0:T(8,128)(2,1)}), bf16[8,4,8,16,256]{4,3,2,1,0:T(8,128)(2,1)S(1)}, u32[]{:S(2)}, u32[]{:S(2)}) async-start(bf16[8,4,8,16,256]{4,3,2,1,0:T(8,128)(2,1)} %get-tuple-element.66), calls=%async_computation | async-start | bytes 4194304 | tf_op jit(solution)/shard_map/all_to_all | solution.py:425
  47.3 3.2 %collective-permute-start.15 = (bf16[2,48,256]{2,1,0:T(8,128)(2,1)S(1)}, bf16[2,48,256]{2,1,0:T(8,128)(2,1)S(1)}, u32[]{:S(2)}, u32[]{:S(2)}) collective-permute-start(bf16[2,48,256]{2,1,0:T(8,128)(2,1)S(1)} %get-tuple-element.61), channel_id=1, source_target_pairs={{0,224},{32,0},{64,32},{96,64},{128,96},{160,128},{192,160},{224,1... | collective-permute-start | bytes 147464 | tf_op jit(solution)/shard_map/ppermute | solution.py:423
  50.5 2.1 %collective-permute-done.14.from_above = bf16[2,48,256]{2,1,0:T(8,128)(2,1)S(1)} collective-permute-done((bf16[2,48,256]{2,1,0:T(8,128)(2,1)S(1)}, bf16[2,48,256]{2,1,0:T(8,128)(2,1)S(1)}, u32[]{:S(2)}, u32[]{:S(2)}) %collective-permute-start.14) | collective-permute-done | bytes 49184 | tf_op jit(solution)/shard_map/ppermute | solution.py:424
  52.6 3.6 %shard_map.101 = (bf16[2,128,1024]{2,1,0:T(8,128)(2,1)S(1)}, bf16[2,128,1024]{2,1,0:T(8,128)(2,1)S(1)}) custom-call(bf16[512,256]{1,0:T(8,128)(2,1)S(1)} %get-tuple-element.46.grad_q, bf16[2,512,256]{2,1,0:T(8,128)(2,1)S(1)} %get-tuple-element.57.inner, f32[2,48,256]{2,1,0:T(8,128)S(1)} %get-tuple-element.58.top, ...), custom_call_target="tpu_custom_call" | custom-call | tf_op jit(solution)/shard_map/pallas_call | solution.py:66
  56.3 1.9 %collective-permute-done.16.got = bf16[2,128,1024]{2,1,0:T(8,128)(2,1)S(1)} collective-permute-done((bf16[2,128,1024]{2,1,0:T(8,128)(2,1)S(1)}, bf16[2,128,1024]{2,1,0:T(8,128)(2,1)S(1)}, u32[]{:S(2)}, u32[]{:S(2)}) %collective-permute-start.16) | collective-permute-done | bytes 524320 | tf_op jit(solution)/shard_map/ppermute | solution.py:439
  59.1 16.6 %all-to-all-done.terms = bf16[8,4,8,16,256]{4,3,2,1,0:T(8,128)(2,1)S(1)} async-done(((bf16[8,4,8,16,256]{4,3,2,1,0:T(8,128)(2,1)}), bf16[8,4,8,16,256]{4,3,2,1,0:T(8,128)(2,1)S(1)}, u32[]{:S(2)}, u32[]{:S(2)}) %all-to-all-start) | async-done | bytes 2097184 | tf_op jit(solution)/shard_map/all_to_all | solution.py:425
  75.7 1.0 %shard_map.103 = bf16[8,16,1024]{2,1,0:T(8,128)(2,1)} custom-call(bf16[8,4,8,16,256]{4,3,2,1,0:T(8,128)(2,1)S(1)} %all-to-all-done.terms), custom_call_target="tpu_custom_call" | custom-call | tf_op jit(solution)/shard_map/pallas_call | solution.py:66
  76.7 4.4 %all-to-all-start.1 = ((bf16[8,16,1024]{2,1,0:T(8,128)(2,1)}), bf16[8,16,1024]{2,1,0:T(8,128)(2,1)S(1)}, u32[]{:S(2)}, u32[]{:S(2)}) async-start(bf16[8,16,1024]{2,1,0:T(8,128)(2,1)} %shard_map.103), calls=%async_computation.1 | async-start | bytes 524288 | tf_op jit(solution)/shard_map/all_to_all | solution.py:445
  81.8 10.9 %all-to-all-done.1.parts = bf16[8,16,1024]{2,1,0:T(8,128)(2,1)S(1)} async-done(((bf16[8,16,1024]{2,1,0:T(8,128)(2,1)}), bf16[8,16,1024]{2,1,0:T(8,128)(2,1)S(1)}, u32[]{:S(2)}, u32[]{:S(2)}) %all-to-all-start.1) | async-done | bytes 262176 | tf_op jit(solution)/shard_map/all_to_all | solution.py:445
  (28 shorter events, 4.7 us)
Async XLA Ops:
  1.5 7.7 %collective-permute-start.3 = (bf16[2,48,256]{2,1,0:T(8,128)(2,1)S(1)}, bf16[2,48,256]{2,1,0:T(8,128)(2,1)S(1)}, u32[]{:S(2)}, u32[]{:S(2)}) collective-permute-start(bf16[2,48,256]{2,1,0:T(8,128)(2,1)S(1)} %get-tuple-element.36.after), channel_id=1, source_target_pairs={{0,224},{32,0},{64,32},{96,64},{128,96},{160,128},{192,160},{224,1... | collective-permute-start | bytes 147464 | tf_op jit(solution)/shard_map/ppermute | solution.py:351
  7.4 5.3 %collective-permute-start.2 = (bf16[2,48,256]{2,1,0:T(8,128)(2,1)S(1)}, bf16[2,48,256]{2,1,0:T(8,128)(2,1)S(1)}, u32[]{:S(2)}, u32[]{:S(2)}) collective-permute-start(bf16[2,48,256]{2,1,0:T(8,128)(2,1)S(1)} %get-tuple-element.40), channel_id=1, source_target_pairs={{0,32},{32,64},{64,96},{96,128},{128,160},{160,192},{192,224},{224... | collective-permute-start | bytes 147464 | tf_op jit(solution)/shard_map/ppermute | solution.py:352
  7.4 9.9 %collective-permute-start.1 = (bf16[128,1024]{1,0:T(8,128)(2,1)}, bf16[128,1024]{1,0:T(8,128)(2,1)S(1)}, u32[]{:S(2)}, u32[]{:S(2)}) collective-permute-start(bf16[128,1024]{1,0:T(8,128)(2,1)} %bitcast.16), channel_id=1, source_target_pairs={{0,2},{2,0},{1,3},{3,1},{4,6},{6,4},{5,7},{7,5},{8,10},{10,8},{9,1... | collective-permute-start | bytes 786440 | tf_op jit(solution)/shard_map/ppermute | solution.py:361
  9.2 14.7 %collective-permute-start.10 = (bf16[128,1024]{1,0:T(8,128)(2,1)}, bf16[128,1024]{1,0:T(8,128)(2,1)S(1)}, u32[]{:S(2)}, u32[]{:S(2)}) collective-permute-start(bf16[128,1024]{1,0:T(8,128)(2,1)} %bitcast.18), channel_id=1, source_target_pairs={{0,2},{2,0},{1,3},{3,1},{4,6},{6,4},{5,7},{7,5},{8,10},{10,8},{9,1... | collective-permute-start | bytes 786440 | tf_op jit(solution)/shard_map/ppermute | solution.py:363
  13.1 7.2 %collective-permute-start.5 = (bf16[2,128,256]{2,1,0:T(8,128)(2,1)S(1)}, bf16[2,128,256]{2,1,0:T(8,128)(2,1)S(1)}, u32[]{:S(2)}, u32[]{:S(2)}) collective-permute-start(bf16[2,128,256]{2,1,0:T(8,128)(2,1)S(1)} %get-tuple-element.45), channel_id=1, source_target_pairs={{0,4},{2,6},{4,8},{6,10},{8,12},{10,14},{12,16},{14,18},{16,20},{1... | collective-permute-start | bytes 393224 | tf_op jit(solution)/shard_map/ppermute | solution.py:367
  14.7 5.6 %collective-permute-start.6 = (bf16[2,128,256]{2,1,0:T(8,128)(2,1)S(1)}, bf16[2,128,256]{2,1,0:T(8,128)(2,1)S(1)}, u32[]{:S(2)}, u32[]{:S(2)}) collective-permute-start(bf16[2,128,256]{2,1,0:T(8,128)(2,1)S(1)} %get-tuple-element.41), channel_id=1, source_target_pairs={{0,30},{2,28},{4,0},{6,2},{8,4},{10,6},{12,8},{14,10},{16,12},{18,... | collective-permute-start | bytes 393224 | tf_op jit(solution)/shard_map/ppermute | solution.py:366
  17.3 6.5 %collective-permute-start = (bf16[128,1024]{1,0:T(8,128)(2,1)S(1)}, bf16[128,1024]{1,0:T(8,128)(2,1)S(1)}, u32[]{:S(2)}, u32[]{:S(2)}) collective-permute-start(bf16[128,1024]{1,0:T(8,128)(2,1)S(1)} %get-tuple-element.38.og0.g0), channel_id=1, source_target_pairs={{0,1},{1,0},{2,3},{3,2},{4,5},{5,4},{6,7},{7,6},{8,9},{9,8},{10,11... | collective-permute-start | bytes 786440 | tf_op jit(solution)/shard_map/ppermute | solution.py:370
  17.3 6.5 %collective-permute-start.4 = (bf16[128,1024]{1,0:T(8,128)(2,1)S(1)}, bf16[128,1024]{1,0:T(8,128)(2,1)S(1)}, u32[]{:S(2)}, u32[]{:S(2)}) collective-permute-start(bf16[128,1024]{1,0:T(8,128)(2,1)S(1)} %collective-permute-done.1.og2.g2), channel_id=1, source_target_pairs={{0,1},{1,0},{2,3},{3,2},{4,5},{5,4},{6,7},{7,6},{8,9},{9,8},{10,11... | collective-permute-start | bytes 786440 | tf_op jit(solution)/shard_map/ppermute | solution.py:369
  20.3 13.6 %collective-permute-start.9 = (bf16[128,1024]{1,0:T(8,128)(2,1)S(1)}, bf16[128,1024]{1,0:T(8,128)(2,1)S(1)}, u32[]{:S(2)}, u32[]{:S(2)}) collective-permute-start(bf16[128,1024]{1,0:T(8,128)(2,1)S(1)} %get-tuple-element.50.h0), channel_id=1, source_target_pairs={{0,1},{1,0},{2,3},{3,2},{4,5},{5,4},{6,7},{7,6},{8,9},{9,8},{10,11... | collective-permute-start | bytes 786440 | tf_op jit(solution)/shard_map/ppermute | solution.py:371
  23.8 10.1 %collective-permute-start.11 = (bf16[128,1024]{1,0:T(8,128)(2,1)S(1)}, bf16[128,1024]{1,0:T(8,128)(2,1)S(1)}, u32[]{:S(2)}, u32[]{:S(2)}) collective-permute-start(bf16[128,1024]{1,0:T(8,128)(2,1)S(1)} %collective-permute-done.10.h2), channel_id=1, source_target_pairs={{0,1},{1,0},{2,3},{3,2},{4,5},{5,4},{6,7},{7,6},{8,9},{9,8},{10,11... | collective-permute-start | bytes 786440 | tf_op jit(solution)/shard_map/ppermute | solution.py:373
  29.5 9.6 %collective-permute-start.7 = (bf16[2,128,256]{2,1,0:T(8,128)(2,1)S(1)}, bf16[2,128,256]{2,1,0:T(8,128)(2,1)S(1)}, u32[]{:S(2)}, u32[]{:S(2)}) collective-permute-start(bf16[2,128,256]{2,1,0:T(8,128)(2,1)S(1)} %get-tuple-element.48), channel_id=1, source_target_pairs={{0,4},{2,6},{4,8},{6,10},{8,12},{10,14},{12,16},{14,18},{16,20},{1... | collective-permute-start | bytes 393224 | tf_op jit(solution)/shard_map/ppermute | solution.py:389
  29.7 9.4 %collective-permute-start.8 = (bf16[2,128,256]{2,1,0:T(8,128)(2,1)S(1)}, bf16[2,128,256]{2,1,0:T(8,128)(2,1)S(1)}, u32[]{:S(2)}, u32[]{:S(2)}) collective-permute-start(bf16[2,128,256]{2,1,0:T(8,128)(2,1)S(1)} %get-tuple-element.49.after), channel_id=1, source_target_pairs={{0,30},{2,28},{4,0},{6,2},{8,4},{10,6},{12,8},{14,10},{16,12},{18,... | collective-permute-start | bytes 393224 | tf_op jit(solution)/shard_map/ppermute | solution.py:388
  34.0 5.9 %collective-permute-start.12 = (bf16[48,1024]{1,0:T(8,128)(2,1)S(1)}, bf16[48,1024]{1,0:T(8,128)(2,1)S(1)}, u32[]{:S(2)}, u32[]{:S(2)}) collective-permute-start(bf16[48,1024]{1,0:T(8,128)(2,1)S(1)} %get-tuple-element.54), channel_id=1, source_target_pairs={{0,32},{32,64},{64,96},{96,128},{128,160},{160,192},{192,224},{224... | collective-permute-start | bytes 294920 | tf_op jit(solution)/shard_map/ppermute | solution.py:395
  34.1 5.8 %collective-permute-start.13 = (bf16[48,1024]{1,0:T(8,128)(2,1)S(1)}, bf16[48,1024]{1,0:T(8,128)(2,1)S(1)}, u32[]{:S(2)}, u32[]{:S(2)}) collective-permute-start(bf16[48,1024]{1,0:T(8,128)(2,1)S(1)} %get-tuple-element.55), channel_id=1, source_target_pairs={{0,224},{32,0},{64,32},{96,64},{128,96},{160,128},{192,160},{224,1... | collective-permute-start | bytes 294920 | tf_op jit(solution)/shard_map/ppermute | solution.py:394
  42.4 33.3 %all-to-all-start = ((bf16[8,4,8,16,256]{4,3,2,1,0:T(8,128)(2,1)}), bf16[8,4,8,16,256]{4,3,2,1,0:T(8,128)(2,1)S(1)}, u32[]{:S(2)}, u32[]{:S(2)}) async-start(bf16[8,4,8,16,256]{4,3,2,1,0:T(8,128)(2,1)} %get-tuple-element.66), calls=%async_computation | async-start | bytes 4194304 | tf_op jit(solution)/shard_map/all_to_all | solution.py:425
  47.3 5.3 %collective-permute-start.14 = (bf16[2,48,256]{2,1,0:T(8,128)(2,1)S(1)}, bf16[2,48,256]{2,1,0:T(8,128)(2,1)S(1)}, u32[]{:S(2)}, u32[]{:S(2)}) collective-permute-start(bf16[2,48,256]{2,1,0:T(8,128)(2,1)S(1)} %get-tuple-element.60), channel_id=1, source_target_pairs={{0,32},{32,64},{64,96},{96,128},{128,160},{160,192},{192,224},{224... | collective-permute-start | bytes 147464 | tf_op jit(solution)/shard_map/ppermute | solution.py:424
  47.3 5.3 %collective-permute-start.15 = (bf16[2,48,256]{2,1,0:T(8,128)(2,1)S(1)}, bf16[2,48,256]{2,1,0:T(8,128)(2,1)S(1)}, u32[]{:S(2)}, u32[]{:S(2)}) collective-permute-start(bf16[2,48,256]{2,1,0:T(8,128)(2,1)S(1)} %get-tuple-element.61), channel_id=1, source_target_pairs={{0,224},{32,0},{64,32},{96,64},{128,96},{160,128},{192,160},{224,1... | collective-permute-start | bytes 147464 | tf_op jit(solution)/shard_map/ppermute | solution.py:423
  56.2 2.0 %collective-permute-start.16 = (bf16[2,128,1024]{2,1,0:T(8,128)(2,1)S(1)}, bf16[2,128,1024]{2,1,0:T(8,128)(2,1)S(1)}, u32[]{:S(2)}, u32[]{:S(2)}) collective-permute-start(bf16[2,128,1024]{2,1,0:T(8,128)(2,1)S(1)} %get-tuple-element.63), channel_id=1, source_target_pairs={{0,1},{1,0},{2,3},{3,2},{4,5},{5,4},{6,7},{7,6},{8,9},{9,8},{10,11... | collective-permute-start | bytes 1572872 | tf_op jit(solution)/shard_map/ppermute | solution.py:439
  58.3 22.7 %collective-permute-start.17 = (bf16[128,1024]{1,0:T(8,128)(2,1)S(1)}, bf16[128,1024]{1,0:T(8,128)(2,1)S(1)}, u32[]{:S(2)}, u32[]{:S(2)}) collective-permute-start(bf16[128,1024]{1,0:T(8,128)(2,1)S(1)} %get-tuple-element.65), channel_id=1, source_target_pairs={{0,2},{2,0},{1,3},{3,1},{4,6},{6,4},{5,7},{7,5},{8,10},{10,8},{9,1... | collective-permute-start | bytes 786440 | tf_op jit(solution)/shard_map/ppermute | solution.py:441
  76.7 16.0 %all-to-all-start.1 = ((bf16[8,16,1024]{2,1,0:T(8,128)(2,1)}), bf16[8,16,1024]{2,1,0:T(8,128)(2,1)S(1)}, u32[]{:S(2)}, u32[]{:S(2)}) async-start(bf16[8,16,1024]{2,1,0:T(8,128)(2,1)} %shard_map.103), calls=%async_computation.1 | async-start | bytes 524288 | tf_op jit(solution)/shard_map/all_to_all | solution.py:445

commit v5 on v4

--- a/solution.py
+++ b/solution.py
@@ -22,11 +22,13 @@
 SLOTS = 4
 BAND = 40 * SLOTS
 SENT = 128
-BLOCKS = 4
+CHUNKS = 4
+PIECE = TOKENS // 4
+BLOCKS = 8
 BLK = TOKENS // BLOCKS
 BLK_ROWS = TH // BLOCKS
 K_MID = (BLK_ROWS + 2 * DEPTH) * TW
-K_BAND = 16 * SLOTS
+K_BAND = 12 * SLOTS
 K_ALL = K_MID + 2 * K_BAND
 Z, YH, X, YL, CORE = 8, 2, 4, 2, 2
 GRID = ("z", "yh", "x")
@@ -141,6 +143,13 @@
     return out
 
 
+def block_of(b):
+    rows = slice(b * BLK, (b + 1) * BLK)
+    m_rows = slice(b * BLK, b * BLK + K_MID)
+    b_rows = slice(b * BLK_ROWS * SLOTS, b * BLK_ROWS * SLOTS + K_BAND)
+    return rows, m_rows, b_rows
+
+
 def attention_kernel(
     q, og0, og1, og2, og3, w_out, mid, sent_left, sent_right,
     attn_out, grad_q, grad_mid, band_left, band_right,
@@ -150,8 +159,8 @@
     tile_row = lax.axis_index("z")
     tile_col = lax.axis_index("yh") * X + lax.axis_index("x")
     for i, piece in enumerate((og0, og1, og2, og3)):
-        at = pl.multiple_of((head ^ i) * BLK, BLK)
-        ga[pl.ds(at, BLK), :] = dot(piece[...], w_out[...], 1, 1).astype(BF16)
+        at = pl.multiple_of((head ^ i) * PIECE, PIECE)
+        ga[pl.ds(at, PIECE), :] = dot(piece[...], w_out[...], 1, 1).astype(BF16)
     spreading = spread(0)
     for i in range(2):
         from_left[i] = dot(spreading, sent_left[i], 1, 0).astype(BF16)
@@ -179,31 +188,47 @@
     near = (row_off >= 0) & (row_off < 7) & (col_off >= 0) & (col_off < 7)
     row_image = tile_row * TH + key_row - DEPTH
 
-    for b in range(BLOCKS):
-        row_here = row_image + b * BLK_ROWS
-        valid = near & (row_here >= 0) & (row_here < IMG_H)
-        bias = jnp.where(valid, 0.0, -jnp.inf).astype(F32)
-        rows = slice(b * BLK, (b + 1) * BLK)
-        m_rows = slice(b * BLK, b * BLK + K_MID)
-        b_rows = slice(b * BLK_ROWS * SLOTS, b * BLK_ROWS * SLOTS + K_BAND)
+    def start(b):
+        rows, m_rows, b_rows = block_of(b)
         kk = jnp.concatenate([mid[0, m_rows], from_left[0, b_rows], from_right[0, b_rows]], axis=0)
         vv = jnp.concatenate([mid[1, m_rows], from_left[1, b_rows], from_right[1, b_rows]], axis=0)
         qs = stacked(q[rows, :] * jnp.asarray(HD**-0.5, BF16))
         gs = stacked(ga[rows, :])
-        s = dot(qs, kk, 1, 1).reshape(HEADS_HERE, BLK, K_ALL) + bias[None]
-        s = s.reshape(HEADS_HERE * BLK, K_ALL)
+        return kk, vv, qs, gs, dot(qs, kk, 1, 1), dot(gs, vv, 1, 1)
+
+    def soften(b, kk, vv, qs, gs, s, dprob):
+        row_here = row_image + b * BLK_ROWS
+        valid = near & (row_here >= 0) & (row_here < IMG_H)
+        bias = jnp.where(valid, 0.0, -jnp.inf).astype(F32)
+        s = (s.reshape(HEADS_HERE, BLK, K_ALL) + bias[None]).reshape(HEADS_HERE * BLK, K_ALL)
         e = jnp.exp(s - jnp.max(s, axis=1, keepdims=True))
         p = e * (1.0 / jnp.sum(e, axis=1, keepdims=True))
-        p16 = p.astype(BF16)
-        attn = dot(p16, vv, 1, 0).astype(BF16)
+        return kk, vv, qs, gs, dprob, p, p.astype(BF16)
+
+    def apply(b, kk, vv, qs, gs, dprob, p, p16):
+        return kk, qs, gs, dprob, p, dot(p16, vv, 1, 0).astype(BF16), dot(p16, gs, 0, 0)
+
+    def finish(b, kk, qs, gs, dprob, p, attn, grad_v):
+        rows, m_rows, b_rows = block_of(b)
         attn_out[rows, :] = unstacked(attn)
         delta = jnp.sum(gs.astype(F32) * attn.astype(F32), axis=1, keepdims=True)
-        ds = (p * (dot(gs, vv, 1, 1) - delta)).astype(BF16)
+        return kk, qs, (p * (dprob - delta)).astype(BF16), grad_v
+
+    def spill(b, kk, qs, ds, grad_v):
+        rows, m_rows, b_rows = block_of(b)
         grad_q[rows, :] = unstacked(dot(ds, kk, 1, 0) * (HD**-0.5)).astype(BF16)
-        for i, g in enumerate((dot(ds, qs, 0, 0), dot(p16, gs, 0, 0))):
+        for i, g in enumerate((dot(ds, qs, 0, 0), grad_v)):
             grad_mid[i, m_rows] += g[:K_MID]
             gl[i, b_rows] += g[K_MID : K_MID + K_BAND]
             gr[i, b_rows] += g[K_MID + K_BAND :]
+
+    stages = (start, soften, apply, finish, spill)
+    held = {b: () for b in range(BLOCKS)}
+    for step in range(BLOCKS + len(stages) - 1):
+        for i, stage in enumerate(stages):
+            if 0 <= step - i < BLOCKS:
+                held[step - i] = stage(step - i, *held[step - i])
+
     joining = spread(1)
     for i in range(2):
         band_left[i] = dot(joining, gl[i].astype(BF16), 1, 0).astype(BF16)
@@ -221,7 +246,7 @@
 def hidden_kernel(after, h0, h1, h2, h3, hidden, to_above, to_below):
     head = head_index()
     for i, piece in enumerate((h0, h1, h2, h3)):
-        hidden[pl.ds(pl.multiple_of((head ^ i) * BLK, BLK), BLK), :] = piece[...]
+        hidden[pl.ds(pl.multiple_of((head ^ i) * PIECE, PIECE), PIECE), :] = piece[...]
     to_above[...] = hidden[:EDGE, :]
     to_below[...] = hidden[TOKENS - EDGE :, :]
 
@@ -229,7 +254,7 @@
 def first_terms_kernel(grad_q, attn, g0, g1, g2, g3, hidden, out, og, terms, sems):
     head = head_index()
     for i, piece in enumerate((g0, g1, g2, g3)):
-        og[pl.ds(pl.multiple_of((head ^ i) * BLK, BLK), BLK), :] = piece[...]
+        og[pl.ds(pl.multiple_of((head ^ i) * PIECE, PIECE), PIECE), :] = piece[...]
     copies = []
     for i, (left, right) in enumerate(((hidden, grad_q), (og, attn))):
         put_term(terms.at[i], dot(left[...], right[...], 0, 0))
@@ -249,18 +274,35 @@
     hid_mid[EDGE + TOKENS :] = hid_below[...]
     left = pick(0, 0)
     right = pick(TW - DEPTH, 0)
-    copies = []
+    both = []
     for i in range(2):
         g = grad_mid[i] + dot(left, from_left[i], 1, 0) + dot(right, from_right[i], 1, 0)
-        g16 = g.astype(BF16)
-        put_term(terms.at[i], dot(hid_mid[...], g16, 0, 0))
-        copies.append(pltpu.make_async_copy(terms.at[i], out.at[:, 2 + i], sems.at[i]))
-        copies[-1].start()
-        to_above[i] = g16[:EDGE]
-        grads[i] = g16[EDGE : EDGE + TOKENS]
+        both.append(g.astype(BF16))
+        to_above[i] = both[i][:EDGE]
+        grads[i] = both[i][EDGE : EDGE + TOKENS]
         top[i] = g[EDGE : 2 * EDGE]
         bottom[i] = g[TOKENS : TOKENS + EDGE]
-        to_below[i] = g16[EDGE + TOKENS :]
+        to_below[i] = both[i][EDGE + TOKENS :]
+    both = jnp.concatenate(both, axis=1)
+    copies = []
+    width = D // CHUNKS
+    deep = Z // CHUNKS
+    for c in range(CHUNKS):
+        term = dot(hid_mid[:, c * width : (c + 1) * width], both, 0, 0).astype(BF16)
+        for i in range(2):
+            for yx in range(YH * X):
+                for z in range(deep):
+                    at = (z * YH * X + yx) * 16
+                    here = term[at : at + 16, i * FEAT : (i + 1) * FEAT]
+                    terms[i, yx, c * deep + z] = here
+        part = pl.ds(c * deep, deep)
+        for i in range(2):
+            copies.append(
+                pltpu.make_async_copy(
+                    terms.at[i, :, part], out.at[:, 2 + i, part], sems.at[2 * c + i]
+                )
+            )
+            copies[-1].start()
     for copy in copies:
         copy.wait()
 
@@ -278,7 +320,7 @@
     copy.wait()
     for yl in range(YL):
         for out, c in ((send, 1 - core), (keep, core)):
-            at = pl.ds(pl.multiple_of((yl * CORE + c) * BLK, BLK), BLK)
+            at = pl.ds(pl.multiple_of((yl * CORE + c) * PIECE, PIECE), PIECE)
             total = dot(grad_q[at, :], w_qkv[0], 1, 1)
             for j in range(2):
                 total += dot(grads[j, at, :], w_qkv[1 + j], 1, 1)
@@ -342,9 +384,9 @@
     edge = shaped((2, EDGE, FEAT))
     band = shaped((2, SENT, FEAT))
     mids = shaped((2, CENTER, FEAT))
-    own = shaped((BLK, D))
-    own_grad = out_grad.reshape(BLK, D)
-    own_hidden = hidden_in.reshape(BLK, D)
+    own = shaped((PIECE, D))
+    own_grad = out_grad.reshape(PIECE, D)
+    own_hidden = hidden_in.reshape(PIECE, D)
     to_above, to_below = call(
         edges_kernel, (edge, edge), scratch=[pltpu.SemaphoreType.DMA((4,))], n_in=2, hbm=(0, 1)
     )(k, v)
@@ -413,7 +455,7 @@
         scratch=[
             pltpu.VMEM((CENTER, D), BF16),
             pltpu.VMEM((2, YH * X, Z, 16, FEAT), BF16),
-            pltpu.SemaphoreType.DMA((2,)),
+            pltpu.SemaphoreType.DMA((2 * CHUNKS,)),
         ],
         n_in=7,
         hbm=(6,),
@@ -424,7 +466,7 @@
     got_above = lax.ppermute(to_below, "z", ring(Z, 1))
     terms = lax.all_to_all(terms, YX, 0, 0, tiled=True)
 
-    half = shaped((YL, BLK, D))
+    half = shaped((YL, PIECE, D))
     keep, send = call(
         hidden_grad_kernel,
         (half, half),
@@ -437,7 +479,7 @@
         hbm=(6,),
     )(grad_q, grads, top, bottom, got_above, got_below, w3)
     got = lax.ppermute(send, "core", SWAP)
-    stay, send = call(halve_kernel, (shaped((BLK, D), F32), shaped((BLK, D))), n_in=2)(keep, got)
+    stay, send = call(halve_kernel, (shaped((PIECE, D), F32), shaped((PIECE, D))), n_in=2)(keep, got)
     got = lax.ppermute(send, "yl", SWAP)
     grad_hidden = (stay + got.astype(F32)).astype(BF16).reshape(1, 8, TW, D)
 

time: 93.7 us -> 91.1 us (0.972)
  Pallas kernels: 18.1 us -> 15.7 us
    pallas_call x11, Pallas kernels: 18.1 us -> 15.7 us  [on(): run(*(hold(a, pltpu.HBM) if i in hbm else a for i, a in enumerate(args)))]
  transfers between devices with their start and end apart: 20 -> 20, of which waited for: 9 -> 9; matrix products, arithmetic and copies ran while one was open for 1% -> 1% of each run, Pallas kernels for 15% -> 13%
where the time goes in v5:
time: 91.1 us; the launch traced here: 90.8 us
  waiting for transfers between devices  40.9 us (45%)
  starting transfers between devices  32.6 us (36%)
  Pallas kernels  15.7 us (17%)
    all_to_all x1, waiting for transfers between devices, per_device(): terms = lax.all_to_all(terms, YX, 0, 0, tiled=True)  16.4 us
    pallas_call x11, Pallas kernels, on(): run(*(hold(a, pltpu.HBM) if i in hbm else a for i, a in enumerate(args)))  15.7 us
    all_to_all x1, waiting for transfers between devices, per_device(): parts = lax.all_to_all(parts, 'z', 0, 0, tiled=True)  10.9 us
    ppermute x1, starting transfers between devices, per_device(): below = lax.ppermute(to_above, 'z', ring(Z, -1))  5.93 us
    all_to_all x1, starting transfers between devices, per_device(): terms = lax.all_to_all(terms, YX, 0, 0, tiled=True)  4.74 us
    all_to_all x1, starting transfers between devices, per_device(): parts = lax.all_to_all(parts, 'z', 0, 0, tiled=True)  4.35 us
    ppermute x1, starting transfers between devices, per_device(): got_right = lax.ppermute(band_left, COLS, columns(-1))  4.12 us
    ppermute x1, waiting for transfers between devices, per_device(): h2 = lax.ppermute(late, 'yl', SWAP)  3.53 us
  transfers between devices with their start and end apart: 20, of which 9 were waited for; matrix products, arithmetic and copies ran while one was open for 1% of the time, Pallas kernels for 13%

profile of v5, /device:TPU:8, one launch (start us, length us, event | category | flops | bytes accessed | tf_op | source)
XLA Modules:
  0.0 90.8 jit_solution(11524598489209472236)
XLA Ops:
  0.6 0.8 shard_map.94
  1.5 5.9 %collective-permute-start.3 = (bf16[2,48,256]{2,1,0:T(8,128)(2,1)S(1)}, bf16[2,48,256]{2,1,0:T(8,128)(2,1)S(1)}, u32[]{:S(2)}, u32[]{:S(2)}) collective-permute-start(bf16[2,48,256]{2,1,0:T(8,128)(2,1)S(1)} %get-tuple-element.36.after), channel_id=1, source_target_pairs={{0,224},{32,0},{64,32},{96,64},{128,96},{160,128},{192,160},{224,1... | collective-permute-start | bytes 147464 | tf_op jit(solution)/shard_map/ppermute | solution.py:393
  7.9 1.3 %collective-permute-done.3.below = bf16[2,48,256]{2,1,0:T(8,128)(2,1)S(1)} collective-permute-done((bf16[2,48,256]{2,1,0:T(8,128)(2,1)S(1)}, bf16[2,48,256]{2,1,0:T(8,128)(2,1)S(1)}, u32[]{:S(2)}, u32[]{:S(2)}) %collective-permute-start.3) | collective-permute-done | bytes 49184 | tf_op jit(solution)/shard_map/ppermute | solution.py:393
  9.6 1.5 %shard_map.95 = (bf16[512,256]{1,0:T(8,128)(2,1)S(1)}, bf16[2,512,256]{2,1,0:T(8,128)(2,1)S(1)}, bf16[256,1024]{1,0:T(8,128)(2,1)S(1)}, bf16[128,1024]{1,0:T(8,128)(2,1)S(1)}, bf16[128,1024]{1,0:T(8,128)(2,1)S(1)}) custom-call(bf16[2,48,256]{2,1,0:T(8,128)(2,1)S(1)} %get-tuple-element.36.after, bf16[512,256]{1,0:T(8,128)(2,1)} %bitcast.15, ...), custom_call_target="tpu_custom_call" | custom-call | flops 10000000000 | tf_op jit(solution)/shard_map/pallas_call | solution.py:68
  11.1 1.6 %collective-permute-done.2.above = bf16[2,48,256]{2,1,0:T(8,128)(2,1)S(1)} collective-permute-done((bf16[2,48,256]{2,1,0:T(8,128)(2,1)S(1)}, bf16[2,48,256]{2,1,0:T(8,128)(2,1)S(1)}, u32[]{:S(2)}, u32[]{:S(2)}) %collective-permute-start.2) | collective-permute-done | bytes 49184 | tf_op jit(solution)/shard_map/ppermute | solution.py:394
  13.1 1.6 %collective-permute-start.5 = (bf16[2,128,256]{2,1,0:T(8,128)(2,1)S(1)}, bf16[2,128,256]{2,1,0:T(8,128)(2,1)S(1)}, u32[]{:S(2)}, u32[]{:S(2)}) collective-permute-start(bf16[2,128,256]{2,1,0:T(8,128)(2,1)S(1)} %get-tuple-element.45), channel_id=1, source_target_pairs={{0,4},{2,6},{4,8},{6,10},{8,12},{10,14},{12,16},{14,18},{16,20},{1... | collective-permute-start | bytes 393224 | tf_op jit(solution)/shard_map/ppermute | solution.py:409
  14.7 2.6 %collective-permute-start.6 = (bf16[2,128,256]{2,1,0:T(8,128)(2,1)S(1)}, bf16[2,128,256]{2,1,0:T(8,128)(2,1)S(1)}, u32[]{:S(2)}, u32[]{:S(2)}) collective-permute-start(bf16[2,128,256]{2,1,0:T(8,128)(2,1)S(1)} %get-tuple-element.41), channel_id=1, source_target_pairs={{0,30},{2,28},{4,0},{6,2},{8,4},{10,6},{12,8},{14,10},{16,12},{18,... | collective-permute-start | bytes 393224 | tf_op jit(solution)/shard_map/ppermute | solution.py:408
  17.8 2.4 %collective-permute-done.5.sent_left = bf16[2,128,256]{2,1,0:T(8,128)(2,1)S(1)} collective-permute-done((bf16[2,128,256]{2,1,0:T(8,128)(2,1)S(1)}, bf16[2,128,256]{2,1,0:T(8,128)(2,1)S(1)}, u32[]{:S(2)}, u32[]{:S(2)}) %collective-permute-start.5) | collective-permute-done | bytes 131104 | tf_op jit(solution)/shard_map/ppermute | solution.py:409
  20.3 3.5 %collective-permute-done.10.h2 = bf16[128,1024]{1,0:T(8,128)(2,1)S(1)} collective-permute-done((bf16[128,1024]{1,0:T(8,128)(2,1)}, bf16[128,1024]{1,0:T(8,128)(2,1)S(1)}, u32[]{:S(2)}, u32[]{:S(2)}) %collective-permute-start.10) | collective-permute-done | bytes 262176 | tf_op jit(solution)/shard_map/ppermute | solution.py:405
  23.8 3.6 %shard_map.97 = (bf16[512,256]{1,0:T(8,128)(2,1)S(1)}, bf16[512,256]{1,0:T(8,128)(2,1)S(1)}, f32[2,608,256]{2,1,0:T(8,128)S(1)}, bf16[2,128,256]{2,1,0:T(8,128)(2,1)S(1)}, bf16[2,128,256]{2,1,0:T(8,128)(2,1)S(1)}) custom-call(bf16[512,256]{1,0:T(8,128)(2,1)S(1)} %get-tuple-element.37.q, bf16[128,1024]{1,0:T(8,128)(2,1)S(1)} %get-tuple-element.38.og0.g0, ...), custom_call_target="tpu_custom_call" | custom-call | tf_op jit(solution)/shard_map/pallas_call | solution.py:68
  27.5 4.1 %collective-permute-start.8 = (bf16[2,128,256]{2,1,0:T(8,128)(2,1)S(1)}, bf16[2,128,256]{2,1,0:T(8,128)(2,1)S(1)}, u32[]{:S(2)}, u32[]{:S(2)}) collective-permute-start(bf16[2,128,256]{2,1,0:T(8,128)(2,1)S(1)} %get-tuple-element.49.after), channel_id=1, source_target_pairs={{0,30},{2,28},{4,0},{6,2},{8,4},{10,6},{12,8},{14,10},{16,12},{18,... | collective-permute-start | bytes 393224 | tf_op jit(solution)/shard_map/ppermute | solution.py:430
  32.0 3.2 %collective-permute-start.13 = (bf16[48,1024]{1,0:T(8,128)(2,1)S(1)}, bf16[48,1024]{1,0:T(8,128)(2,1)S(1)}, u32[]{:S(2)}, u32[]{:S(2)}) collective-permute-start(bf16[48,1024]{1,0:T(8,128)(2,1)S(1)} %get-tuple-element.55), channel_id=1, source_target_pairs={{0,224},{32,0},{64,32},{96,64},{128,96},{160,128},{192,160},{224,1... | collective-permute-start | bytes 294920 | tf_op jit(solution)/shard_map/ppermute | solution.py:436
  35.2 1.8 %shard_map.99.first = bf16[8,4,8,16,256]{4,3,2,1,0:T(8,128)(2,1)} custom-call(bf16[512,256]{1,0:T(8,128)(2,1)S(1)} %get-tuple-element.46.grad_q, bf16[512,256]{1,0:T(8,128)(2,1)S(1)} %get-tuple-element.56.attn, bf16[128,1024]{1,0:T(8,128)(2,1)S(1)} %get-tuple-element.38.og0.g0, bf16[128,1024]{1,0:T(8,128)(2,1)S(1)} %collective-permute-done.og1.g1, ...), custom_call_target="tpu_custom_call" | custom-call | flops 10000000000 | tf_op jit(solution)/shard_map/pallas_call | solution.py:68
  37.9 2.1 %shard_map.100 = (bf16[8,4,8,16,256]{4,3,2,1,0:T(8,128)(2,1)}, bf16[2,512,256]{2,1,0:T(8,128)(2,1)S(1)}, f32[2,48,256]{2,1,0:T(8,128)S(1)}, f32[2,48,256]{2,1,0:...) custom-call(f32[2,608,256]{2,1,0:T(8,128)S(1)} %get-tuple-element.47, ...), custom_call_target="tpu_custom_call", output_to_operand_aliasing={{0}: (6, {})} | custom-call | tf_op jit(solution)/shard_map/pallas_call | solution.py:68
  40.0 4.7 %all-to-all-start = ((bf16[8,4,8,16,256]{4,3,2,1,0:T(8,128)(2,1)}), bf16[8,4,8,16,256]{4,3,2,1,0:T(8,128)(2,1)S(1)}, u32[]{:S(2)}, u32[]{:S(2)}) async-start(bf16[8,4,8,16,256]{4,3,2,1,0:T(8,128)(2,1)} %get-tuple-element.66), calls=%async_computation | async-start | bytes 4194304 | tf_op jit(solution)/shard_map/all_to_all | solution.py:467
  44.8 3.2 %collective-permute-start.15 = (bf16[2,48,256]{2,1,0:T(8,128)(2,1)S(1)}, bf16[2,48,256]{2,1,0:T(8,128)(2,1)S(1)}, u32[]{:S(2)}, u32[]{:S(2)}) collective-permute-start(bf16[2,48,256]{2,1,0:T(8,128)(2,1)S(1)} %get-tuple-element.61), channel_id=1, source_target_pairs={{0,224},{32,0},{64,32},{96,64},{128,96},{160,128},{192,160},{224,1... | collective-permute-start | bytes 147464 | tf_op jit(solution)/shard_map/ppermute | solution.py:465
  48.0 2.1 %collective-permute-done.14.from_above = bf16[2,48,256]{2,1,0:T(8,128)(2,1)S(1)} collective-permute-done((bf16[2,48,256]{2,1,0:T(8,128)(2,1)S(1)}, bf16[2,48,256]{2,1,0:T(8,128)(2,1)S(1)}, u32[]{:S(2)}, u32[]{:S(2)}) %collective-permute-start.14) | collective-permute-done | bytes 49184 | tf_op jit(solution)/shard_map/ppermute | solution.py:466
  50.1 3.6 %shard_map.101 = (bf16[2,128,1024]{2,1,0:T(8,128)(2,1)S(1)}, bf16[2,128,1024]{2,1,0:T(8,128)(2,1)S(1)}) custom-call(bf16[512,256]{1,0:T(8,128)(2,1)S(1)} %get-tuple-element.46.grad_q, bf16[2,512,256]{2,1,0:T(8,128)(2,1)S(1)} %get-tuple-element.57.inner, f32[2,48,256]{2,1,0:T(8,128)S(1)} %get-tuple-element.58.top, ...), custom_call_target="tpu_custom_call" | custom-call | tf_op jit(solution)/shard_map/pallas_call | solution.py:68
  53.7 1.9 %collective-permute-done.16.got = bf16[2,128,1024]{2,1,0:T(8,128)(2,1)S(1)} collective-permute-done((bf16[2,128,1024]{2,1,0:T(8,128)(2,1)S(1)}, bf16[2,128,1024]{2,1,0:T(8,128)(2,1)S(1)}, u32[]{:S(2)}, u32[]{:S(2)}) %collective-permute-start.16) | collective-permute-done | bytes 524320 | tf_op jit(solution)/shard_map/ppermute | solution.py:481
  55.7 1.0 %collective-permute-start.17 = (bf16[128,1024]{1,0:T(8,128)(2,1)S(1)}, bf16[128,1024]{1,0:T(8,128)(2,1)S(1)}, u32[]{:S(2)}, u32[]{:S(2)}) collective-permute-start(bf16[128,1024]{1,0:T(8,128)(2,1)S(1)} %get-tuple-element.65), channel_id=1, source_target_pairs={{0,2},{2,0},{1,3},{3,1},{4,6},{6,4},{5,7},{7,5},{8,10},{10,8},{9,1... | collective-permute-start | bytes 786440 | tf_op jit(solution)/shard_map/ppermute | solution.py:483
  56.7 16.4 %all-to-all-done.terms = bf16[8,4,8,16,256]{4,3,2,1,0:T(8,128)(2,1)S(1)} async-done(((bf16[8,4,8,16,256]{4,3,2,1,0:T(8,128)(2,1)}), bf16[8,4,8,16,256]{4,3,2,1,0:T(8,128)(2,1)S(1)}, u32[]{:S(2)}, u32[]{:S(2)}) %all-to-all-start) | async-done | bytes 2097184 | tf_op jit(solution)/shard_map/all_to_all | solution.py:467
  73.1 1.0 %shard_map.103 = bf16[8,16,1024]{2,1,0:T(8,128)(2,1)} custom-call(bf16[8,4,8,16,256]{4,3,2,1,0:T(8,128)(2,1)S(1)} %all-to-all-done.terms), custom_call_target="tpu_custom_call" | custom-call | tf_op jit(solution)/shard_map/pallas_call | solution.py:68
  74.1 4.3 %all-to-all-start.1 = ((bf16[8,16,1024]{2,1,0:T(8,128)(2,1)}), bf16[8,16,1024]{2,1,0:T(8,128)(2,1)S(1)}, u32[]{:S(2)}, u32[]{:S(2)}) async-start(bf16[8,16,1024]{2,1,0:T(8,128)(2,1)} %shard_map.103), calls=%async_computation.1 | async-start | bytes 524288 | tf_op jit(solution)/shard_map/all_to_all | solution.py:487
  79.2 10.9 %all-to-all-done.1.parts = bf16[8,16,1024]{2,1,0:T(8,128)(2,1)S(1)} async-done(((bf16[8,16,1024]{2,1,0:T(8,128)(2,1)}), bf16[8,16,1024]{2,1,0:T(8,128)(2,1)S(1)}, u32[]{:S(2)}, u32[]{:S(2)}) %all-to-all-start.1) | async-done | bytes 262176 | tf_op jit(solution)/shard_map/all_to_all | solution.py:487
  (28 shorter events, 4.7 us)
Async XLA Ops:
  1.5 7.7 %collective-permute-start.3 = (bf16[2,48,256]{2,1,0:T(8,128)(2,1)S(1)}, bf16[2,48,256]{2,1,0:T(8,128)(2,1)S(1)}, u32[]{:S(2)}, u32[]{:S(2)}) collective-permute-start(bf16[2,48,256]{2,1,0:T(8,128)(2,1)S(1)} %get-tuple-element.36.after), channel_id=1, source_target_pairs={{0,224},{32,0},{64,32},{96,64},{128,96},{160,128},{192,160},{224,1... | collective-permute-start | bytes 147464 | tf_op jit(solution)/shard_map/ppermute | solution.py:393
  7.4 5.3 %collective-permute-start.2 = (bf16[2,48,256]{2,1,0:T(8,128)(2,1)S(1)}, bf16[2,48,256]{2,1,0:T(8,128)(2,1)S(1)}, u32[]{:S(2)}, u32[]{:S(2)}) collective-permute-start(bf16[2,48,256]{2,1,0:T(8,128)(2,1)S(1)} %get-tuple-element.40), channel_id=1, source_target_pairs={{0,32},{32,64},{64,96},{96,128},{128,160},{160,192},{192,224},{224... | collective-permute-start | bytes 147464 | tf_op jit(solution)/shard_map/ppermute | solution.py:394
  7.4 9.9 %collective-permute-start.1 = (bf16[128,1024]{1,0:T(8,128)(2,1)}, bf16[128,1024]{1,0:T(8,128)(2,1)S(1)}, u32[]{:S(2)}, u32[]{:S(2)}) collective-permute-start(bf16[128,1024]{1,0:T(8,128)(2,1)} %bitcast.16), channel_id=1, source_target_pairs={{0,2},{2,0},{1,3},{3,1},{4,6},{6,4},{5,7},{7,5},{8,10},{10,8},{9,1... | collective-permute-start | bytes 786440 | tf_op jit(solution)/shard_map/ppermute | solution.py:403
  9.2 14.7 %collective-permute-start.10 = (bf16[128,1024]{1,0:T(8,128)(2,1)}, bf16[128,1024]{1,0:T(8,128)(2,1)S(1)}, u32[]{:S(2)}, u32[]{:S(2)}) collective-permute-start(bf16[128,1024]{1,0:T(8,128)(2,1)} %bitcast.18), channel_id=1, source_target_pairs={{0,2},{2,0},{1,3},{3,1},{4,6},{6,4},{5,7},{7,5},{8,10},{10,8},{9,1... | collective-permute-start | bytes 786440 | tf_op jit(solution)/shard_map/ppermute | solution.py:405
  13.1 7.2 %collective-permute-start.5 = (bf16[2,128,256]{2,1,0:T(8,128)(2,1)S(1)}, bf16[2,128,256]{2,1,0:T(8,128)(2,1)S(1)}, u32[]{:S(2)}, u32[]{:S(2)}) collective-permute-start(bf16[2,128,256]{2,1,0:T(8,128)(2,1)S(1)} %get-tuple-element.45), channel_id=1, source_target_pairs={{0,4},{2,6},{4,8},{6,10},{8,12},{10,14},{12,16},{14,18},{16,20},{1... | collective-permute-start | bytes 393224 | tf_op jit(solution)/shard_map/ppermute | solution.py:409
  14.7 5.6 %collective-permute-start.6 = (bf16[2,128,256]{2,1,0:T(8,128)(2,1)S(1)}, bf16[2,128,256]{2,1,0:T(8,128)(2,1)S(1)}, u32[]{:S(2)}, u32[]{:S(2)}) collective-permute-start(bf16[2,128,256]{2,1,0:T(8,128)(2,1)S(1)} %get-tuple-element.41), channel_id=1, source_target_pairs={{0,30},{2,28},{4,0},{6,2},{8,4},{10,6},{12,8},{14,10},{16,12},{18,... | collective-permute-start | bytes 393224 | tf_op jit(solution)/shard_map/ppermute | solution.py:408
  17.3 6.5 %collective-permute-start = (bf16[128,1024]{1,0:T(8,128)(2,1)S(1)}, bf16[128,1024]{1,0:T(8,128)(2,1)S(1)}, u32[]{:S(2)}, u32[]{:S(2)}) collective-permute-start(bf16[128,1024]{1,0:T(8,128)(2,1)S(1)} %get-tuple-element.38.og0.g0), channel_id=1, source_target_pairs={{0,1},{1,0},{2,3},{3,2},{4,5},{5,4},{6,7},{7,6},{8,9},{9,8},{10,11... | collective-permute-start | bytes 786440 | tf_op jit(solution)/shard_map/ppermute | solution.py:412
  17.3 6.5 %collective-permute-start.4 = (bf16[128,1024]{1,0:T(8,128)(2,1)S(1)}, bf16[128,1024]{1,0:T(8,128)(2,1)S(1)}, u32[]{:S(2)}, u32[]{:S(2)}) collective-permute-start(bf16[128,1024]{1,0:T(8,128)(2,1)S(1)} %collective-permute-done.1.og2.g2), channel_id=1, source_target_pairs={{0,1},{1,0},{2,3},{3,2},{4,5},{5,4},{6,7},{7,6},{8,9},{9,8},{10,11... | collective-permute-start | bytes 786440 | tf_op jit(solution)/shard_map/ppermute | solution.py:411
  20.3 11.4 %collective-permute-start.9 = (bf16[128,1024]{1,0:T(8,128)(2,1)S(1)}, bf16[128,1024]{1,0:T(8,128)(2,1)S(1)}, u32[]{:S(2)}, u32[]{:S(2)}) collective-permute-start(bf16[128,1024]{1,0:T(8,128)(2,1)S(1)} %get-tuple-element.50.h0), channel_id=1, source_target_pairs={{0,1},{1,0},{2,3},{3,2},{4,5},{5,4},{6,7},{7,6},{8,9},{9,8},{10,11... | collective-permute-start | bytes 786440 | tf_op jit(solution)/shard_map/ppermute | solution.py:413
  23.8 7.8 %collective-permute-start.11 = (bf16[128,1024]{1,0:T(8,128)(2,1)S(1)}, bf16[128,1024]{1,0:T(8,128)(2,1)S(1)}, u32[]{:S(2)}, u32[]{:S(2)}) collective-permute-start(bf16[128,1024]{1,0:T(8,128)(2,1)S(1)} %collective-permute-done.10.h2), channel_id=1, source_target_pairs={{0,1},{1,0},{2,3},{3,2},{4,5},{5,4},{6,7},{7,6},{8,9},{9,8},{10,11... | collective-permute-start | bytes 786440 | tf_op jit(solution)/shard_map/ppermute | solution.py:415
  27.4 9.6 %collective-permute-start.7 = (bf16[2,128,256]{2,1,0:T(8,128)(2,1)S(1)}, bf16[2,128,256]{2,1,0:T(8,128)(2,1)S(1)}, u32[]{:S(2)}, u32[]{:S(2)}) collective-permute-start(bf16[2,128,256]{2,1,0:T(8,128)(2,1)S(1)} %get-tuple-element.48), channel_id=1, source_target_pairs={{0,4},{2,6},{4,8},{6,10},{8,12},{10,14},{12,16},{14,18},{16,20},{1... | collective-permute-start | bytes 393224 | tf_op jit(solution)/shard_map/ppermute | solution.py:431
  27.5 9.6 %collective-permute-start.8 = (bf16[2,128,256]{2,1,0:T(8,128)(2,1)S(1)}, bf16[2,128,256]{2,1,0:T(8,128)(2,1)S(1)}, u32[]{:S(2)}, u32[]{:S(2)}) collective-permute-start(bf16[2,128,256]{2,1,0:T(8,128)(2,1)S(1)} %get-tuple-element.49.after), channel_id=1, source_target_pairs={{0,30},{2,28},{4,0},{6,2},{8,4},{10,6},{12,8},{14,10},{16,12},{18,... | collective-permute-start | bytes 393224 | tf_op jit(solution)/shard_map/ppermute | solution.py:430
  31.7 6.1 %collective-permute-start.12 = (bf16[48,1024]{1,0:T(8,128)(2,1)S(1)}, bf16[48,1024]{1,0:T(8,128)(2,1)S(1)}, u32[]{:S(2)}, u32[]{:S(2)}) collective-permute-start(bf16[48,1024]{1,0:T(8,128)(2,1)S(1)} %get-tuple-element.54), channel_id=1, source_target_pairs={{0,32},{32,64},{64,96},{96,128},{128,160},{160,192},{192,224},{224... | collective-permute-start | bytes 294920 | tf_op jit(solution)/shard_map/ppermute | solution.py:437
  32.0 5.8 %collective-permute-start.13 = (bf16[48,1024]{1,0:T(8,128)(2,1)S(1)}, bf16[48,1024]{1,0:T(8,128)(2,1)S(1)}, u32[]{:S(2)}, u32[]{:S(2)}) collective-permute-start(bf16[48,1024]{1,0:T(8,128)(2,1)S(1)} %get-tuple-element.55), channel_id=1, source_target_pairs={{0,224},{32,0},{64,32},{96,64},{128,96},{160,128},{192,160},{224,1... | collective-permute-start | bytes 294920 | tf_op jit(solution)/shard_map/ppermute | solution.py:436
  40.0 33.1 %all-to-all-start = ((bf16[8,4,8,16,256]{4,3,2,1,0:T(8,128)(2,1)}), bf16[8,4,8,16,256]{4,3,2,1,0:T(8,128)(2,1)S(1)}, u32[]{:S(2)}, u32[]{:S(2)}) async-start(bf16[8,4,8,16,256]{4,3,2,1,0:T(8,128)(2,1)} %get-tuple-element.66), calls=%async_computation | async-start | bytes 4194304 | tf_op jit(solution)/shard_map/all_to_all | solution.py:467
  44.8 5.3 %collective-permute-start.14 = (bf16[2,48,256]{2,1,0:T(8,128)(2,1)S(1)}, bf16[2,48,256]{2,1,0:T(8,128)(2,1)S(1)}, u32[]{:S(2)}, u32[]{:S(2)}) collective-permute-start(bf16[2,48,256]{2,1,0:T(8,128)(2,1)S(1)} %get-tuple-element.60), channel_id=1, source_target_pairs={{0,32},{32,64},{64,96},{96,128},{128,160},{160,192},{192,224},{224... | collective-permute-start | bytes 147464 | tf_op jit(solution)/shard_map/ppermute | solution.py:466
  44.8 5.3 %collective-permute-start.15 = (bf16[2,48,256]{2,1,0:T(8,128)(2,1)S(1)}, bf16[2,48,256]{2,1,0:T(8,128)(2,1)S(1)}, u32[]{:S(2)}, u32[]{:S(2)}) collective-permute-start(bf16[2,48,256]{2,1,0:T(8,128)(2,1)S(1)} %get-tuple-element.61), channel_id=1, source_target_pairs={{0,224},{32,0},{64,32},{96,64},{128,96},{160,128},{192,160},{224,1... | collective-permute-start | bytes 147464 | tf_op jit(solution)/shard_map/ppermute | solution.py:465
  53.6 2.0 %collective-permute-start.16 = (bf16[2,128,1024]{2,1,0:T(8,128)(2,1)S(1)}, bf16[2,128,1024]{2,1,0:T(8,128)(2,1)S(1)}, u32[]{:S(2)}, u32[]{:S(2)}) collective-permute-start(bf16[2,128,1024]{2,1,0:T(8,128)(2,1)S(1)} %get-tuple-element.63), channel_id=1, source_target_pairs={{0,1},{1,0},{2,3},{3,2},{4,5},{5,4},{6,7},{7,6},{8,9},{9,8},{10,11... | collective-permute-start | bytes 1572872 | tf_op jit(solution)/shard_map/ppermute | solution.py:481
  55.7 22.7 %collective-permute-start.17 = (bf16[128,1024]{1,0:T(8,128)(2,1)S(1)}, bf16[128,1024]{1,0:T(8,128)(2,1)S(1)}, u32[]{:S(2)}, u32[]{:S(2)}) collective-permute-start(bf16[128,1024]{1,0:T(8,128)(2,1)S(1)} %get-tuple-element.65), channel_id=1, source_target_pairs={{0,2},{2,0},{1,3},{3,1},{4,6},{6,4},{5,7},{7,5},{8,10},{10,8},{9,1... | collective-permute-start | bytes 786440 | tf_op jit(solution)/shard_map/ppermute | solution.py:483
  74.1 16.0 %all-to-all-start.1 = ((bf16[8,16,1024]{2,1,0:T(8,128)(2,1)}), bf16[8,16,1024]{2,1,0:T(8,128)(2,1)S(1)}, u32[]{:S(2)}, u32[]{:S(2)}) async-start(bf16[8,16,1024]{2,1,0:T(8,128)(2,1)} %shard_map.103), calls=%async_computation.1 | async-start | bytes 524288 | tf_op jit(solution)/shard_map/all_to_all | solution.py:487

commit v6 on v5

--- a/solution.py
+++ b/solution.py
@@ -31,8 +31,7 @@
 K_BAND = 12 * SLOTS
 K_ALL = K_MID + 2 * K_BAND
 Z, YH, X, YL, CORE = 8, 2, 4, 2, 2
-GRID = ("z", "yh", "x")
-YX = ("yh", "x")
+GRID = ("z", "yh", "xh", "xl")
 HEAD = ("yl", "core")
 F32 = jnp.float32
 BF16 = jnp.bfloat16
@@ -157,7 +156,7 @@
 ):
     head = head_index()
     tile_row = lax.axis_index("z")
-    tile_col = lax.axis_index("yh") * X + lax.axis_index("x")
+    tile_col = lax.axis_index("yh") * X + lax.axis_index("xh") * 2 + lax.axis_index("xl")
     for i, piece in enumerate((og0, og1, og2, og3)):
         at = pl.multiple_of((head ^ i) * PIECE, PIECE)
         ga[pl.ds(at, PIECE), :] = dot(piece[...], w_out[...], 1, 1).astype(BF16)
@@ -235,12 +234,16 @@
         band_right[i] = dot(joining, gr[i].astype(BF16), 1, 0).astype(BF16)
 
 
+def slot(yx):
+    return (yx // X) * X + (yx % 2) * 2 + (yx % X) // 2
+
+
 def put_term(out, term):
     term = term.astype(BF16)
     for yx in range(YH * X):
         for z in range(Z):
             at = (z * YH * X + yx) * 16
-            out[yx, z] = term[at : at + 16]
+            out[slot(yx), z] = term[at : at + 16]
 
 
 def hidden_kernel(after, h0, h1, h2, h3, hidden, to_above, to_below):
@@ -294,7 +297,7 @@
                 for z in range(deep):
                     at = (z * YH * X + yx) * 16
                     here = term[at : at + 16, i * FEAT : (i + 1) * FEAT]
-                    terms[i, yx, c * deep + z] = here
+                    terms[i, slot(yx), c * deep + z] = here
         part = pl.ds(c * deep, deep)
         for i in range(2):
             copies.append(
@@ -361,7 +364,7 @@
 
 
 SWAP = [(0, 1), (1, 0)]
-COLS = ("yh", "x", "yl")
+COLS = ("yh", "xh", "xl", "yl")
 
 
 def columns(step):
@@ -464,7 +467,7 @@
     )(grad_mid, got_left, got_right, hidden, hid_above, hid_below, terms)
     got_below = lax.ppermute(to_above, "z", ring(Z, -1))
     got_above = lax.ppermute(to_below, "z", ring(Z, 1))
-    terms = lax.all_to_all(terms, YX, 0, 0, tiled=True)
+    terms = lax.all_to_all(terms, ("yh", "xl", "xh"), 0, 0, tiled=True)
 
     half = shaped((YL, PIECE, D))
     keep, send = call(
@@ -492,7 +495,7 @@
 
 
 def solution(mesh):
-    fine = Mesh(mesh.devices.reshape(Z, YH, X, YL, CORE), GRID + HEAD)
+    fine = Mesh(mesh.devices.reshape(Z, YH, 2, 2, YL, CORE), GRID + HEAD)
     return jax.shard_map(
         per_device,
         mesh=fine,

time: 91.1 us -> 91.1 us (level)
  no operation moved by 1% of the time
where the time goes in v6:
time: 91.1 us; the launch traced here: 90.8 us
  waiting for transfers between devices  40.9 us (45%)
  starting transfers between devices  32.6 us (36%)
  Pallas kernels  15.7 us (17%)
    all_to_all x1, waiting for transfers between devices, per_device(): terms = lax.all_to_all(terms, ('yh', 'xl', 'xh'), 0, 0, tiled=True)  16.4 us
    pallas_call x11, Pallas kernels, on(): run(*(hold(a, pltpu.HBM) if i in hbm else a for i, a in enumerate(args)))  15.7 us
    all_to_all x1, waiting for transfers between devices, per_device(): parts = lax.all_to_all(parts, 'z', 0, 0, tiled=True)  10.9 us
    ppermute x1, starting transfers between devices, per_device(): below = lax.ppermute(to_above, 'z', ring(Z, -1))  5.93 us
    all_to_all x1, starting transfers between devices, per_device(): terms = lax.all_to_all(terms, ('yh', 'xl', 'xh'), 0, 0, tiled=True)  4.74 us
    all_to_all x1, starting transfers between devices, per_device(): parts = lax.all_to_all(parts, 'z', 0, 0, tiled=True)  4.35 us
    ppermute x1, starting transfers between devices, per_device(): got_right = lax.ppermute(band_left, COLS, columns(-1))  4.12 us
    ppermute x1, waiting for transfers between devices, per_device(): h2 = lax.ppermute(late, 'yl', SWAP)  3.53 us
  transfers between devices with their start and end apart: 20, of which 9 were waited for; matrix products, arithmetic and copies ran while one was open for 1% of the time, Pallas kernels for 13%

profile of v6, /device:TPU:8, one launch (start us, length us, event | category | flops | bytes accessed | tf_op | source)
XLA Modules:
  0.0 90.8 jit_solution(17524458711275237656)
XLA Ops:
  0.6 0.8 shard_map.94
  1.5 5.9 %collective-permute-start.3 = (bf16[2,48,256]{2,1,0:T(8,128)(2,1)S(1)}, bf16[2,48,256]{2,1,0:T(8,128)(2,1)S(1)}, u32[]{:S(2)}, u32[]{:S(2)}) collective-permute-start(bf16[2,48,256]{2,1,0:T(8,128)(2,1)S(1)} %get-tuple-element.36.after), channel_id=1, source_target_pairs={{0,224},{32,0},{64,32},{96,64},{128,96},{160,128},{192,160},{224,1... | collective-permute-start | bytes 147464 | tf_op jit(solution)/shard_map/ppermute | solution.py:396
  7.9 1.3 %collective-permute-done.3.below = bf16[2,48,256]{2,1,0:T(8,128)(2,1)S(1)} collective-permute-done((bf16[2,48,256]{2,1,0:T(8,128)(2,1)S(1)}, bf16[2,48,256]{2,1,0:T(8,128)(2,1)S(1)}, u32[]{:S(2)}, u32[]{:S(2)}) %collective-permute-start.3) | collective-permute-done | bytes 49184 | tf_op jit(solution)/shard_map/ppermute | solution.py:396
  9.6 1.5 %shard_map.95 = (bf16[512,256]{1,0:T(8,128)(2,1)S(1)}, bf16[2,512,256]{2,1,0:T(8,128)(2,1)S(1)}, bf16[256,1024]{1,0:T(8,128)(2,1)S(1)}, bf16[128,1024]{1,0:T(8,128)(2,1)S(1)}, bf16[128,1024]{1,0:T(8,128)(2,1)S(1)}) custom-call(bf16[2,48,256]{2,1,0:T(8,128)(2,1)S(1)} %get-tuple-element.36.after, bf16[512,256]{1,0:T(8,128)(2,1)} %bitcast.15, ...), custom_call_target="tpu_custom_call" | custom-call | flops 10000000000 | tf_op jit(solution)/shard_map/pallas_call | solution.py:67
  11.1 1.6 %collective-permute-done.2.above = bf16[2,48,256]{2,1,0:T(8,128)(2,1)S(1)} collective-permute-done((bf16[2,48,256]{2,1,0:T(8,128)(2,1)S(1)}, bf16[2,48,256]{2,1,0:T(8,128)(2,1)S(1)}, u32[]{:S(2)}, u32[]{:S(2)}) %collective-permute-start.2) | collective-permute-done | bytes 49184 | tf_op jit(solution)/shard_map/ppermute | solution.py:397
  13.1 1.6 %collective-permute-start.5 = (bf16[2,128,256]{2,1,0:T(8,128)(2,1)S(1)}, bf16[2,128,256]{2,1,0:T(8,128)(2,1)S(1)}, u32[]{:S(2)}, u32[]{:S(2)}) collective-permute-start(bf16[2,128,256]{2,1,0:T(8,128)(2,1)S(1)} %get-tuple-element.45), channel_id=1, source_target_pairs={{0,4},{2,6},{4,8},{6,10},{8,12},{10,14},{12,16},{14,18},{16,20},{1... | collective-permute-start | bytes 393224 | tf_op jit(solution)/shard_map/ppermute | solution.py:412
  14.7 2.6 %collective-permute-start.6 = (bf16[2,128,256]{2,1,0:T(8,128)(2,1)S(1)}, bf16[2,128,256]{2,1,0:T(8,128)(2,1)S(1)}, u32[]{:S(2)}, u32[]{:S(2)}) collective-permute-start(bf16[2,128,256]{2,1,0:T(8,128)(2,1)S(1)} %get-tuple-element.41), channel_id=1, source_target_pairs={{0,30},{2,28},{4,0},{6,2},{8,4},{10,6},{12,8},{14,10},{16,12},{18,... | collective-permute-start | bytes 393224 | tf_op jit(solution)/shard_map/ppermute | solution.py:411
  17.8 2.4 %collective-permute-done.5.sent_left = bf16[2,128,256]{2,1,0:T(8,128)(2,1)S(1)} collective-permute-done((bf16[2,128,256]{2,1,0:T(8,128)(2,1)S(1)}, bf16[2,128,256]{2,1,0:T(8,128)(2,1)S(1)}, u32[]{:S(2)}, u32[]{:S(2)}) %collective-permute-start.5) | collective-permute-done | bytes 131104 | tf_op jit(solution)/shard_map/ppermute | solution.py:412
  20.3 3.5 %collective-permute-done.10.h2 = bf16[128,1024]{1,0:T(8,128)(2,1)S(1)} collective-permute-done((bf16[128,1024]{1,0:T(8,128)(2,1)}, bf16[128,1024]{1,0:T(8,128)(2,1)S(1)}, u32[]{:S(2)}, u32[]{:S(2)}) %collective-permute-start.10) | collective-permute-done | bytes 262176 | tf_op jit(solution)/shard_map/ppermute | solution.py:408
  23.8 3.6 %shard_map.97 = (bf16[512,256]{1,0:T(8,128)(2,1)S(1)}, bf16[512,256]{1,0:T(8,128)(2,1)S(1)}, f32[2,608,256]{2,1,0:T(8,128)S(1)}, bf16[2,128,256]{2,1,0:T(8,128)(2,1)S(1)}, bf16[2,128,256]{2,1,0:T(8,128)(2,1)S(1)}) custom-call(bf16[512,256]{1,0:T(8,128)(2,1)S(1)} %get-tuple-element.37.q, bf16[128,1024]{1,0:T(8,128)(2,1)S(1)} %get-tuple-element.38.og0.g0, ...), custom_call_target="tpu_custom_call" | custom-call | tf_op jit(solution)/shard_map/pallas_call | solution.py:67
  27.5 4.1 %collective-permute-start.8 = (bf16[2,128,256]{2,1,0:T(8,128)(2,1)S(1)}, bf16[2,128,256]{2,1,0:T(8,128)(2,1)S(1)}, u32[]{:S(2)}, u32[]{:S(2)}) collective-permute-start(bf16[2,128,256]{2,1,0:T(8,128)(2,1)S(1)} %get-tuple-element.49.after), channel_id=1, source_target_pairs={{0,30},{2,28},{4,0},{6,2},{8,4},{10,6},{12,8},{14,10},{16,12},{18,... | collective-permute-start | bytes 393224 | tf_op jit(solution)/shard_map/ppermute | solution.py:433
  32.0 3.2 %collective-permute-start.13 = (bf16[48,1024]{1,0:T(8,128)(2,1)S(1)}, bf16[48,1024]{1,0:T(8,128)(2,1)S(1)}, u32[]{:S(2)}, u32[]{:S(2)}) collective-permute-start(bf16[48,1024]{1,0:T(8,128)(2,1)S(1)} %get-tuple-element.55), channel_id=1, source_target_pairs={{0,224},{32,0},{64,32},{96,64},{128,96},{160,128},{192,160},{224,1... | collective-permute-start | bytes 294920 | tf_op jit(solution)/shard_map/ppermute | solution.py:439
  35.2 1.8 %shard_map.99.first = bf16[8,4,8,16,256]{4,3,2,1,0:T(8,128)(2,1)} custom-call(bf16[512,256]{1,0:T(8,128)(2,1)S(1)} %get-tuple-element.46.grad_q, bf16[512,256]{1,0:T(8,128)(2,1)S(1)} %get-tuple-element.56.attn, bf16[128,1024]{1,0:T(8,128)(2,1)S(1)} %get-tuple-element.38.og0.g0, bf16[128,1024]{1,0:T(8,128)(2,1)S(1)} %collective-permute-done.og1.g1, ...), custom_call_target="tpu_custom_call" | custom-call | flops 10000000000 | tf_op jit(solution)/shard_map/pallas_call | solution.py:67
  37.9 2.1 %shard_map.100 = (bf16[8,4,8,16,256]{4,3,2,1,0:T(8,128)(2,1)}, bf16[2,512,256]{2,1,0:T(8,128)(2,1)S(1)}, f32[2,48,256]{2,1,0:T(8,128)S(1)}, f32[2,48,256]{2,1,0:...) custom-call(f32[2,608,256]{2,1,0:T(8,128)S(1)} %get-tuple-element.47, ...), custom_call_target="tpu_custom_call", output_to_operand_aliasing={{0}: (6, {})} | custom-call | tf_op jit(solution)/shard_map/pallas_call | solution.py:67
  40.0 4.7 %all-to-all-start = ((bf16[8,4,8,16,256]{4,3,2,1,0:T(8,128)(2,1)}), bf16[8,4,8,16,256]{4,3,2,1,0:T(8,128)(2,1)S(1)}, u32[]{:S(2)}, u32[]{:S(2)}) async-start(bf16[8,4,8,16,256]{4,3,2,1,0:T(8,128)(2,1)} %get-tuple-element.66), calls=%async_computation | async-start | bytes 4194304 | tf_op jit(solution)/shard_map/all_to_all | solution.py:470
  44.8 3.2 %collective-permute-start.15 = (bf16[2,48,256]{2,1,0:T(8,128)(2,1)S(1)}, bf16[2,48,256]{2,1,0:T(8,128)(2,1)S(1)}, u32[]{:S(2)}, u32[]{:S(2)}) collective-permute-start(bf16[2,48,256]{2,1,0:T(8,128)(2,1)S(1)} %get-tuple-element.61), channel_id=1, source_target_pairs={{0,224},{32,0},{64,32},{96,64},{128,96},{160,128},{192,160},{224,1... | collective-permute-start | bytes 147464 | tf_op jit(solution)/shard_map/ppermute | solution.py:468
  48.0 2.1 %collective-permute-done.14.from_above = bf16[2,48,256]{2,1,0:T(8,128)(2,1)S(1)} collective-permute-done((bf16[2,48,256]{2,1,0:T(8,128)(2,1)S(1)}, bf16[2,48,256]{2,1,0:T(8,128)(2,1)S(1)}, u32[]{:S(2)}, u32[]{:S(2)}) %collective-permute-start.14) | collective-permute-done | bytes 49184 | tf_op jit(solution)/shard_map/ppermute | solution.py:469
  50.1 3.6 %shard_map.101 = (bf16[2,128,1024]{2,1,0:T(8,128)(2,1)S(1)}, bf16[2,128,1024]{2,1,0:T(8,128)(2,1)S(1)}) custom-call(bf16[512,256]{1,0:T(8,128)(2,1)S(1)} %get-tuple-element.46.grad_q, bf16[2,512,256]{2,1,0:T(8,128)(2,1)S(1)} %get-tuple-element.57.inner, f32[2,48,256]{2,1,0:T(8,128)S(1)} %get-tuple-element.58.top, ...), custom_call_target="tpu_custom_call" | custom-call | tf_op jit(solution)/shard_map/pallas_call | solution.py:67
  53.7 1.9 %collective-permute-done.16.got = bf16[2,128,1024]{2,1,0:T(8,128)(2,1)S(1)} collective-permute-done((bf16[2,128,1024]{2,1,0:T(8,128)(2,1)S(1)}, bf16[2,128,1024]{2,1,0:T(8,128)(2,1)S(1)}, u32[]{:S(2)}, u32[]{:S(2)}) %collective-permute-start.16) | collective-permute-done | bytes 524320 | tf_op jit(solution)/shard_map/ppermute | solution.py:484
  55.7 1.0 %collective-permute-start.17 = (bf16[128,1024]{1,0:T(8,128)(2,1)S(1)}, bf16[128,1024]{1,0:T(8,128)(2,1)S(1)}, u32[]{:S(2)}, u32[]{:S(2)}) collective-permute-start(bf16[128,1024]{1,0:T(8,128)(2,1)S(1)} %get-tuple-element.65), channel_id=1, source_target_pairs={{0,2},{2,0},{1,3},{3,1},{4,6},{6,4},{5,7},{7,5},{8,10},{10,8},{9,1... | collective-permute-start | bytes 786440 | tf_op jit(solution)/shard_map/ppermute | solution.py:486
  56.7 16.4 %all-to-all-done.terms = bf16[8,4,8,16,256]{4,3,2,1,0:T(8,128)(2,1)S(1)} async-done(((bf16[8,4,8,16,256]{4,3,2,1,0:T(8,128)(2,1)}), bf16[8,4,8,16,256]{4,3,2,1,0:T(8,128)(2,1)S(1)}, u32[]{:S(2)}, u32[]{:S(2)}) %all-to-all-start) | async-done | bytes 2097184 | tf_op jit(solution)/shard_map/all_to_all | solution.py:470
  73.1 1.0 %shard_map.103 = bf16[8,16,1024]{2,1,0:T(8,128)(2,1)} custom-call(bf16[8,4,8,16,256]{4,3,2,1,0:T(8,128)(2,1)S(1)} %all-to-all-done.terms), custom_call_target="tpu_custom_call" | custom-call | tf_op jit(solution)/shard_map/pallas_call | solution.py:67
  74.1 4.4 %all-to-all-start.1 = ((bf16[8,16,1024]{2,1,0:T(8,128)(2,1)}), bf16[8,16,1024]{2,1,0:T(8,128)(2,1)S(1)}, u32[]{:S(2)}, u32[]{:S(2)}) async-start(bf16[8,16,1024]{2,1,0:T(8,128)(2,1)} %shard_map.103), calls=%async_computation.1 | async-start | bytes 524288 | tf_op jit(solution)/shard_map/all_to_all | solution.py:490
  79.2 10.9 %all-to-all-done.1.parts = bf16[8,16,1024]{2,1,0:T(8,128)(2,1)S(1)} async-done(((bf16[8,16,1024]{2,1,0:T(8,128)(2,1)}), bf16[8,16,1024]{2,1,0:T(8,128)(2,1)S(1)}, u32[]{:S(2)}, u32[]{:S(2)}) %all-to-all-start.1) | async-done | bytes 262176 | tf_op jit(solution)/shard_map/all_to_all | solution.py:490
  (28 shorter events, 4.7 us)
Async XLA Ops:
  1.5 7.7 %collective-permute-start.3 = (bf16[2,48,256]{2,1,0:T(8,128)(2,1)S(1)}, bf16[2,48,256]{2,1,0:T(8,128)(2,1)S(1)}, u32[]{:S(2)}, u32[]{:S(2)}) collective-permute-start(bf16[2,48,256]{2,1,0:T(8,128)(2,1)S(1)} %get-tuple-element.36.after), channel_id=1, source_target_pairs={{0,224},{32,0},{64,32},{96,64},{128,96},{160,128},{192,160},{224,1... | collective-permute-start | bytes 147464 | tf_op jit(solution)/shard_map/ppermute | solution.py:396
  7.4 5.3 %collective-permute-start.2 = (bf16[2,48,256]{2,1,0:T(8,128)(2,1)S(1)}, bf16[2,48,256]{2,1,0:T(8,128)(2,1)S(1)}, u32[]{:S(2)}, u32[]{:S(2)}) collective-permute-start(bf16[2,48,256]{2,1,0:T(8,128)(2,1)S(1)} %get-tuple-element.40), channel_id=1, source_target_pairs={{0,32},{32,64},{64,96},{96,128},{128,160},{160,192},{192,224},{224... | collective-permute-start | bytes 147464 | tf_op jit(solution)/shard_map/ppermute | solution.py:397
  7.4 9.9 %collective-permute-start.1 = (bf16[128,1024]{1,0:T(8,128)(2,1)}, bf16[128,1024]{1,0:T(8,128)(2,1)S(1)}, u32[]{:S(2)}, u32[]{:S(2)}) collective-permute-start(bf16[128,1024]{1,0:T(8,128)(2,1)} %bitcast.16), channel_id=1, source_target_pairs={{0,2},{2,0},{1,3},{3,1},{4,6},{6,4},{5,7},{7,5},{8,10},{10,8},{9,1... | collective-permute-start | bytes 786440 | tf_op jit(solution)/shard_map/ppermute | solution.py:406
  9.2 14.7 %collective-permute-start.10 = (bf16[128,1024]{1,0:T(8,128)(2,1)}, bf16[128,1024]{1,0:T(8,128)(2,1)S(1)}, u32[]{:S(2)}, u32[]{:S(2)}) collective-permute-start(bf16[128,1024]{1,0:T(8,128)(2,1)} %bitcast.18), channel_id=1, source_target_pairs={{0,2},{2,0},{1,3},{3,1},{4,6},{6,4},{5,7},{7,5},{8,10},{10,8},{9,1... | collective-permute-start | bytes 786440 | tf_op jit(solution)/shard_map/ppermute | solution.py:408
  13.1 7.2 %collective-permute-start.5 = (bf16[2,128,256]{2,1,0:T(8,128)(2,1)S(1)}, bf16[2,128,256]{2,1,0:T(8,128)(2,1)S(1)}, u32[]{:S(2)}, u32[]{:S(2)}) collective-permute-start(bf16[2,128,256]{2,1,0:T(8,128)(2,1)S(1)} %get-tuple-element.45), channel_id=1, source_target_pairs={{0,4},{2,6},{4,8},{6,10},{8,12},{10,14},{12,16},{14,18},{16,20},{1... | collective-permute-start | bytes 393224 | tf_op jit(solution)/shard_map/ppermute | solution.py:412
  14.7 5.6 %collective-permute-start.6 = (bf16[2,128,256]{2,1,0:T(8,128)(2,1)S(1)}, bf16[2,128,256]{2,1,0:T(8,128)(2,1)S(1)}, u32[]{:S(2)}, u32[]{:S(2)}) collective-permute-start(bf16[2,128,256]{2,1,0:T(8,128)(2,1)S(1)} %get-tuple-element.41), channel_id=1, source_target_pairs={{0,30},{2,28},{4,0},{6,2},{8,4},{10,6},{12,8},{14,10},{16,12},{18,... | collective-permute-start | bytes 393224 | tf_op jit(solution)/shard_map/ppermute | solution.py:411
  17.3 6.5 %collective-permute-start = (bf16[128,1024]{1,0:T(8,128)(2,1)S(1)}, bf16[128,1024]{1,0:T(8,128)(2,1)S(1)}, u32[]{:S(2)}, u32[]{:S(2)}) collective-permute-start(bf16[128,1024]{1,0:T(8,128)(2,1)S(1)} %get-tuple-element.38.og0.g0), channel_id=1, source_target_pairs={{0,1},{1,0},{2,3},{3,2},{4,5},{5,4},{6,7},{7,6},{8,9},{9,8},{10,11... | collective-permute-start | bytes 786440 | tf_op jit(solution)/shard_map/ppermute | solution.py:415
  17.3 6.5 %collective-permute-start.4 = (bf16[128,1024]{1,0:T(8,128)(2,1)S(1)}, bf16[128,1024]{1,0:T(8,128)(2,1)S(1)}, u32[]{:S(2)}, u32[]{:S(2)}) collective-permute-start(bf16[128,1024]{1,0:T(8,128)(2,1)S(1)} %collective-permute-done.1.og2.g2), channel_id=1, source_target_pairs={{0,1},{1,0},{2,3},{3,2},{4,5},{5,4},{6,7},{7,6},{8,9},{9,8},{10,11... | collective-permute-start | bytes 786440 | tf_op jit(solution)/shard_map/ppermute | solution.py:414
  20.3 11.4 %collective-permute-start.9 = (bf16[128,1024]{1,0:T(8,128)(2,1)S(1)}, bf16[128,1024]{1,0:T(8,128)(2,1)S(1)}, u32[]{:S(2)}, u32[]{:S(2)}) collective-permute-start(bf16[128,1024]{1,0:T(8,128)(2,1)S(1)} %get-tuple-element.50.h0), channel_id=1, source_target_pairs={{0,1},{1,0},{2,3},{3,2},{4,5},{5,4},{6,7},{7,6},{8,9},{9,8},{10,11... | collective-permute-start | bytes 786440 | tf_op jit(solution)/shard_map/ppermute | solution.py:416
  23.8 7.8 %collective-permute-start.11 = (bf16[128,1024]{1,0:T(8,128)(2,1)S(1)}, bf16[128,1024]{1,0:T(8,128)(2,1)S(1)}, u32[]{:S(2)}, u32[]{:S(2)}) collective-permute-start(bf16[128,1024]{1,0:T(8,128)(2,1)S(1)} %collective-permute-done.10.h2), channel_id=1, source_target_pairs={{0,1},{1,0},{2,3},{3,2},{4,5},{5,4},{6,7},{7,6},{8,9},{9,8},{10,11... | collective-permute-start | bytes 786440 | tf_op jit(solution)/shard_map/ppermute | solution.py:418
  27.4 9.6 %collective-permute-start.7 = (bf16[2,128,256]{2,1,0:T(8,128)(2,1)S(1)}, bf16[2,128,256]{2,1,0:T(8,128)(2,1)S(1)}, u32[]{:S(2)}, u32[]{:S(2)}) collective-permute-start(bf16[2,128,256]{2,1,0:T(8,128)(2,1)S(1)} %get-tuple-element.48), channel_id=1, source_target_pairs={{0,4},{2,6},{4,8},{6,10},{8,12},{10,14},{12,16},{14,18},{16,20},{1... | collective-permute-start | bytes 393224 | tf_op jit(solution)/shard_map/ppermute | solution.py:434
  27.5 9.6 %collective-permute-start.8 = (bf16[2,128,256]{2,1,0:T(8,128)(2,1)S(1)}, bf16[2,128,256]{2,1,0:T(8,128)(2,1)S(1)}, u32[]{:S(2)}, u32[]{:S(2)}) collective-permute-start(bf16[2,128,256]{2,1,0:T(8,128)(2,1)S(1)} %get-tuple-element.49.after), channel_id=1, source_target_pairs={{0,30},{2,28},{4,0},{6,2},{8,4},{10,6},{12,8},{14,10},{16,12},{18,... | collective-permute-start | bytes 393224 | tf_op jit(solution)/shard_map/ppermute | solution.py:433
  31.7 6.1 %collective-permute-start.12 = (bf16[48,1024]{1,0:T(8,128)(2,1)S(1)}, bf16[48,1024]{1,0:T(8,128)(2,1)S(1)}, u32[]{:S(2)}, u32[]{:S(2)}) collective-permute-start(bf16[48,1024]{1,0:T(8,128)(2,1)S(1)} %get-tuple-element.54), channel_id=1, source_target_pairs={{0,32},{32,64},{64,96},{96,128},{128,160},{160,192},{192,224},{224... | collective-permute-start | bytes 294920 | tf_op jit(solution)/shard_map/ppermute | solution.py:440
  32.0 5.8 %collective-permute-start.13 = (bf16[48,1024]{1,0:T(8,128)(2,1)S(1)}, bf16[48,1024]{1,0:T(8,128)(2,1)S(1)}, u32[]{:S(2)}, u32[]{:S(2)}) collective-permute-start(bf16[48,1024]{1,0:T(8,128)(2,1)S(1)} %get-tuple-element.55), channel_id=1, source_target_pairs={{0,224},{32,0},{64,32},{96,64},{128,96},{160,128},{192,160},{224,1... | collective-permute-start | bytes 294920 | tf_op jit(solution)/shard_map/ppermute | solution.py:439
  40.0 33.1 %all-to-all-start = ((bf16[8,4,8,16,256]{4,3,2,1,0:T(8,128)(2,1)}), bf16[8,4,8,16,256]{4,3,2,1,0:T(8,128)(2,1)S(1)}, u32[]{:S(2)}, u32[]{:S(2)}) async-start(bf16[8,4,8,16,256]{4,3,2,1,0:T(8,128)(2,1)} %get-tuple-element.66), calls=%async_computation | async-start | bytes 4194304 | tf_op jit(solution)/shard_map/all_to_all | solution.py:470
  44.8 5.3 %collective-permute-start.14 = (bf16[2,48,256]{2,1,0:T(8,128)(2,1)S(1)}, bf16[2,48,256]{2,1,0:T(8,128)(2,1)S(1)}, u32[]{:S(2)}, u32[]{:S(2)}) collective-permute-start(bf16[2,48,256]{2,1,0:T(8,128)(2,1)S(1)} %get-tuple-element.60), channel_id=1, source_target_pairs={{0,32},{32,64},{64,96},{96,128},{128,160},{160,192},{192,224},{224... | collective-permute-start | bytes 147464 | tf_op jit(solution)/shard_map/ppermute | solution.py:469
  44.8 5.3 %collective-permute-start.15 = (bf16[2,48,256]{2,1,0:T(8,128)(2,1)S(1)}, bf16[2,48,256]{2,1,0:T(8,128)(2,1)S(1)}, u32[]{:S(2)}, u32[]{:S(2)}) collective-permute-start(bf16[2,48,256]{2,1,0:T(8,128)(2,1)S(1)} %get-tuple-element.61), channel_id=1, source_target_pairs={{0,224},{32,0},{64,32},{96,64},{128,96},{160,128},{192,160},{224,1... | collective-permute-start | bytes 147464 | tf_op jit(solution)/shard_map/ppermute | solution.py:468
  53.6 2.0 %collective-permute-start.16 = (bf16[2,128,1024]{2,1,0:T(8,128)(2,1)S(1)}, bf16[2,128,1024]{2,1,0:T(8,128)(2,1)S(1)}, u32[]{:S(2)}, u32[]{:S(2)}) collective-permute-start(bf16[2,128,1024]{2,1,0:T(8,128)(2,1)S(1)} %get-tuple-element.63), channel_id=1, source_target_pairs={{0,1},{1,0},{2,3},{3,2},{4,5},{5,4},{6,7},{7,6},{8,9},{9,8},{10,11... | collective-permute-start | bytes 1572872 | tf_op jit(solution)/shard_map/ppermute | solution.py:484
  55.7 22.7 %collective-permute-start.17 = (bf16[128,1024]{1,0:T(8,128)(2,1)S(1)}, bf16[128,1024]{1,0:T(8,128)(2,1)S(1)}, u32[]{:S(2)}, u32[]{:S(2)}) collective-permute-start(bf16[128,1024]{1,0:T(8,128)(2,1)S(1)} %get-tuple-element.65), channel_id=1, source_target_pairs={{0,2},{2,0},{1,3},{3,1},{4,6},{6,4},{5,7},{7,5},{8,10},{10,8},{9,1... | collective-permute-start | bytes 786440 | tf_op jit(solution)/shard_map/ppermute | solution.py:486
  74.1 16.0 %all-to-all-start.1 = ((bf16[8,16,1024]{2,1,0:T(8,128)(2,1)}), bf16[8,16,1024]{2,1,0:T(8,128)(2,1)S(1)}, u32[]{:S(2)}, u32[]{:S(2)}) async-start(bf16[8,16,1024]{2,1,0:T(8,128)(2,1)} %shard_map.103), calls=%async_computation.1 | async-start | bytes 524288 | tf_op jit(solution)/shard_map/all_to_all | solution.py:490

commit v7 on v6

--- a/solution.py
+++ b/solution.py
@@ -31,7 +31,8 @@
 K_BAND = 12 * SLOTS
 K_ALL = K_MID + 2 * K_BAND
 Z, YH, X, YL, CORE = 8, 2, 4, 2, 2
-GRID = ("z", "yh", "xh", "xl")
+ZZ = ("zh", "zl")
+GRID = ZZ + ("yh", "xh", "xl")
 HEAD = ("yl", "core")
 F32 = jnp.float32
 BF16 = jnp.bfloat16
@@ -155,7 +156,7 @@
     ga, gl, gr, from_left, from_right,
 ):
     head = head_index()
-    tile_row = lax.axis_index("z")
+    tile_row = lax.axis_index("zh") * 2 + lax.axis_index("zl")
     tile_col = lax.axis_index("yh") * X + lax.axis_index("xh") * 2 + lax.axis_index("xl")
     for i, piece in enumerate((og0, og1, og2, og3)):
         at = pl.multiple_of((head ^ i) * PIECE, PIECE)
@@ -348,7 +349,9 @@
         total = terms[0, j].astype(F32)
         for i in range(1, YH * X):
             total += terms[i, j].astype(F32)
-        out[:, :, j * FEAT : (j + 1) * FEAT] = total.astype(BF16)
+        for z in range(Z):
+            at = (z % 2) * (Z // 2) + z // 2
+            out[at, :, j * FEAT : (j + 1) * FEAT] = total[z].astype(BF16)
 
 
 def last_kernel(parts, grad_wqkv, grad_wout):
@@ -393,8 +396,8 @@
     to_above, to_below = call(
         edges_kernel, (edge, edge), scratch=[pltpu.SemaphoreType.DMA((4,))], n_in=2, hbm=(0, 1)
     )(k, v)
-    below = lax.ppermute(to_above, "z", ring(Z, -1))
-    above = lax.ppermute(to_below, "z", ring(Z, 1))
+    below = lax.ppermute(to_above, ZZ, ring(Z, -1))
+    above = lax.ppermute(to_below, ZZ, ring(Z, 1))
     q, kv, w_out, g0, h0 = call(
         load_kernel,
         (flat, shaped((2, TOKENS, FEAT)), shaped((FEAT, D)), own, own),
@@ -436,8 +439,8 @@
     hidden, to_above, to_below = call(
         hidden_kernel, (shaped((TOKENS, D)), hid_edge, hid_edge), n_in=5
     )(band_left, h0, h1, h2, h3)
-    hid_below = lax.ppermute(to_above, "z", ring(Z, -1))
-    hid_above = lax.ppermute(to_below, "z", ring(Z, 1))
+    hid_below = lax.ppermute(to_above, ZZ, ring(Z, -1))
+    hid_above = lax.ppermute(to_below, ZZ, ring(Z, 1))
     all_terms = shaped((YH * X, 4, Z, 16, FEAT))
     (terms,) = call(
         first_terms_kernel,
@@ -465,8 +468,8 @@
         hbm_out=(0,),
         alias={6: 0},
     )(grad_mid, got_left, got_right, hidden, hid_above, hid_below, terms)
-    got_below = lax.ppermute(to_above, "z", ring(Z, -1))
-    got_above = lax.ppermute(to_below, "z", ring(Z, 1))
+    got_below = lax.ppermute(to_above, ZZ, ring(Z, -1))
+    got_above = lax.ppermute(to_below, ZZ, ring(Z, 1))
     terms = lax.all_to_all(terms, ("yh", "xl", "xh"), 0, 0, tiled=True)
 
     half = shaped((YL, PIECE, D))
@@ -487,7 +490,7 @@
     grad_hidden = (stay + got.astype(F32)).astype(BF16).reshape(1, 8, TW, D)
 
     (parts,) = call(sum_kernel, (shaped((Z, 16, 4 * FEAT)),), n_in=1)(terms)
-    parts = lax.all_to_all(parts, "z", 0, 0, tiled=True)
+    parts = lax.all_to_all(parts, ("zl", "zh"), 0, 0, tiled=True)
     grad_wqkv, grad_wout = call(
         last_kernel, (shaped((3, 16, FEAT), F32), shaped((16, FEAT), F32)), n_in=1
     )(parts)
@@ -495,7 +498,7 @@
 
 
 def solution(mesh):
-    fine = Mesh(mesh.devices.reshape(Z, YH, 2, 2, YL, CORE), GRID + HEAD)
+    fine = Mesh(mesh.devices.reshape(Z // 2, 2, YH, 2, 2, YL, CORE), GRID + HEAD)
     return jax.shard_map(
         per_device,
         mesh=fine,

time: 91.1 us -> 90 us (0.988); the launches traced: 90.8 us -> 88.6 us
  waiting for transfers between devices: 40.9 us -> 38.7 us
    all_to_all x1, waiting for transfers between devices: 10.9 us -> 8.68 us  [per_device(): parts = lax.all_to_all(parts, ('zl', 'zh'), 0, 0, tiled=True)]
  transfers between devices with their start and end apart: 20 -> 20, of which waited for: 9 -> 9; matrix products, arithmetic and copies ran while one was open for 1% -> 1% of each run, Pallas kernels for 13% -> 14%
where the time goes in v7:
time: 90 us; the launch traced here: 88.6 us
  waiting for transfers between devices  38.7 us (43%)
  starting transfers between devices  32.6 us (36%)
  Pallas kernels  15.7 us (17%)
    all_to_all x1, waiting for transfers between devices, per_device(): terms = lax.all_to_all(terms, ('yh', 'xl', 'xh'), 0, 0, tiled=True)  16.4 us
    pallas_call x11, Pallas kernels, on(): run(*(hold(a, pltpu.HBM) if i in hbm else a for i, a in enumerate(args)))  15.7 us
    all_to_all x1, waiting for transfers between devices, per_device(): parts = lax.all_to_all(parts, ('zl', 'zh'), 0, 0, tiled=True)  8.68 us
    ppermute x1, starting transfers between devices, per_device(): below = lax.ppermute(to_above, ZZ, ring(Z, -1))  5.93 us
    all_to_all x1, starting transfers between devices, per_device(): terms = lax.all_to_all(terms, ('yh', 'xl', 'xh'), 0, 0, tiled=True)  4.74 us
    all_to_all x1, starting transfers between devices, per_device(): parts = lax.all_to_all(parts, ('zl', 'zh'), 0, 0, tiled=True)  4.35 us
    ppermute x1, starting transfers between devices, per_device(): got_right = lax.ppermute(band_left, COLS, columns(-1))  4.12 us
    ppermute x1, waiting for transfers between devices, per_device(): h2 = lax.ppermute(late, 'yl', SWAP)  3.53 us
  transfers between devices with their start and end apart: 20, of which 9 were waited for; matrix products, arithmetic and copies ran while one was open for 1% of the time, Pallas kernels for 14%

profile of v7, /device:TPU:8, one launch (start us, length us, event | category | flops | bytes accessed | tf_op | source)
XLA Modules:
  0.0 88.6 jit_solution(16662018336211206936)
XLA Ops:
  0.6 0.8 shard_map.94
  1.5 5.9 %collective-permute-start.3 = (bf16[2,48,256]{2,1,0:T(8,128)(2,1)S(1)}, bf16[2,48,256]{2,1,0:T(8,128)(2,1)S(1)}, u32[]{:S(2)}, u32[]{:S(2)}) collective-permute-start(bf16[2,48,256]{2,1,0:T(8,128)(2,1)S(1)} %get-tuple-element.36.after), channel_id=1, source_target_pairs={{0,224},{32,0},{64,32},{96,64},{128,96},{160,128},{192,160},{224,1... | collective-permute-start | bytes 147464 | tf_op jit(solution)/shard_map/ppermute | solution.py:399
  7.9 1.3 %collective-permute-done.3.below = bf16[2,48,256]{2,1,0:T(8,128)(2,1)S(1)} collective-permute-done((bf16[2,48,256]{2,1,0:T(8,128)(2,1)S(1)}, bf16[2,48,256]{2,1,0:T(8,128)(2,1)S(1)}, u32[]{:S(2)}, u32[]{:S(2)}) %collective-permute-start.3) | collective-permute-done | bytes 49184 | tf_op jit(solution)/shard_map/ppermute | solution.py:399
  9.6 1.5 %shard_map.95 = (bf16[512,256]{1,0:T(8,128)(2,1)S(1)}, bf16[2,512,256]{2,1,0:T(8,128)(2,1)S(1)}, bf16[256,1024]{1,0:T(8,128)(2,1)S(1)}, bf16[128,1024]{1,0:T(8,128)(2,1)S(1)}, bf16[128,1024]{1,0:T(8,128)(2,1)S(1)}) custom-call(bf16[2,48,256]{2,1,0:T(8,128)(2,1)S(1)} %get-tuple-element.36.after, bf16[512,256]{1,0:T(8,128)(2,1)} %bitcast.15, ...), custom_call_target="tpu_custom_call" | custom-call | flops 10000000000 | tf_op jit(solution)/shard_map/pallas_call | solution.py:68
  11.1 1.6 %collective-permute-done.2.above = bf16[2,48,256]{2,1,0:T(8,128)(2,1)S(1)} collective-permute-done((bf16[2,48,256]{2,1,0:T(8,128)(2,1)S(1)}, bf16[2,48,256]{2,1,0:T(8,128)(2,1)S(1)}, u32[]{:S(2)}, u32[]{:S(2)}) %collective-permute-start.2) | collective-permute-done | bytes 49184 | tf_op jit(solution)/shard_map/ppermute | solution.py:400
  13.1 1.6 %collective-permute-start.5 = (bf16[2,128,256]{2,1,0:T(8,128)(2,1)S(1)}, bf16[2,128,256]{2,1,0:T(8,128)(2,1)S(1)}, u32[]{:S(2)}, u32[]{:S(2)}) collective-permute-start(bf16[2,128,256]{2,1,0:T(8,128)(2,1)S(1)} %get-tuple-element.45), channel_id=1, source_target_pairs={{0,4},{2,6},{4,8},{6,10},{8,12},{10,14},{12,16},{14,18},{16,20},{1... | collective-permute-start | bytes 393224 | tf_op jit(solution)/shard_map/ppermute | solution.py:415
  14.7 2.6 %collective-permute-start.6 = (bf16[2,128,256]{2,1,0:T(8,128)(2,1)S(1)}, bf16[2,128,256]{2,1,0:T(8,128)(2,1)S(1)}, u32[]{:S(2)}, u32[]{:S(2)}) collective-permute-start(bf16[2,128,256]{2,1,0:T(8,128)(2,1)S(1)} %get-tuple-element.41), channel_id=1, source_target_pairs={{0,30},{2,28},{4,0},{6,2},{8,4},{10,6},{12,8},{14,10},{16,12},{18,... | collective-permute-start | bytes 393224 | tf_op jit(solution)/shard_map/ppermute | solution.py:414
  17.8 2.4 %collective-permute-done.5.sent_left = bf16[2,128,256]{2,1,0:T(8,128)(2,1)S(1)} collective-permute-done((bf16[2,128,256]{2,1,0:T(8,128)(2,1)S(1)}, bf16[2,128,256]{2,1,0:T(8,128)(2,1)S(1)}, u32[]{:S(2)}, u32[]{:S(2)}) %collective-permute-start.5) | collective-permute-done | bytes 131104 | tf_op jit(solution)/shard_map/ppermute | solution.py:415
  20.3 3.5 %collective-permute-done.10.h2 = bf16[128,1024]{1,0:T(8,128)(2,1)S(1)} collective-permute-done((bf16[128,1024]{1,0:T(8,128)(2,1)}, bf16[128,1024]{1,0:T(8,128)(2,1)S(1)}, u32[]{:S(2)}, u32[]{:S(2)}) %collective-permute-start.10) | collective-permute-done | bytes 262176 | tf_op jit(solution)/shard_map/ppermute | solution.py:411
  23.8 3.6 %shard_map.97 = (bf16[512,256]{1,0:T(8,128)(2,1)S(1)}, bf16[512,256]{1,0:T(8,128)(2,1)S(1)}, f32[2,608,256]{2,1,0:T(8,128)S(1)}, bf16[2,128,256]{2,1,0:T(8,128)(2,1)S(1)}, bf16[2,128,256]{2,1,0:T(8,128)(2,1)S(1)}) custom-call(bf16[512,256]{1,0:T(8,128)(2,1)S(1)} %get-tuple-element.37.q, bf16[128,1024]{1,0:T(8,128)(2,1)S(1)} %get-tuple-element.38.og0.g0, ...), custom_call_target="tpu_custom_call" | custom-call | tf_op jit(solution)/shard_map/pallas_call | solution.py:68
  27.5 4.1 %collective-permute-start.8 = (bf16[2,128,256]{2,1,0:T(8,128)(2,1)S(1)}, bf16[2,128,256]{2,1,0:T(8,128)(2,1)S(1)}, u32[]{:S(2)}, u32[]{:S(2)}) collective-permute-start(bf16[2,128,256]{2,1,0:T(8,128)(2,1)S(1)} %get-tuple-element.49.after), channel_id=1, source_target_pairs={{0,30},{2,28},{4,0},{6,2},{8,4},{10,6},{12,8},{14,10},{16,12},{18,... | collective-permute-start | bytes 393224 | tf_op jit(solution)/shard_map/ppermute | solution.py:436
  32.0 3.2 %collective-permute-start.13 = (bf16[48,1024]{1,0:T(8,128)(2,1)S(1)}, bf16[48,1024]{1,0:T(8,128)(2,1)S(1)}, u32[]{:S(2)}, u32[]{:S(2)}) collective-permute-start(bf16[48,1024]{1,0:T(8,128)(2,1)S(1)} %get-tuple-element.55), channel_id=1, source_target_pairs={{0,224},{32,0},{64,32},{96,64},{128,96},{160,128},{192,160},{224,1... | collective-permute-start | bytes 294920 | tf_op jit(solution)/shard_map/ppermute | solution.py:442
  35.2 1.8 %shard_map.99.first = bf16[8,4,8,16,256]{4,3,2,1,0:T(8,128)(2,1)} custom-call(bf16[512,256]{1,0:T(8,128)(2,1)S(1)} %get-tuple-element.46.grad_q, bf16[512,256]{1,0:T(8,128)(2,1)S(1)} %get-tuple-element.56.attn, bf16[128,1024]{1,0:T(8,128)(2,1)S(1)} %get-tuple-element.38.og0.g0, bf16[128,1024]{1,0:T(8,128)(2,1)S(1)} %collective-permute-done.og1.g1, ...), custom_call_target="tpu_custom_call" | custom-call | flops 10000000000 | tf_op jit(solution)/shard_map/pallas_call | solution.py:68
  37.9 2.1 %shard_map.100 = (bf16[8,4,8,16,256]{4,3,2,1,0:T(8,128)(2,1)}, bf16[2,512,256]{2,1,0:T(8,128)(2,1)S(1)}, f32[2,48,256]{2,1,0:T(8,128)S(1)}, f32[2,48,256]{2,1,0:...) custom-call(f32[2,608,256]{2,1,0:T(8,128)S(1)} %get-tuple-element.47, ...), custom_call_target="tpu_custom_call", output_to_operand_aliasing={{0}: (6, {})} | custom-call | tf_op jit(solution)/shard_map/pallas_call | solution.py:68
  40.0 4.7 %all-to-all-start = ((bf16[8,4,8,16,256]{4,3,2,1,0:T(8,128)(2,1)}), bf16[8,4,8,16,256]{4,3,2,1,0:T(8,128)(2,1)S(1)}, u32[]{:S(2)}, u32[]{:S(2)}) async-start(bf16[8,4,8,16,256]{4,3,2,1,0:T(8,128)(2,1)} %get-tuple-element.66), calls=%async_computation | async-start | bytes 4194304 | tf_op jit(solution)/shard_map/all_to_all | solution.py:473
  44.8 3.2 %collective-permute-start.15 = (bf16[2,48,256]{2,1,0:T(8,128)(2,1)S(1)}, bf16[2,48,256]{2,1,0:T(8,128)(2,1)S(1)}, u32[]{:S(2)}, u32[]{:S(2)}) collective-permute-start(bf16[2,48,256]{2,1,0:T(8,128)(2,1)S(1)} %get-tuple-element.61), channel_id=1, source_target_pairs={{0,224},{32,0},{64,32},{96,64},{128,96},{160,128},{192,160},{224,1... | collective-permute-start | bytes 147464 | tf_op jit(solution)/shard_map/ppermute | solution.py:471
  48.0 2.1 %collective-permute-done.14.from_above = bf16[2,48,256]{2,1,0:T(8,128)(2,1)S(1)} collective-permute-done((bf16[2,48,256]{2,1,0:T(8,128)(2,1)S(1)}, bf16[2,48,256]{2,1,0:T(8,128)(2,1)S(1)}, u32[]{:S(2)}, u32[]{:S(2)}) %collective-permute-start.14) | collective-permute-done | bytes 49184 | tf_op jit(solution)/shard_map/ppermute | solution.py:472
  50.1 3.6 %shard_map.101 = (bf16[2,128,1024]{2,1,0:T(8,128)(2,1)S(1)}, bf16[2,128,1024]{2,1,0:T(8,128)(2,1)S(1)}) custom-call(bf16[512,256]{1,0:T(8,128)(2,1)S(1)} %get-tuple-element.46.grad_q, bf16[2,512,256]{2,1,0:T(8,128)(2,1)S(1)} %get-tuple-element.57.inner, f32[2,48,256]{2,1,0:T(8,128)S(1)} %get-tuple-element.58.top, ...), custom_call_target="tpu_custom_call" | custom-call | tf_op jit(solution)/shard_map/pallas_call | solution.py:68
  53.7 1.9 %collective-permute-done.16.got = bf16[2,128,1024]{2,1,0:T(8,128)(2,1)S(1)} collective-permute-done((bf16[2,128,1024]{2,1,0:T(8,128)(2,1)S(1)}, bf16[2,128,1024]{2,1,0:T(8,128)(2,1)S(1)}, u32[]{:S(2)}, u32[]{:S(2)}) %collective-permute-start.16) | collective-permute-done | bytes 524320 | tf_op jit(solution)/shard_map/ppermute | solution.py:487
  55.7 1.0 %collective-permute-start.17 = (bf16[128,1024]{1,0:T(8,128)(2,1)S(1)}, bf16[128,1024]{1,0:T(8,128)(2,1)S(1)}, u32[]{:S(2)}, u32[]{:S(2)}) collective-permute-start(bf16[128,1024]{1,0:T(8,128)(2,1)S(1)} %get-tuple-element.65), channel_id=1, source_target_pairs={{0,2},{2,0},{1,3},{3,1},{4,6},{6,4},{5,7},{7,5},{8,10},{10,8},{9,1... | collective-permute-start | bytes 786440 | tf_op jit(solution)/shard_map/ppermute | solution.py:489
  56.7 16.4 %all-to-all-done.terms = bf16[8,4,8,16,256]{4,3,2,1,0:T(8,128)(2,1)S(1)} async-done(((bf16[8,4,8,16,256]{4,3,2,1,0:T(8,128)(2,1)}), bf16[8,4,8,16,256]{4,3,2,1,0:T(8,128)(2,1)S(1)}, u32[]{:S(2)}, u32[]{:S(2)}) %all-to-all-start) | async-done | bytes 2097184 | tf_op jit(solution)/shard_map/all_to_all | solution.py:473
  73.1 1.0 %shard_map.103 = bf16[8,16,1024]{2,1,0:T(8,128)(2,1)} custom-call(bf16[8,4,8,16,256]{4,3,2,1,0:T(8,128)(2,1)S(1)} %all-to-all-done.terms), custom_call_target="tpu_custom_call" | custom-call | tf_op jit(solution)/shard_map/pallas_call | solution.py:68
  74.1 4.4 %all-to-all-start.1 = ((bf16[8,16,1024]{2,1,0:T(8,128)(2,1)}), bf16[8,16,1024]{2,1,0:T(8,128)(2,1)S(1)}, u32[]{:S(2)}, u32[]{:S(2)}) async-start(bf16[8,16,1024]{2,1,0:T(8,128)(2,1)} %shard_map.103), calls=%async_computation.1 | async-start | bytes 524288 | tf_op jit(solution)/shard_map/all_to_all | solution.py:493
  79.2 8.7 %all-to-all-done.1.parts = bf16[8,16,1024]{2,1,0:T(8,128)(2,1)S(1)} async-done(((bf16[8,16,1024]{2,1,0:T(8,128)(2,1)}), bf16[8,16,1024]{2,1,0:T(8,128)(2,1)S(1)}, u32[]{:S(2)}, u32[]{:S(2)}) %all-to-all-start.1) | async-done | bytes 262176 | tf_op jit(solution)/shard_map/all_to_all | solution.py:493
  (28 shorter events, 4.7 us)
Async XLA Ops:
  1.5 7.7 %collective-permute-start.3 = (bf16[2,48,256]{2,1,0:T(8,128)(2,1)S(1)}, bf16[2,48,256]{2,1,0:T(8,128)(2,1)S(1)}, u32[]{:S(2)}, u32[]{:S(2)}) collective-permute-start(bf16[2,48,256]{2,1,0:T(8,128)(2,1)S(1)} %get-tuple-element.36.after), channel_id=1, source_target_pairs={{0,224},{32,0},{64,32},{96,64},{128,96},{160,128},{192,160},{224,1... | collective-permute-start | bytes 147464 | tf_op jit(solution)/shard_map/ppermute | solution.py:399
  7.4 5.3 %collective-permute-start.2 = (bf16[2,48,256]{2,1,0:T(8,128)(2,1)S(1)}, bf16[2,48,256]{2,1,0:T(8,128)(2,1)S(1)}, u32[]{:S(2)}, u32[]{:S(2)}) collective-permute-start(bf16[2,48,256]{2,1,0:T(8,128)(2,1)S(1)} %get-tuple-element.40), channel_id=1, source_target_pairs={{0,32},{32,64},{64,96},{96,128},{128,160},{160,192},{192,224},{224... | collective-permute-start | bytes 147464 | tf_op jit(solution)/shard_map/ppermute | solution.py:400
  7.4 9.9 %collective-permute-start.1 = (bf16[128,1024]{1,0:T(8,128)(2,1)}, bf16[128,1024]{1,0:T(8,128)(2,1)S(1)}, u32[]{:S(2)}, u32[]{:S(2)}) collective-permute-start(bf16[128,1024]{1,0:T(8,128)(2,1)} %bitcast.16), channel_id=1, source_target_pairs={{0,2},{2,0},{1,3},{3,1},{4,6},{6,4},{5,7},{7,5},{8,10},{10,8},{9,1... | collective-permute-start | bytes 786440 | tf_op jit(solution)/shard_map/ppermute | solution.py:409
  9.2 14.7 %collective-permute-start.10 = (bf16[128,1024]{1,0:T(8,128)(2,1)}, bf16[128,1024]{1,0:T(8,128)(2,1)S(1)}, u32[]{:S(2)}, u32[]{:S(2)}) collective-permute-start(bf16[128,1024]{1,0:T(8,128)(2,1)} %bitcast.18), channel_id=1, source_target_pairs={{0,2},{2,0},{1,3},{3,1},{4,6},{6,4},{5,7},{7,5},{8,10},{10,8},{9,1... | collective-permute-start | bytes 786440 | tf_op jit(solution)/shard_map/ppermute | solution.py:411
  13.1 7.2 %collective-permute-start.5 = (bf16[2,128,256]{2,1,0:T(8,128)(2,1)S(1)}, bf16[2,128,256]{2,1,0:T(8,128)(2,1)S(1)}, u32[]{:S(2)}, u32[]{:S(2)}) collective-permute-start(bf16[2,128,256]{2,1,0:T(8,128)(2,1)S(1)} %get-tuple-element.45), channel_id=1, source_target_pairs={{0,4},{2,6},{4,8},{6,10},{8,12},{10,14},{12,16},{14,18},{16,20},{1... | collective-permute-start | bytes 393224 | tf_op jit(solution)/shard_map/ppermute | solution.py:415
  14.7 5.6 %collective-permute-start.6 = (bf16[2,128,256]{2,1,0:T(8,128)(2,1)S(1)}, bf16[2,128,256]{2,1,0:T(8,128)(2,1)S(1)}, u32[]{:S(2)}, u32[]{:S(2)}) collective-permute-start(bf16[2,128,256]{2,1,0:T(8,128)(2,1)S(1)} %get-tuple-element.41), channel_id=1, source_target_pairs={{0,30},{2,28},{4,0},{6,2},{8,4},{10,6},{12,8},{14,10},{16,12},{18,... | collective-permute-start | bytes 393224 | tf_op jit(solution)/shard_map/ppermute | solution.py:414
  17.3 6.5 %collective-permute-start = (bf16[128,1024]{1,0:T(8,128)(2,1)S(1)}, bf16[128,1024]{1,0:T(8,128)(2,1)S(1)}, u32[]{:S(2)}, u32[]{:S(2)}) collective-permute-start(bf16[128,1024]{1,0:T(8,128)(2,1)S(1)} %get-tuple-element.38.og0.g0), channel_id=1, source_target_pairs={{0,1},{1,0},{2,3},{3,2},{4,5},{5,4},{6,7},{7,6},{8,9},{9,8},{10,11... | collective-permute-start | bytes 786440 | tf_op jit(solution)/shard_map/ppermute | solution.py:418
  17.3 6.5 %collective-permute-start.4 = (bf16[128,1024]{1,0:T(8,128)(2,1)S(1)}, bf16[128,1024]{1,0:T(8,128)(2,1)S(1)}, u32[]{:S(2)}, u32[]{:S(2)}) collective-permute-start(bf16[128,1024]{1,0:T(8,128)(2,1)S(1)} %collective-permute-done.1.og2.g2), channel_id=1, source_target_pairs={{0,1},{1,0},{2,3},{3,2},{4,5},{5,4},{6,7},{7,6},{8,9},{9,8},{10,11... | collective-permute-start | bytes 786440 | tf_op jit(solution)/shard_map/ppermute | solution.py:417
  20.3 11.4 %collective-permute-start.9 = (bf16[128,1024]{1,0:T(8,128)(2,1)S(1)}, bf16[128,1024]{1,0:T(8,128)(2,1)S(1)}, u32[]{:S(2)}, u32[]{:S(2)}) collective-permute-start(bf16[128,1024]{1,0:T(8,128)(2,1)S(1)} %get-tuple-element.50.h0), channel_id=1, source_target_pairs={{0,1},{1,0},{2,3},{3,2},{4,5},{5,4},{6,7},{7,6},{8,9},{9,8},{10,11... | collective-permute-start | bytes 786440 | tf_op jit(solution)/shard_map/ppermute | solution.py:419
  23.8 7.8 %collective-permute-start.11 = (bf16[128,1024]{1,0:T(8,128)(2,1)S(1)}, bf16[128,1024]{1,0:T(8,128)(2,1)S(1)}, u32[]{:S(2)}, u32[]{:S(2)}) collective-permute-start(bf16[128,1024]{1,0:T(8,128)(2,1)S(1)} %collective-permute-done.10.h2), channel_id=1, source_target_pairs={{0,1},{1,0},{2,3},{3,2},{4,5},{5,4},{6,7},{7,6},{8,9},{9,8},{10,11... | collective-permute-start | bytes 786440 | tf_op jit(solution)/shard_map/ppermute | solution.py:421
  27.4 9.6 %collective-permute-start.7 = (bf16[2,128,256]{2,1,0:T(8,128)(2,1)S(1)}, bf16[2,128,256]{2,1,0:T(8,128)(2,1)S(1)}, u32[]{:S(2)}, u32[]{:S(2)}) collective-permute-start(bf16[2,128,256]{2,1,0:T(8,128)(2,1)S(1)} %get-tuple-element.48), channel_id=1, source_target_pairs={{0,4},{2,6},{4,8},{6,10},{8,12},{10,14},{12,16},{14,18},{16,20},{1... | collective-permute-start | bytes 393224 | tf_op jit(solution)/shard_map/ppermute | solution.py:437
  27.5 9.6 %collective-permute-start.8 = (bf16[2,128,256]{2,1,0:T(8,128)(2,1)S(1)}, bf16[2,128,256]{2,1,0:T(8,128)(2,1)S(1)}, u32[]{:S(2)}, u32[]{:S(2)}) collective-permute-start(bf16[2,128,256]{2,1,0:T(8,128)(2,1)S(1)} %get-tuple-element.49.after), channel_id=1, source_target_pairs={{0,30},{2,28},{4,0},{6,2},{8,4},{10,6},{12,8},{14,10},{16,12},{18,... | collective-permute-start | bytes 393224 | tf_op jit(solution)/shard_map/ppermute | solution.py:436
  31.7 6.1 %collective-permute-start.12 = (bf16[48,1024]{1,0:T(8,128)(2,1)S(1)}, bf16[48,1024]{1,0:T(8,128)(2,1)S(1)}, u32[]{:S(2)}, u32[]{:S(2)}) collective-permute-start(bf16[48,1024]{1,0:T(8,128)(2,1)S(1)} %get-tuple-element.54), channel_id=1, source_target_pairs={{0,32},{32,64},{64,96},{96,128},{128,160},{160,192},{192,224},{224... | collective-permute-start | bytes 294920 | tf_op jit(solution)/shard_map/ppermute | solution.py:443
  32.0 5.8 %collective-permute-start.13 = (bf16[48,1024]{1,0:T(8,128)(2,1)S(1)}, bf16[48,1024]{1,0:T(8,128)(2,1)S(1)}, u32[]{:S(2)}, u32[]{:S(2)}) collective-permute-start(bf16[48,1024]{1,0:T(8,128)(2,1)S(1)} %get-tuple-element.55), channel_id=1, source_target_pairs={{0,224},{32,0},{64,32},{96,64},{128,96},{160,128},{192,160},{224,1... | collective-permute-start | bytes 294920 | tf_op jit(solution)/shard_map/ppermute | solution.py:442
  40.0 33.1 %all-to-all-start = ((bf16[8,4,8,16,256]{4,3,2,1,0:T(8,128)(2,1)}), bf16[8,4,8,16,256]{4,3,2,1,0:T(8,128)(2,1)S(1)}, u32[]{:S(2)}, u32[]{:S(2)}) async-start(bf16[8,4,8,16,256]{4,3,2,1,0:T(8,128)(2,1)} %get-tuple-element.66), calls=%async_computation | async-start | bytes 4194304 | tf_op jit(solution)/shard_map/all_to_all | solution.py:473
  44.8 5.3 %collective-permute-start.14 = (bf16[2,48,256]{2,1,0:T(8,128)(2,1)S(1)}, bf16[2,48,256]{2,1,0:T(8,128)(2,1)S(1)}, u32[]{:S(2)}, u32[]{:S(2)}) collective-permute-start(bf16[2,48,256]{2,1,0:T(8,128)(2,1)S(1)} %get-tuple-element.60), channel_id=1, source_target_pairs={{0,32},{32,64},{64,96},{96,128},{128,160},{160,192},{192,224},{224... | collective-permute-start | bytes 147464 | tf_op jit(solution)/shard_map/ppermute | solution.py:472
  44.8 5.3 %collective-permute-start.15 = (bf16[2,48,256]{2,1,0:T(8,128)(2,1)S(1)}, bf16[2,48,256]{2,1,0:T(8,128)(2,1)S(1)}, u32[]{:S(2)}, u32[]{:S(2)}) collective-permute-start(bf16[2,48,256]{2,1,0:T(8,128)(2,1)S(1)} %get-tuple-element.61), channel_id=1, source_target_pairs={{0,224},{32,0},{64,32},{96,64},{128,96},{160,128},{192,160},{224,1... | collective-permute-start | bytes 147464 | tf_op jit(solution)/shard_map/ppermute | solution.py:471
  53.6 2.0 %collective-permute-start.16 = (bf16[2,128,1024]{2,1,0:T(8,128)(2,1)S(1)}, bf16[2,128,1024]{2,1,0:T(8,128)(2,1)S(1)}, u32[]{:S(2)}, u32[]{:S(2)}) collective-permute-start(bf16[2,128,1024]{2,1,0:T(8,128)(2,1)S(1)} %get-tuple-element.63), channel_id=1, source_target_pairs={{0,1},{1,0},{2,3},{3,2},{4,5},{5,4},{6,7},{7,6},{8,9},{9,8},{10,11... | collective-permute-start | bytes 1572872 | tf_op jit(solution)/shard_map/ppermute | solution.py:487
  55.7 22.7 %collective-permute-start.17 = (bf16[128,1024]{1,0:T(8,128)(2,1)S(1)}, bf16[128,1024]{1,0:T(8,128)(2,1)S(1)}, u32[]{:S(2)}, u32[]{:S(2)}) collective-permute-start(bf16[128,1024]{1,0:T(8,128)(2,1)S(1)} %get-tuple-element.65), channel_id=1, source_target_pairs={{0,2},{2,0},{1,3},{3,1},{4,6},{6,4},{5,7},{7,5},{8,10},{10,8},{9,1... | collective-permute-start | bytes 786440 | tf_op jit(solution)/shard_map/ppermute | solution.py:489
  74.1 13.8 %all-to-all-start.1 = ((bf16[8,16,1024]{2,1,0:T(8,128)(2,1)}), bf16[8,16,1024]{2,1,0:T(8,128)(2,1)S(1)}, u32[]{:S(2)}, u32[]{:S(2)}) async-start(bf16[8,16,1024]{2,1,0:T(8,128)(2,1)} %shard_map.103), calls=%async_computation.1 | async-start | bytes 524288 | tf_op jit(solution)/shard_map/all_to_all | solution.py:493
